TPU v7x, 32 devices: a whole 2x2x4 slice. The times are simulated.
32 devices in a mesh: grp: 2 (over y), freq: 4 (over z), tri: 2 (over x), sta: 2 (over core).
Axes of the slice: x: 2, y: 2, z: 4, core: 2. Of those that a mesh axis runs over, the one named last changes fastest.
Arguments:
- slip: float32 [8, 8192], P(None, ('grp', 'freq', 'tri')), parts along dimension 1, may hold values from 0 to 1
- green: float32 [32, 8, 64, 128], P('freq'), may hold values from -0.09375 to 0.09375
- pattern: int32 [64, 64], P('sta'), may hold values from -1 to 7
- observed: float32 [2, 64, 4096], P(None, ('grp', 'freq'), 'sta'), parts along dimension 1, may hold values from -6 to 6
- adjacency: int32 [3, 2048], P(None, ('freq', 'tri')), may hold values from 0 to 2047, as said below
- smooth_weight: float32 [2], P('grp'), parts along dimension 0, may hold values from 2 to 8
Outputs:
- new_slip: float32 [8, 8192], P(None, ('grp', 'freq', 'tri')), parts along dimension 1
- residual: float32 [2, 64, 4096], P(None, ('grp', 'freq'), 'sta'), parts along dimension 1
There are 2 independent parts, one for each index of `grp`. A program takes and returns all parts, laid end to end along the dimension named above; an argument that names none is the same for every part. Nothing has to cross between parts.
Inputs may be any that keep to these rules, and one draw needn't show every extreme that they name: adjacency[j, t] differs from t by 1 to 256, and adjacency[0, t] differs from t by exactly 256. `pattern`: -1 marks an absent block.
All inputs are finite; a program needn't handle non-finite values.
Results may differ from a plain program's by a relative error of at most 0.000058.
Values sent between devices are 32-bit elements; how exact they have to be, the bound alone decides.
No kernel may reach another device: no remote copies, remote signals or barrier semaphores. Data moves between devices by JAX's collectives and lax.ppermute only.
A program may use at most 64 MiB of HBM per device.

v0:
```python
import math

import jax
import jax.numpy as jnp
from jax import lax
from jax.sharding import PartitionSpec as P

PRECISE = lax.Precision.HIGHEST


def padded_2(shard, sides, width):
    for axis, dim in sides:
        peers, length = (lax.axis_size(axis), shard.shape[dim])
        up = [(i, (i + 1) % peers) for i in range(peers - 1)]
        down = [(j, i) for i, j in up]
        last = lax.slice_in_dim(shard, length - width, length, axis=dim)
        initial = lax.slice_in_dim(shard, 0, width, axis=dim)
        before = lax.ppermute(last, axis, up)
        after = lax.ppermute(initial, axis, down)
        shard = jnp.concatenate([before, shard, after], axis=dim)
    return shard


def phase_tables(first_freq, freq_count, freq_total, windows):
    frequency = jnp.arange(freq_count, dtype=jnp.float32) + first_freq + 1.0
    window = jnp.arange(windows, dtype=jnp.float32) + 0.5
    phases = 4.0 * math.pi / freq_total * frequency[:, None] * window[None, :]
    return (jnp.cos(phases), -jnp.sin(phases))


def apply_green(spectra, green, onehot, block):
    freqs = spectra.shape[1]
    columns = spectra.reshape(2, freqs, -1, block)
    summed = jnp.einsum("skc,rfcx->rfskx", onehot, columns, precision=PRECISE)
    green_real = green[:, :, :, :block]
    green_imag = green[:, :, :, block:]

    def product(left, right):
        return jnp.einsum("fkyx,fskx->fsy", left, right, precision=PRECISE)

    real_part = product(green_real, summed[0]) - product(green_imag, summed[1])
    imag_part = product(green_real, summed[1]) + product(green_imag, summed[0])
    return jnp.stack([real_part, imag_part]).reshape(2, freqs, -1)


def adjoint_green(misfit, green, onehot, block):
    freqs = misfit.shape[1]
    blocks = misfit.reshape(2, freqs, -1, block)
    green_real = green[:, :, :, :block]
    green_imag = green[:, :, :, block:]

    def product(left, right):
        return jnp.einsum("fkyx,fsy->fskx", left, right, precision=PRECISE)

    real_part = product(green_real, blocks[0]) + product(green_imag, blocks[1])
    imag_part = product(green_real, blocks[1]) - product(green_imag, blocks[0])
    result = jnp.einsum(
        "skc,rfskx->rfcx", onehot, jnp.stack([real_part, imag_part]), precision=PRECISE
    )
    return result.reshape(2, freqs, -1)


def local(slip, green, pattern, observed, adjacency, smooth_weight):
    smoothing = smooth_weight[0]
    n_freq = lax.axis_size("freq")
    n_tri = lax.axis_size("tri")
    freq_dev = green.shape[0]
    classes = green.shape[1]
    block = green.shape[2]
    freq_total = freq_dev * n_freq
    windows, columns = slip.shape
    tri_dev = columns // 2
    per_block = columns // block
    station_rows = pattern.shape[0]
    layout = pattern.reshape(station_rows, n_freq, n_tri, per_block)
    layout = lax.dynamic_index_in_dim(layout, lax.axis_index("tri"), 2, keepdims=False)
    layout = layout.reshape(station_rows, n_freq * per_block)
    onehot = (layout[:, None, :] == jnp.arange(classes, dtype=jnp.int32)[None, :, None]).astype(
        jnp.float32
    )
    cos_table, sin_table = phase_tables(0, freq_total, freq_total, windows)

    def to_spectra(field):
        spread = jnp.stack(
            [
                jnp.dot(cos_table, field, precision=PRECISE),
                jnp.dot(sin_table, field, precision=PRECISE),
            ]
        )
        return lax.all_to_all(spread, "freq", split_axis=1, concat_axis=2, tiled=True)

    def predict(field):
        partial_data = apply_green(to_spectra(field), green, onehot, block)
        return lax.psum(partial_data, "tri")

    predicted = predict(slip)
    residual = predicted - observed
    adjoint_part = adjoint_green(residual, green, onehot, block)
    adjoint_part = lax.psum(adjoint_part, "sta")
    by_frequency = lax.all_to_all(adjoint_part, "freq", split_axis=2, concat_axis=1, tiled=True)
    data_grad = jnp.dot(cos_table.T, by_frequency[0], precision=PRECISE) + jnp.dot(
        sin_table.T, by_frequency[1], precision=PRECISE
    )
    padded = padded_2(slip, ((("freq", "tri"), 1),), columns)
    padded_grid = padded.reshape(windows, 3 * tri_dev, 2)
    device_pos = lax.axis_index(("freq", "tri"))
    local_index = adjacency - (device_pos * tri_dev - tri_dev)
    picked = jnp.take(padded_grid, local_index, axis=1)
    neighbour_mean = (picked[:, 0] + picked[:, 1] + picked[:, 2]) / 3.0
    gradient = data_grad + smoothing * (slip - neighbour_mean.reshape(windows, columns))
    numerator = lax.psum(jnp.sum(gradient * gradient), ("freq", "tri"))
    image_data = predict(gradient)
    image_total = lax.psum(jnp.sum(image_data * image_data), ("freq", "sta"))
    denominator = image_total + smoothing * numerator
    step_length = numerator / denominator
    new_slip = jnp.maximum(slip - step_length * gradient, 0.0)
    return (new_slip, residual)


def solution(mesh):
    placed = (
        P(None, ("grp", "freq", "tri")),
        P("freq", None, None, None),
        P("sta", None),
        P(None, ("grp", "freq"), "sta"),
        P(None, ("freq", "tri")),
        P("grp"),
    )
    return jax.shard_map(
        local,
        mesh=mesh,
        in_specs=placed,
        out_specs=(P(None, ("grp", "freq", "tri")), P(None, ("grp", "freq"), "sta")),
        check_vma=False,
    )
```

profile of v0, /device:TPU:0, one launch (start us, length us, event | category | flops | bytes accessed | tf_op | source)
XLA Modules:
  0.0 188.8 jit_solution(9437272294900684459)
XLA Ops:
  7.2 5.0 %collective-permute-start = (f32[8,512]{1,0:T(8,128)}, f32[8,512]{1,0:T(8,128)S(1)}, u32[]{:S(2)}, u32[]{:S(2)}) collective-permute-start(f32[8,512]{1,0:T(8,128)} %param.6), channel_id=1, source_target_pairs={{0,2},{2,4},{4,6},{6,8},{8,10},{10,12},{12,14},{1,3},{3,5},{5,7},{... | collective-permute-start | bytes 49160 | tf_op jit(solution)/shard_map/ppermute | solution.py:18
  16.4 6.9 %all-to-all-start = ((f32[2,32,512]{2,0,1:T(2,128)}), f32[2,32,512]{2,0,1:T(2,128)S(1)}, u32[]{:S(2)}, u32[]{:S(2)}) async-start(f32[2,32,512]{2,0,1:T(2,128)} %copy.59), calls=%async_computation | async-start | bytes 262144 | tf_op jit(solution)/shard_map/all_to_all | solution.py:90
  26.2 3.1 %all-to-all-done = f32[2,32,512]{2,0,1:T(2,128)S(1)} async-done(((f32[2,32,512]{2,0,1:T(2,128)}), f32[2,32,512]{2,0,1:T(2,128)S(1)}, u32[]{:S(2)}, u32[]{:S(2)}) %all-to-all-start) | async-done | bytes 131104 | tf_op jit(solution)/shard_map/all_to_all | solution.py:90
  30.5 1.9 %fusion.43 = f32[8,32,64]{2,1,0:T(8,128)S(1)} fusion(f32[8,8,64,128]{3,2,1,0:T(8,128)S(1)} %copy-done, f32[2,8,32,8,64]{4,2,3,1,0:T(8,128)S(1)} %convolution_bitcast_fusion.1), kind=kOutput, calls=%fused_computation.36 | convolution fusion | flops 100663296 | bytes 3211264 | tf_op jit(solution)/shard_map/fkyx,fskx->fsy/dot_general | solution.py:39
  32.4 1.9 %fusion.46 = f32[8,32,64]{2,1,0:T(8,128)S(1)} fusion(f32[8,8,64,128]{3,2,1,0:T(8,128)S(1)} %copy-done, f32[2,8,32,8,64]{4,2,3,1,0:T(8,128)S(1)} %convolution_bitcast_fusion.1), kind=kOutput, calls=%fused_computation.37 | convolution fusion | flops 100663296 | bytes 3211264 | tf_op jit(solution)/shard_map/fkyx,fskx->fsy/dot_general | solution.py:39
  34.4 2.2 %fusion.76 = f32[8,32,64]{2,1,0:T(8,128)S(1)} fusion(f32[8,32,64]{2,1,0:T(8,128)S(1)} %fusion.43, f32[8,8,64,128]{3,2,1,0:T(8,128)S(1)} %copy-done, f32[2,8,32,8,64]{4,2,3,1,0:T(8,128)S(1)} %convolution_bitcast_fusion.1), kind=kOutput, calls=%fused_computation.47 | convolution fusion | flops 100679680 | bytes 3342336 | tf_op jit(solution)/shard_map/fkyx,fskx->fsy/dot_general | solution.py:39
  36.7 3.4 %fusion.73 = f32[8,32,64]{2,1,0:T(8,128)S(1)} fusion(f32[8,32,64]{2,1,0:T(8,128)S(1)} %fusion.46, f32[8,8,64,128]{3,2,1,0:T(8,128)S(1)} %copy-done, f32[2,8,32,8,64]{4,2,3,1,0:T(8,128)} %copy-done.2), kind=kOutput, calls=%fused_computation.46 | convolution fusion | flops 100679680 | bytes 3276800 | tf_op jit(solution)/shard_map/fkyx,fskx->fsy/dot_general | solution.py:39
  41.4 3.2 %gather_fusion = f32[768,8,2]{1,2,0:T(2,128)} fusion(f32[8,768,2]{0,2,1:T(2,128)S(1)} %bitcast.129, s32[1024]{0:T(1024)S(1)} %pad_clamp_fusion), kind=kCustom, calls=%fused_computation | custom fusion | bytes 101376 | tf_op jit(solution)/shard_map/jit(_take)/gather | solution.py:108
  44.6 1.9 copy.70
  46.5 14.1 %all-reduce.4.cloned.1.call-done = f32[2,8,2048]{2,1,0:T(8,128)} async-done(((f32[2,8,2048]{2,1,0:T(8,128)}), f32[2,8,2048]{2,1,0:T(8,128)}) %all-reduce.4.cloned.1.call-update) | async-done | bytes 131088 | tf_op jit(solution)/shard_map/psum | solution.py:94
  69.7 2.3 %copy.91 = f32[2,8,32,64]{1,0,3,2:T(2,128)} copy(f32[2,8,32,64]{3,2,1,0:T(8,128)S(1)} %fusion.40) | data formatting | bytes 262144 | tf_op jit(solution)/shard_map/reshape | solution.py:60
  72.1 21.3 %all-reduce.6.cloned.1.call-done = f32[2,8,2048]{1,0,2:T(2,128)} async-done(((f32[2,8,2048]{1,0,2:T(2,128)}), f32[2,8,2048]{1,0,2:T(2,128)}) %all-reduce.6.cloned.1.call-update) | async-done | bytes 131088 | tf_op jit(solution)/shard_map/psum | solution.py:99
  93.4 5.6 %reshape.99 = f32[4,1,8192]{2,1,0:T(1,128)} reshape(f32[2048,2,8]{2,1,0:T(2,128)} %bitcast.133) | data formatting | bytes 262144
  99.0 4.9 %all-to-all-start.1 = ((f32[4,1,8192]{2,1,0:T(1,128)}), f32[4,1,8192]{2,1,0:T(1,128)S(1)}, u32[]{:S(2)}, u32[]{:S(2)}) async-start(f32[4,1,8192]{2,1,0:T(1,128)} %reshape.99), calls=%async_computation.1 | async-start | bytes 262144 | tf_op jit(solution)/shard_map/all_to_all | solution.py:100
  104.1 6.1 %all-to-all-done.1 = f32[4,1,8192]{2,1,0:T(1,128)S(1)} async-done(((f32[4,1,8192]{2,1,0:T(1,128)}), f32[4,1,8192]{2,1,0:T(1,128)S(1)}, u32[]{:S(2)}, u32[]{:S(2)}) %all-to-all-start.1) | async-done | bytes 131104 | tf_op jit(solution)/shard_map/all_to_all | solution.py:100
  111.7 4.6 %reshape.100 = f32[2048,2,8]{2,1,0:T(2,128)} reshape(f32[4,8192]{1,0:T(4,128)S(1)} %reduce) | data formatting | bytes 262144
  116.3 2.6 %copy.92 = f32[2,8,4,512]{3,2,1,0:T(4,128)S(1)} copy(f32[2,8,4,512]{1,0,3,2:T(2,128)} %bitcast.132) | data formatting | bytes 262144 | tf_op jit(solution)/shard_map/all_to_all | solution.py:100
  121.0 8.6 %all_to_all.45 = f32[2,32,512]{2,0,1:T(2,128)S(1)} all-to-all(f32[2,32,512]{2,0,1:T(2,128)S(1)} %copy.73), channel_id=1, replica_groups=mesh['grp'=2,'freq'=4,'tri'=2,'sta'=2] {'freq'}, dimensions={1} | all-to-all | bytes 262144 | tf_op jit(solution)/shard_map/all_to_all | solution.py:90
  130.9 1.9 %fusion.49 = f32[8,32,64]{2,1,0:T(8,128)S(1)} fusion(f32[8,8,64,128]{3,2,1,0:T(8,128)S(1)} %copy-done, f32[2,8,32,8,64]{4,2,3,1,0:T(8,128)S(1)} %convolution_bitcast_fusion), kind=kOutput, calls=%fused_computation.38 | convolution fusion | flops 100663296 | bytes 3211264 | tf_op jit(solution)/shard_map/fkyx,fskx->fsy/dot_general | solution.py:39
  132.8 1.9 %fusion.52 = f32[8,32,64]{2,1,0:T(8,128)S(1)} fusion(f32[8,8,64,128]{3,2,1,0:T(8,128)S(1)} %copy-done, f32[2,8,32,8,64]{4,2,3,1,0:T(8,128)S(1)} %convolution_bitcast_fusion), kind=kOutput, calls=%fused_computation.39 | convolution fusion | flops 100663296 | bytes 3211264 | tf_op jit(solution)/shard_map/fkyx,fskx->fsy/dot_general | solution.py:39
  134.8 2.2 %fusion.70 = f32[8,32,64]{2,1,0:T(8,128)S(1)} fusion(f32[8,32,64]{2,1,0:T(8,128)S(1)} %fusion.49, f32[8,8,64,128]{3,2,1,0:T(8,128)S(1)} %copy-done, f32[2,8,32,8,64]{4,2,3,1,0:T(8,128)S(1)} %convolution_bitcast_fusion), kind=kOutput, calls=%fused_computation.45 | convolution fusion | flops 100679680 | bytes 3342336 | tf_op jit(solution)/shard_map/fkyx,fskx->fsy/dot_general | solution.py:39
  137.0 3.4 %fusion.67 = f32[8,32,64]{2,1,0:T(8,128)S(1)} fusion(f32[8,32,64]{2,1,0:T(8,128)S(1)} %fusion.52, f32[8,8,64,128]{3,2,1,0:T(8,128)S(1)} %copy-done, f32[2,8,32,8,64]{4,2,3,1,0:T(8,128)} %copy-done.1), kind=kOutput, calls=%fused_computation.44 | convolution fusion | flops 100679680 | bytes 3276800 | tf_op jit(solution)/shard_map/fkyx,fskx->fsy/dot_general | solution.py:39
  141.2 20.3 %psum.37 = f32[]{:T(128)} all-reduce(f32[]{:T(128)} %get-tuple-element.8), channel_id=1, replica_groups=mesh['grp'=2,'freq'=4,'tri'=2,'sta'=2] {'freq','tri'}, use_global_device_ids=true, to_apply=%region_3.4 | all-reduce | flops 1 | bytes 8 | tf_op jit(solution)/shard_map/psum | solution.py:111
  164.1 16.4 %psum.39 = f32[]{:T(128)} all-reduce(f32[]{:T(128)} %multiply_reduce_fusion), channel_id=1, replica_groups=mesh['grp'=2,'freq'=4,'tri'=2,'sta'=2] {'freq','sta'}, use_global_device_ids=true, to_apply=%region_6.7 | all-reduce | flops 1 | bytes 8 | tf_op jit(solution)/shard_map/psum | solution.py:113
  (88 shorter events, 26.5 us)
Async XLA Ops:
  7.2 23.3 %copy-start = (f32[8,8,64,128]{3,2,1,0:T(8,128)S(1)}, f32[8,8,64,128]{3,2,1,0:T(8,128)}, u32[]{:S(2)}) copy-start(f32[8,8,64,128]{3,2,1,0:T(8,128)} %param.7) | copy-start | bytes 6291460
  7.2 33.9 %collective-permute-start = (f32[8,512]{1,0:T(8,128)}, f32[8,512]{1,0:T(8,128)S(1)}, u32[]{:S(2)}, u32[]{:S(2)}) collective-permute-start(f32[8,512]{1,0:T(8,128)} %param.6), channel_id=1, source_target_pairs={{0,2},{2,4},{4,6},{6,8},{8,10},{10,12},{12,14},{1,3},{3,5},{5,7},{... | collective-permute-start | bytes 49160 | tf_op jit(solution)/shard_map/ppermute | solution.py:18
  12.2 28.9 %collective-permute-start.1 = (f32[8,512]{1,0:T(8,128)}, f32[8,512]{1,0:T(8,128)S(1)}, u32[]{:S(2)}, u32[]{:S(2)}) collective-permute-start(f32[8,512]{1,0:T(8,128)} %param.6), channel_id=1, source_target_pairs={{2,0},{4,2},{6,4},{8,6},{10,8},{12,10},{14,12},{3,1},{5,3},{7,5},{... | collective-permute-start | bytes 49160 | tf_op jit(solution)/shard_map/ppermute | solution.py:19
  13.5 1.1 copy-start.9
  13.5 1.1 copy-start.11
  16.4 12.8 %all-to-all-start = ((f32[2,32,512]{2,0,1:T(2,128)}), f32[2,32,512]{2,0,1:T(2,128)S(1)}, u32[]{:S(2)}, u32[]{:S(2)}) async-start(f32[2,32,512]{2,0,1:T(2,128)} %copy.59), calls=%async_computation | async-start | bytes 262144 | tf_op jit(solution)/shard_map/all_to_all | solution.py:90
  23.3 37.2 %all-reduce.4.cloned.1.call-start = ((), (), s32[]{:S(2)}) async-start(), calls=%async_computation.3 | async-start | bytes 262144 | tf_op jit(solution)/shard_map/psum | solution.py:94
  25.5 6.9 %copy-start.5 = (s32[32,32]{1,0:T(8,128)}, s32[32,32]{1,0:T(8,128)S(1)}, u32[]{:S(2)}) copy-start(s32[32,32]{1,0:T(8,128)S(1)} %copy.62) | copy-start | bytes 12292
  30.5 3.9 %copy-start.2 = (f32[2,8,32,8,64]{4,2,3,1,0:T(8,128)}, f32[2,8,32,8,64]{4,2,3,1,0:T(8,128)S(1)}, u32[]{:S(2)}) copy-start(f32[2,8,32,8,64]{4,2,3,1,0:T(8,128)S(1)} %convolution_bitcast_fusion.1) | copy-start | bytes 3145732
  36.6 4.5 %copy-start.4 = (f32[8,512]{1,0:T(8,128)S(1)}, f32[8,512]{1,0:T(8,128)}, u32[]{:S(2)}) copy-start(f32[8,512]{1,0:T(8,128)} %param.6) | copy-start | bytes 49156
  40.8 52.6 %all-reduce.6.cloned.1.call-start = ((), (), s32[]{:S(2)}) async-start(), calls=%async_computation.4 | async-start | bytes 4194304 | tf_op jit(solution)/shard_map/psum | solution.py:99
  41.4 19.2 %copy-start.8 = (f32[2,8,2048]{2,1,0:T(8,128)S(1)}, f32[2,8,2048]{2,1,0:T(8,128)}, u32[]{:S(2)}) copy-start(f32[2,8,2048]{2,1,0:T(8,128)} %param.9) | copy-start | bytes 393220
  61.5 4.8 %copy-start.3 = (f32[2,8,2048]{2,1,0:T(8,128)}, f32[2,8,2048]{2,1,0:T(8,128)S(1)}, u32[]{:S(2)}) copy-start(f32[2,8,2048]{2,1,0:T(8,128)S(1)} %sub.28) | copy-start | bytes 393220
  67.5 1.2 copy-start.6
  69.7 2.3 %copy-start.7 = (f32[3,256,8,2]{1,2,3,0:T(8,128)S(1)}, f32[3,256,8,2]{1,2,3,0:T(8,128)}, u32[]{:S(2)}) copy-start(f32[3,256,8,2]{1,2,3,0:T(8,128)} %copy.70) | copy-start | bytes 147460
  69.7 2.3 %copy-start.13 = (pred[3,256]{1,0:T(4,128)(4,1)S(1)}, pred[3,256]{1,0:T(4,128)(4,1)}, u32[]{:S(2)}) copy-start(pred[3,256]{1,0:T(4,128)(4,1)} %get-tuple-element.2) | copy-start | bytes 2308
  99.0 11.2 %all-to-all-start.1 = ((f32[4,1,8192]{2,1,0:T(1,128)}), f32[4,1,8192]{2,1,0:T(1,128)S(1)}, u32[]{:S(2)}, u32[]{:S(2)}) async-start(f32[4,1,8192]{2,1,0:T(1,128)} %reshape.99), calls=%async_computation.1 | async-start | bytes 262144 | tf_op jit(solution)/shard_map/all_to_all | solution.py:100
  103.8 58.1 %all-reduce.8.cloned.1.call-start = ((), (), s32[]{:S(2)}) async-start(), calls=%async_computation.5 | async-start | bytes 262144 | tf_op jit(solution)/shard_map/psum | solution.py:94
  111.7 7.3 %copy-start.10 = (f32[32]{0:T(128)S(1)}, f32[32]{0:T(128)}, u32[]{:S(2)}) copy-start(f32[32]{0:T(128)} %copy-done.9) | copy-start | bytes 388
  111.7 7.3 %copy-start.12 = (f32[8]{0:T(128)S(1)}, f32[8]{0:T(128)}, u32[]{:S(2)}) copy-start(f32[8]{0:T(128)} %copy-done.11) | copy-start | bytes 100
  130.9 3.9 %copy-start.1 = (f32[2,8,32,8,64]{4,2,3,1,0:T(8,128)}, f32[2,8,32,8,64]{4,2,3,1,0:T(8,128)S(1)}, u32[]{:S(2)}) copy-start(f32[2,8,32,8,64]{4,2,3,1,0:T(8,128)S(1)} %convolution_bitcast_fusion) | copy-start | bytes 3145732
Sparse Core Ops, SparseCore 0:
  40.9 19.5 all-reduce.3
  72.1 21.2 all-reduce.5
  141.3 20.5 all-reduce.7
where the time goes:
time: 190 us; the launch traced here: 189 us
  blocking collectives  45.3 us (24%)
  waiting for transfers between devices  45.1 us (24%)
  matrix products  31.2 us (16%)
  local copies, waits for them, and re-layouts  25.5 us (13%)
  starting transfers between devices  18.3 us (10%)
  between operations  16.7 us (9%)
  other arithmetic  6.71 us (4%)
    psum x1, waiting for transfers between devices, local(): adjoint_part = lax.psum(adjoint_part, 'sta')  21.3 us
    psum x1, blocking collectives, local(): numerator = lax.psum(jnp.sum(gradient * gradient), ('freq', 'tri'))  20.3 us
    dot_general x8, matrix products, product(): return jnp.einsum('fkyx,fskx->fsy', left, right, precision=PRECISE)  18.8 us
    psum x1, blocking collectives, local(): image_total = lax.psum(jnp.sum(image_data * image_data), ('freq', 'sta'))  16.4 us
    psum x2, waiting for transfers between devices, predict(): return lax.psum(partial_data, 'tri')  14.5 us
    unnamed x31, local copies, waits for them, and re-layouts  11 us
    all_to_all x1, blocking collectives, to_spectra(): lax.all_to_all(spread, 'freq', split_axis=1, concat_axis=2, tiled=True)  8.61 us
    all_to_all x1, starting transfers between devices, to_spectra(): lax.all_to_all(spread, 'freq', split_axis=1, concat_axis=2, tiled=True)  6.93 us
  transfers between devices with their start and end apart: 7, of which 5 were waited for; matrix products, arithmetic and copies ran while one was open for 12% of the time, Pallas kernels for 0%

commit v1 on v0

v1 whole, which is shorter than its diff:
```python
import math

import jax
import jax.numpy as jnp
import numpy as np
from jax import lax
from jax.experimental import pallas as pl
from jax.experimental.pallas import tpu as pltpu
from jax.sharding import PartitionSpec as P

F32 = jnp.float32
BF16 = jnp.bfloat16
LANES = 128
CHUNK = 64
SHARD_ROWS = 16


def phase_table(freq_total, windows, block):
    frequency = np.arange(freq_total, dtype=np.float32) + np.float32(1.0)
    window = np.arange(windows, dtype=np.float32) + np.float32(0.5)
    phases = np.float32(4.0 * math.pi / freq_total) * frequency[:, None] * window[None, :]
    phases = phases.astype(np.float64)
    both = np.stack([np.cos(phases), -np.sin(phases)], axis=-1).astype(np.float32)
    return np.repeat(both, block, axis=-1)


def split(value):
    high = value.astype(BF16)
    return high, (value - high.astype(F32)).astype(BF16)


def low_lanes(shape, block):
    return lax.broadcasted_iota(jnp.int32, shape, len(shape) - 1) < block


def spread_columns(read, parts, spread):
    def one(p, carry):
        value = read(p)
        for j in range(value.shape[1] // LANES):
            piece = value[:, j * LANES : (j + 1) * LANES]
            turned = pltpu.roll(piece, LANES // 2, 1)
            low = low_lanes(piece.shape, LANES // 2)
            row = (p * (value.shape[1] // LANES) + j) * 16
            row = row if isinstance(row, int) else pl.multiple_of(row, 16)
            spread[pl.ds(row, 8), :] = jnp.where(low, piece, turned)
            spread[pl.ds(row + 8, 8), :] = jnp.where(low, turned, piece)
        return carry

    if parts <= 8:
        for p in range(parts):
            one(p, 0)
    else:
        lax.fori_loop(0, parts, one, 0)


def onehot_of(pattern, classes):
    doubled = jnp.concatenate([pattern, pattern], axis=1)
    return jnp.concatenate(
        [(doubled == k).astype(F32).astype(BF16) for k in range(classes)], axis=0
    )


def over_chunks(count, step):
    if count == 1:
        step(0)
    else:
        lax.fori_loop(0, count, lambda n, carry: (step(n), carry)[1], 0)


def pattern_sums(spread, table, first, pattern_ref, summed, freqs, classes):
    windows = table.shape[1]

    def step(n):
        base = n * CHUNK * windows
        fields = [spread[pl.ds(base + w, CHUNK, stride=windows), :] for w in range(windows)]
        spectra = []
        for f in range(freqs):
            row = table[first + f]
            total = row[0:1] * fields[0]
            for w in range(1, windows):
                total = total + row[w : w + 1] * fields[w]
            spectra.append(jnp.concatenate(split(total), axis=0))
        product = jnp.dot(
            onehot_of(pattern_ref[n], classes),
            jnp.concatenate(spectra, axis=1),
            preferred_element_type=F32,
        )
        if isinstance(n, int):
            summed[...] = product
        else:
            summed[...] += product

    chunks = pattern_ref.shape[0]
    if chunks > 1:
        summed[...] = jnp.zeros_like(summed)
    over_chunks(chunks, step)


def green_rows(green_ref, f):
    pieces = [
        jnp.concatenate(split(green_ref[f, k]), axis=0) for k in range(green_ref.shape[1])
    ]
    return jnp.concatenate(pieces, axis=1)


def predict_one(summed, green, f, classes, stations, block):
    value = summed[:, f * LANES : (f + 1) * LANES]
    sign = jnp.where(low_lanes(value.shape, block), 1.0, -1.0)
    real = value * sign
    imag = pltpu.roll(value, block, 1)
    rows = []
    for half in zip(split(real), split(imag)):
        for part in half:
            rows.append(
                jnp.concatenate(
                    [part[k * stations : (k + 1) * stations] for k in range(classes)], axis=1
                )
            )
    left = jnp.concatenate(rows, axis=0)
    out = lax.dot_general(left, green, (((1,), (1,)), ((), ())), preferred_element_type=F32)
    high = out[: 2 * stations]
    low = out[2 * stations :]
    cross = jnp.where(low_lanes(low.shape, block), low, 0.0)
    total = high + cross
    return total + pltpu.roll(total, block, 1)


def forward_kernel(
    windows,
    place,
    shards,
    green_ref,
    pattern_ref,
    observed,
    table,
    residual_out,
    partial_out,
    spread,
    summed,
    apart,
    fields,
):
    freqs, classes, block, _ = green_ref.shape
    stations = pattern_ref.shape[1]
    parts = shards.shape[0]
    first = place[0] * freqs
    half = place[2]
    low8 = low_lanes((8, LANES), block)
    for r in range(2):
        for j in range(stations // 2):
            piece = observed[r, :, j * LANES : (j + 1) * LANES]
            apart[r, 2 * j * freqs : (2 * j + 1) * freqs, :] = piece
            apart[r, (2 * j + 1) * freqs : (2 * j + 2) * freqs, :] = pltpu.roll(piece, block, 1)
    spread_columns(lambda p: shards[p, :windows, :], parts, spread)
    pattern_sums(spread, table, first, pattern_ref, summed, freqs, classes)
    for f in range(freqs):
        green = green_rows(green_ref, f)
        predicted = predict_one(summed, green, f, classes, stations, block)
        low = low_lanes(predicted.shape, block)
        seen = jnp.concatenate(
            [apart[r, pl.ds(f, stations, stride=freqs), :] for r in range(2)], axis=0
        )
        misfit = predicted - seen
        for r in range(2):
            apart[r, pl.ds(f, stations, stride=freqs), :] = misfit[r * stations : (r + 1) * stations]
        misfit = jnp.where(low, misfit, pltpu.roll(misfit, block, 1))
        high, rest = split(misfit)
        left = jnp.concatenate([high, rest[:, :block]], axis=1)
        right = jnp.concatenate([green, green[:block]], axis=0)
        out = jnp.dot(left, right, preferred_element_type=F32)
        sign = jnp.where(low_lanes((stations, LANES), block), 1.0, -1.0)
        for k in range(classes):
            real = out[:stations, k * LANES : (k + 1) * LANES]
            imag = out[stations:, k * LANES : (k + 1) * LANES]
            summed[k * stations : (k + 1) * stations, f * LANES : (f + 1) * LANES] = (
                real * sign + pltpu.roll(imag, block, 1)
            )
    for r in range(2):
        for j in range(stations // 2):
            even = apart[r, 2 * j * freqs : (2 * j + 1) * freqs, :]
            odd = apart[r, (2 * j + 1) * freqs : (2 * j + 2) * freqs, :]
            residual_out[r, :, j * LANES : (j + 1) * LANES] = jnp.where(
                low8, even, pltpu.roll(odd, block, 1)
            )

    right = jnp.concatenate(split(summed[...]), axis=0)
    per_part = shards.shape[2] // block
    chunk_parts = CHUNK // per_part

    def step(n):
        onehot = onehot_of(pattern_ref[n], classes)[:, :block].astype(F32).T.astype(BF16)
        left = jnp.concatenate([onehot, onehot], axis=1)
        adjoint = jnp.dot(left, right, preferred_element_type=F32)
        for w in range(windows):
            total = table[first, w : w + 1, :] * adjoint[:, :LANES]
            for f in range(1, freqs):
                total = total + table[first + f, w : w + 1, :] * adjoint[:, f * LANES : (f + 1) * LANES]
            fields[pl.ds(w, CHUNK, stride=windows), :] = total + pltpu.roll(total, block, 1)
        for q in range(chunk_parts):
            p = n * chunk_parts + q
            side = lax.rem(p // (parts // 2) + half, 2)
            slot = lax.rem(jnp.asarray(p, jnp.int32), parts // 2)
            for j in range(per_part // 2):
                row = (q * per_part + 2 * j) * windows
                partial_out[side, slot, :, j * LANES : (j + 1) * LANES] = jnp.where(
                    low8, fields[row : row + windows, :], fields[row + windows : row + 2 * windows, :]
                )

    over_chunks(pattern_ref.shape[0], step)


def smooth_kernel(windows, place, weight, shards, out):
    parts, _, width = shards.shape
    count = out.shape[0]
    pieces = width // LANES
    lane = lax.broadcasted_iota(jnp.int32, (windows, LANES), 1)

    def pick(source, index):
        return jnp.take_along_axis(source, index, axis=1, mode="promise_in_bounds")

    def one(slot, carry):
        p = place[2] * count + slot
        around = [jnp.maximum(p - 1, 0), p, jnp.minimum(p + 1, parts - 1)]
        source = [
            shards[a, :windows, j * LANES : (j + 1) * LANES] for a in around for j in range(pieces)
        ]
        for q in range(pieces):
            total = None
            for j in range(3):
                row = shards[p, windows + j : windows + j + 1, (q // 2) * LANES : (q // 2 + 1) * LANES]
                row = jnp.broadcast_to(row, (windows, LANES))
                target = pick(row, (q % 2) * (LANES // 2) + lane // 2).astype(jnp.int32)
                column = 2 * target + lane % 2 - (p - 1) * width
                inside = jnp.bitwise_and(column, LANES - 1)
                which = jnp.right_shift(column, 7)
                value = jnp.zeros((windows, LANES), F32)
                for v in range(q, q + 2 * pieces + 1):
                    value = jnp.where(which == v, pick(source[v], inside), value)
                total = value if total is None else total + value
            own = source[pieces + q]
            out[slot, :, q * LANES : (q + 1) * LANES] = weight[0] * (own - total / 3.0)
        return carry

    lax.fori_loop(0, count, one, 0)


def image_kernel(
    place, mine, other, green_ref, pattern_ref, table, own_out, sums_out, spread, summed
):
    freqs, classes, block, _ = green_ref.shape
    stations = pattern_ref.shape[1]
    count, windows, width = mine.shape
    first = place[0] * freqs
    half = place[2]

    def read(p):
        slot = p % count if isinstance(p, int) else lax.rem(p, count)
        return jnp.where(p // count == half, mine[slot], other[slot])

    spread_columns(read, 2 * count, spread)
    pattern_sums(spread, table, first, pattern_ref, summed, freqs, classes)
    me = place[1]
    slot = lax.rem(me, count)
    own_out[...] = jnp.where(me // count == half, mine[slot], other[slot])

    def squares(p, total):
        value = read(p)
        value = value * value
        for j in range(width // LANES):
            total = total + value[:, j * LANES : (j + 1) * LANES]
        return total

    numerator = lax.fori_loop(0, 2 * count, squares, jnp.zeros((windows, LANES), F32), unroll=count <= 4)
    image = jnp.zeros((8, LANES), F32)
    for f in range(freqs):
        predicted = predict_one(summed, green_rows(green_ref, f), f, classes, stations, block)
        predicted = predicted * predicted
        for j in range(predicted.shape[0] // 8):
            image = image + predicted[8 * j : 8 * j + 8]
    image = jnp.where(low_lanes(image.shape, block), image, 0.0)
    sums_out[0] = jnp.broadcast_to(jnp.sum(image), (8, LANES))
    sums_out[1] = jnp.broadcast_to(jnp.sum(numerator), (8, LANES))


def update_kernel(count, weight, *refs):
    sums, slip, own, out = refs[0], refs[1 + count], refs[2 + count], refs[3 + count]
    image = sums[0]
    for r in refs[1 : 1 + count]:
        image = image + r[...]
    numerator = sums[1]
    step = numerator / (image + weight[0] * numerator)
    step = jnp.concatenate([step] * (slip.shape[1] // LANES), axis=1)
    out[...] = jnp.maximum(slip[...] - step * own[...], 0.0)


SMEM = pl.BlockSpec(memory_space=pltpu.SMEM)
VMEM = pl.BlockSpec(memory_space=pltpu.VMEM)


def local(slip, green, pattern, observed, adjacency, smooth_weight, *, table):
    n_freq, n_tri, n_sta = (lax.axis_size(a) for a in ("freq", "tri", "sta"))
    parts = n_freq * n_tri
    count = parts // n_sta
    freqs, classes, block, _ = green.shape
    windows, columns = slip.shape
    stations, blocks = pattern.shape
    index = [lax.axis_index(a) for a in (("freq",), ("freq", "tri"), ("sta",))]
    place = jnp.stack(index).astype(jnp.int32)
    pattern = pattern.reshape(stations, blocks // CHUNK, CHUNK).transpose(1, 0, 2)
    limit = pltpu.CompilerParams(vmem_limit_bytes=48 * 2**20)

    triangles = adjacency.shape[1]
    packed = jnp.concatenate(
        [
            slip,
            jnp.pad(
                adjacency.astype(F32),
                ((0, SHARD_ROWS - windows - adjacency.shape[0]), (0, columns - triangles)),
            ),
        ],
        axis=0,
    )
    shards = lax.all_to_all(
        jnp.broadcast_to(packed[None], (parts,) + packed.shape), ("freq", "tri"), 0, 0, tiled=True
    )

    flops = 2 * freqs * 128 * 1024 * 256
    residual, partial = pl.pallas_call(
        lambda *refs: forward_kernel(windows, *refs),
        out_shape=(
            jax.ShapeDtypeStruct(observed.shape, F32),
            jax.ShapeDtypeStruct((n_sta, count, windows, columns), F32),
        ),
        in_specs=[SMEM] + [VMEM] * 5,
        out_specs=(VMEM, VMEM),
        scratch_shapes=[
            pltpu.VMEM((blocks * windows, LANES), F32),
            pltpu.VMEM((classes * stations, freqs * LANES), F32),
            pltpu.VMEM((2, stations * freqs, LANES), F32),
            pltpu.VMEM((CHUNK * windows, LANES), F32),
        ],
        compiler_params=limit,
        cost_estimate=pl.CostEstimate(flops=flops, bytes_accessed=4 * 2**20, transcendentals=0),
    )(place, shards, green, pattern, observed, table)

    smooth = pl.pallas_call(
        lambda *refs: smooth_kernel(windows, *refs),
        out_shape=jax.ShapeDtypeStruct((count, windows, columns), F32),
        in_specs=[SMEM, SMEM, VMEM],
        out_specs=VMEM,
        compiler_params=limit,
        cost_estimate=pl.CostEstimate(flops=10**6, bytes_accessed=4 * 2**20, transcendentals=0),
    )(place, smooth_weight, shards)

    cores = [(0, 1), (1, 0)]
    mine = partial[0] + lax.ppermute(partial[1], "sta", cores)

    def across(value):
        return [
            lax.ppermute(value, "freq", [(i, i ^ k) for i in range(n_freq)])
            for k in range(1, n_freq)
        ]

    if n_freq <= 8:
        mine = sum(across(mine), mine) + smooth
    else:
        mine = lax.psum(mine, "freq") + smooth
    other = lax.ppermute(mine, "sta", cores)

    own, sums = pl.pallas_call(
        image_kernel,
        out_shape=(
            jax.ShapeDtypeStruct(slip.shape, F32),
            jax.ShapeDtypeStruct((2, 8, LANES), F32),
        ),
        in_specs=[SMEM] + [VMEM] * 5,
        out_specs=(VMEM, VMEM),
        scratch_shapes=[
            pltpu.VMEM((blocks * windows, LANES), F32),
            pltpu.VMEM((classes * stations, freqs * LANES), F32),
        ],
        compiler_params=limit,
        cost_estimate=pl.CostEstimate(flops=flops, bytes_accessed=4 * 2**20, transcendentals=0),
    )(place, mine, other, green, pattern, table)

    image = sums[0] + lax.ppermute(sums[0], "sta", cores)
    if n_freq <= 8:
        others = across(image)
    else:
        image, others = lax.psum(image, "freq"), []
    sums = jnp.stack([image, sums[1]])
    new_slip = pl.pallas_call(
        lambda *refs: update_kernel(len(others), *refs),
        out_shape=jax.ShapeDtypeStruct(slip.shape, F32),
        in_specs=[SMEM] + [VMEM] * (3 + len(others)),
        out_specs=VMEM,
    )(smooth_weight, sums, *others, slip, own)
    return new_slip, residual


def solution(mesh):
    n_freq = mesh.shape["freq"]
    placed = (
        P(None, ("grp", "freq", "tri")),
        P("freq", None, None, None),
        P("sta", None),
        P(None, ("grp", "freq"), "sta"),
        P(None, ("freq", "tri")),
        P("grp"),
    )

    def step(slip, green, pattern, observed, adjacency, smooth_weight):
        windows, block = slip.shape[0], green.shape[2]
        table = phase_table(green.shape[0] // n_freq * n_freq, windows, block)

        def body(*args):
            return local(*args, table=jnp.asarray(table))

        return jax.shard_map(
            body,
            mesh=mesh,
            in_specs=placed,
            out_specs=(P(None, ("grp", "freq", "tri")), P(None, ("grp", "freq"), "sta")),
            check_vma=False,
        )(slip, green, pattern, observed, adjacency, smooth_weight)

    return step
```

time: 190 us -> 52.5 us (0.28)
  blocking collectives: 45.3 us -> 0 us
  matrix products: 31.2 us -> 0 us
  waiting for transfers between devices: 45.1 us -> 14.9 us
  local copies, waits for them, and re-layouts: 25.5 us -> 5.45 us
  between operations: 16.7 us -> 1.35 us
  Pallas kernels: 0 us -> 11.8 us
  other arithmetic: 6.71 us -> 2.13 us
  starting transfers between devices: 18.3 us -> 16.4 us
    psum x2 -> x0, blocking collectives: 36.7 us -> none  [the longest x1 20.3 us: local(): numerator = lax.psum(jnp.sum(gradient * gradient), ('freq', 'tri'))]
    psum x3 -> x0, waiting for transfers between devices: 35.9 us -> none  [the longest x1 21.3 us: local(): adjoint_part = lax.psum(adjoint_part, 'sta')]
    dot_general x21 -> x0, matrix products: 31.2 us -> none  [the longest x8 18.8 us: product(): return jnp.einsum('fkyx,fskx->fsy', left, right, precision=PRECISE)]
    pallas_call x0 -> x4, Pallas kernels: none -> 11.8 us  [the longest x1 6.1 us: local(): pl.pallas_call(lambda *refs: forward_kernel(windows, *refs), out_shape=(j...]
    all_to_all x1 -> x0, blocking collectives: 8.61 us -> none  [to_spectra(): lax.all_to_all(spread, 'freq', split_axis=1, concat_axis=2, tiled=True)]
    unnamed x31 -> x18, local copies, waits for them, and re-layouts: 11 us -> 4.71 us
    ppermute x2 -> x9, waiting for transfers between devices: 0.01 us -> 6.06 us  [the longest x6 2.56 us: across(): lax.ppermute(value, 'freq', [(i, i ^ k) for i in range(n_freq)])]
    gather x2 -> x0, local copies, waits for them, and re-layouts: 5.11 us -> none  [local(): picked = jnp.take(padded_grid, local_index, axis=1)]
  transfers between devices with their start and end apart: 7 -> 10, of which waited for: 5 -> 7; matrix products, arithmetic and copies ran while one was open for 12% -> 1% of each run, Pallas kernels for 0% -> 5%
where the time goes in v1:
time: 52.5 us; the launch traced here: 52 us
  starting transfers between devices  16.4 us (31%)
  waiting for transfers between devices  14.9 us (28%)
  Pallas kernels  11.8 us (22%)
  local copies, waits for them, and re-layouts  5.45 us (10%)
  other arithmetic  2.13 us (4%)
  between operations  1.35 us (3%)
    all_to_all x1, waiting for transfers between devices, local(): lax.all_to_all(jnp.broadcast_to(packed[None], (parts,) + packed.shape), (...  8.84 us
    ppermute x6, starting transfers between devices, across(): lax.ppermute(value, 'freq', [(i, i ^ k) for i in range(n_freq)])  8.84 us
    all_to_all x1, starting transfers between devices, local(): lax.all_to_all(jnp.broadcast_to(packed[None], (parts,) + packed.shape), (...  7.25 us
    pallas_call x1, Pallas kernels, local(): pl.pallas_call(lambda *refs: forward_kernel(windows, *refs), out_shape=(j...  6.1 us
    unnamed x18, local copies, waits for them, and re-layouts  4.71 us
    ppermute x6, waiting for transfers between devices, across(): lax.ppermute(value, 'freq', [(i, i ^ k) for i in range(n_freq)])  2.56 us
    pallas_call x1, Pallas kernels, local(): pl.pallas_call(lambda *refs: smooth_kernel(windows, *refs), out_shape=jax...  2.39 us
    pallas_call x1, Pallas kernels, local(): pl.pallas_call(image_kernel, out_shape=(jax.ShapeDtypeStruct(slip.shape,...  1.95 us
  transfers between devices with their start and end apart: 10, of which 7 were waited for; matrix products, arithmetic and copies ran while one was open for 1% of the time, Pallas kernels for 5%

profile of v1, /device:TPU:0, one launch (start us, length us, event | category | flops | bytes accessed | tf_op | source)
XLA Modules:
  0.0 52.0 jit_solution(12513994507115126963)
XLA Ops:
  0.6 0.7 %convert_element_type.5 = f32[3,256]{1,0:T(4,128)S(1)} convert(s32[3,256]{1,0:T(4,128)} %param.11) | non-fusion elementwise | flops 768 | bytes 6144 | tf_op jit(solution)/shard_map/convert_element_type | solution.py:317
  1.3 0.7 %select_maximum_fusion = f32[16,512]{1,0:T(8,128)S(1)} fusion(f32[3,256]{1,0:T(4,128)S(1)} %convert_element_type.5, f32[8,512]{1,0:T(8,128)} %refs_5_.2), kind=kLoop, calls=%fused_computation.3 | loop fusion | flops 24576 | bytes 52224 | tf_op jit(solution)/shard_map/concatenate | solution.py:313
  2.0 0.7 %broadcast_in_dim.2 = f32[8,16,512]{2,1,0:T(8,128)} broadcast(f32[16,512]{1,0:T(8,128)S(1)} %select_maximum_fusion), dimensions={1,2} | broadcast | bytes 294912 | tf_op jit(solution)/shard_map/broadcast_in_dim | solution.py:324
  2.8 7.3 %all-to-all-start = ((f32[8,16,512]{2,1,0:T(8,128)}), f32[8,16,512]{2,1,0:T(8,128)S(1)}, u32[]{:S(2)}, u32[]{:S(2)}) async-start(f32[8,16,512]{2,1,0:T(8,128)} %broadcast_in_dim.2), calls=%async_computation | async-start | bytes 524288 | tf_op jit(solution)/shard_map/all_to_all | solution.py:323
  10.1 8.8 %all-to-all-done.refs_1_.refs_2_ = f32[8,16,512]{2,1,0:T(8,128)S(1)} async-done(((f32[8,16,512]{2,1,0:T(8,128)}), f32[8,16,512]{2,1,0:T(8,128)S(1)}, u32[]{:S(2)}, u32[]{:S(2)}) %all-to-all-start) | async-done | bytes 262176 | tf_op jit(solution)/shard_map/all_to_all | solution.py:323
  18.9 1.6 %copy-done = f32[8,8,64,128]{3,2,1,0:T(8,128)S(1)} copy-done((f32[8,8,64,128]{3,2,1,0:T(8,128)S(1)}, f32[8,8,64,128]{3,2,1,0:T(8,128)}, u32[]{:S(2)}) %copy-start) | copy-done | bytes 2097176
  20.5 0.9 %copy-done.2 = f32[32,8,128]{2,1,0:T(8,128)S(1)} copy-done((f32[32,8,128]{2,1,0:T(8,128)S(1)}, f32[32,8,128]{2,1,0:T(8,128)}, u32[]{:S(2)}) %copy-start.2) | copy-done | bytes 131096
  21.4 0.9 %copy-done.3 = f32[2,8,2048]{2,1,0:T(8,128)S(1)} copy-done((f32[2,8,2048]{2,1,0:T(8,128)S(1)}, f32[2,8,2048]{2,1,0:T(8,128)}, u32[]{:S(2)}) %copy-start.3) | copy-done | bytes 131096
  22.3 0.7 %copy-done.4 = s32[32,64]{1,0:T(8,128)S(1)} copy-done((s32[32,64]{1,0:T(8,128)S(1)}, s32[32,64]{1,0:T(8,128)}, u32[]{:S(2)}) %copy-start.4) | copy-done | bytes 8216
  23.1 6.1 %shard_map.86 = (f32[2,8,2048]{2,1,0:T(8,128)}, f32[2,4,8,512]{3,2,1,0:T(8,128)S(1)}) custom-call(s32[3]{0:T(128)S(1)} %pad_add_fusion.refs_0_.place, f32[8,16,512]{2,1,0:T(8,128)S(1)} %all-to-all-done.refs_1_.refs_2_, f32[8,8,64,128]{3,2,1,0:T(8,128)S(1)} %copy-done, s32[1,32,64]{2,1,0:T(8,128)S(1)} %bitcast.13, f32[2,8,2048]{2,1,0:T(8,128)S(1)} %copy-done.3, ...), custom_call_target="tpu_custom_call" | custom-call | flops 536870912 | bytes 4194304 | tf_op jit(solution)/shard_map/pallas_call | solution.py:328
  29.2 1.2 %collective-permute-done = f32[4,8,512]{2,1,0:T(8,128)S(1)} collective-permute-done((f32[4,8,512]{2,1,0:T(8,128)S(1)}, f32[4,8,512]{2,1,0:T(8,128)S(1)}, u32[]{:S(2)}, u32[]{:S(2)}) %collective-permute-start) | collective-permute-done | bytes 65568 | tf_op jit(solution)/shard_map/ppermute | solution.py:356
  30.4 1.2 %collective-permute-start.3 = (f32[4,8,512]{2,1,0:T(8,128)S(1)}, f32[4,8,512]{2,1,0:T(8,128)S(1)}, u32[]{:S(2)}, u32[]{:S(2)}) collective-permute-start(f32[4,8,512]{2,1,0:T(8,128)S(1)} %bitcast_add_fusion), channel_id=1, source_target_pairs={{0,12},{4,8},{8,4},{12,0},{1,13},{5,9},{9,5},{13,1},{2,14},{6,10},... | collective-permute-start | bytes 196616 | tf_op jit(solution)/shard_map/ppermute | solution.py:360
  31.6 1.4 %collective-permute-start.2 = (f32[4,8,512]{2,1,0:T(8,128)S(1)}, f32[4,8,512]{2,1,0:T(8,128)S(1)}, u32[]{:S(2)}, u32[]{:S(2)}) collective-permute-start(f32[4,8,512]{2,1,0:T(8,128)S(1)} %bitcast_add_fusion), channel_id=1, source_target_pairs={{0,8},{4,12},{8,0},{12,4},{1,9},{5,13},{9,1},{13,5},{2,10},{6,14},... | collective-permute-start | bytes 196616 | tf_op jit(solution)/shard_map/ppermute | solution.py:360
  33.0 1.9 %collective-permute-start.1 = (f32[4,8,512]{2,1,0:T(8,128)S(1)}, f32[4,8,512]{2,1,0:T(8,128)S(1)}, u32[]{:S(2)}, u32[]{:S(2)}) collective-permute-start(f32[4,8,512]{2,1,0:T(8,128)S(1)} %bitcast_add_fusion), channel_id=1, source_target_pairs={{0,4},{4,0},{8,12},{12,8},{1,5},{5,1},{9,13},{13,9},{2,6},{6,2},{1... | collective-permute-start | bytes 196616 | tf_op jit(solution)/shard_map/ppermute | solution.py:360
  35.5 2.4 %shard_map.87 = f32[4,8,512]{2,1,0:T(8,128)S(1)} custom-call(s32[3]{0:T(128)S(1)} %pad_add_fusion.refs_0_.place, f32[1]{0:T(128)S(6)} %copy.9.refs_1_.refs_0_, f32[8,16,512]{2,1,0:T(8,128)S(1)} %all-to-all-done.refs_1_.refs_2_), custom_call_target="tpu_custom_call" | custom-call | flops 1000000 | bytes 4194304 | tf_op jit(solution)/shard_map/pallas_call | solution.py:346
  37.9 1.5 %collective-permute-done.2 = f32[4,8,512]{2,1,0:T(8,128)S(1)} collective-permute-done((f32[4,8,512]{2,1,0:T(8,128)S(1)}, f32[4,8,512]{2,1,0:T(8,128)S(1)}, u32[]{:S(2)}, u32[]{:S(2)}) %collective-permute-start.2) | collective-permute-done | bytes 65568 | tf_op jit(solution)/shard_map/ppermute | solution.py:360
  39.6 1.2 %collective-permute-done.4.other = f32[4,8,512]{2,1,0:T(8,128)S(1)} collective-permute-done((f32[4,8,512]{2,1,0:T(8,128)S(1)}, f32[4,8,512]{2,1,0:T(8,128)S(1)}, u32[]{:S(2)}, u32[]{:S(2)}) %collective-permute-start.4) | collective-permute-done | bytes 65568 | tf_op jit(solution)/shard_map/ppermute | solution.py:368
  40.8 1.9 %shard_map.88 = (f32[8,512]{1,0:T(8,128)S(1)}, f32[2,8,128]{2,1,0:T(8,128)S(1)}) custom-call(s32[3]{0:T(128)S(1)} %pad_add_fusion.refs_0_.place, f32[4,8,512]{2,1,0:T(8,128)S(1)} %add_add_fusion.mine, f32[4,8,512]{2,1,0:T(8,128)S(1)} %collective-permute-done.4.other, f32[8,8,64,128]{3,2,1,0:T(8,128)S(1)} %copy-done.1, s32[1,32,64]{2,1,0:T(8,128)S(1)} %bitcast.14, ...), custom_call_target="tpu_custom_call" | custom-call | flops 536870912 | bytes 4194304 | tf_op jit(solution)/shard_map/pallas_call | solution.py:370
  43.0 1.0 %collective-permute-done.5 = f32[8,128]{1,0:T(8,128)S(1)} collective-permute-done((f32[8,128]{1,0:T(8,128)S(1)}, f32[8,128]{1,0:T(8,128)S(1)}, u32[]{:S(2)}, u32[]{:S(2)}) %collective-permute-start.5) | collective-permute-done | bytes 4128 | tf_op jit(solution)/shard_map/ppermute | solution.py:386
  44.1 1.5 %collective-permute-start.8 = (f32[8,128]{1,0:T(8,128)S(1)}, f32[8,128]{1,0:T(8,128)S(1)}, u32[]{:S(2)}, u32[]{:S(2)}) collective-permute-start(f32[8,128]{1,0:T(8,128)S(1)} %fusion), channel_id=1, source_target_pairs={{0,12},{4,8},{8,4},{12,0},{1,13},{5,9},{9,5},{13,1},{2,14},{6,10},... | collective-permute-start | bytes 12296 | tf_op jit(solution)/shard_map/ppermute | solution.py:360
  45.5 2.9 %collective-permute-start.6 = (f32[8,128]{1,0:T(8,128)S(1)}, f32[8,128]{1,0:T(8,128)S(1)}, u32[]{:S(2)}, u32[]{:S(2)}) collective-permute-start(f32[8,128]{1,0:T(8,128)S(1)} %fusion), channel_id=1, source_target_pairs={{0,4},{4,0},{8,12},{12,8},{1,5},{5,1},{9,13},{13,9},{2,6},{6,2},{1... | collective-permute-start | bytes 12296 | tf_op jit(solution)/shard_map/ppermute | solution.py:360
  48.4 0.6 %pad_maximum_fusion.refs_1_ = f32[2,8,128]{2,1,0:T(8,128)} fusion(f32[1,8,128]{2,1,0:T(8,128)S(1)} %get-tuple-element.11, f32[1,8,128]{2,1,0:T(8,128)S(1)} %bitcast.15), kind=kLoop, calls=%fused_computation.5 | loop fusion | flops 2048 | bytes 16384 | tf_op jit(solution)/shard_map/stack | solution.py:391
  49.5 0.6 %collective-permute-done.7.refs_3_ = f32[8,128]{1,0:T(8,128)S(1)} collective-permute-done((f32[8,128]{1,0:T(8,128)S(1)}, f32[8,128]{1,0:T(8,128)S(1)}, u32[]{:S(2)}, u32[]{:S(2)}) %collective-permute-start.7) | collective-permute-done | bytes 4128 | tf_op jit(solution)/shard_map/ppermute | solution.py:360
  50.7 1.4 %shard_map.89 = f32[8,512]{1,0:T(8,128)} custom-call(f32[1]{0:T(128)S(6)} %copy.9.refs_1_.refs_0_, f32[2,8,128]{2,1,0:T(8,128)} %pad_maximum_fusion.refs_1_, f32[8,128]{1,0:T(8,128)} %copy-done.8, f32[8,128]{1,0:T(8,128)} %copy-done.7, f32[8,128]{1,0:T(8,128)} %copy-done.6, f32[8,512]{1,0:T(8,128)} %refs_5_.2, f32[8,512]{1,0:T(8,128)} %copy-done.5), custom_call_target="tpu_custom_call" | custom-call | tf_op jit(solution)/shard_map/pallas_call | solution.py:392
  (28 shorter events, 1.5 us)
Async XLA Ops:
  2.8 16.2 %all-to-all-start = ((f32[8,16,512]{2,1,0:T(8,128)}), f32[8,16,512]{2,1,0:T(8,128)S(1)}, u32[]{:S(2)}, u32[]{:S(2)}) async-start(f32[8,16,512]{2,1,0:T(8,128)} %broadcast_in_dim.2), calls=%async_computation | async-start | bytes 524288 | tf_op jit(solution)/shard_map/all_to_all | solution.py:323
  18.9 1.6 %copy-start = (f32[8,8,64,128]{3,2,1,0:T(8,128)S(1)}, f32[8,8,64,128]{3,2,1,0:T(8,128)}, u32[]{:S(2)}) copy-start(f32[8,8,64,128]{3,2,1,0:T(8,128)} %green_ref.1) | copy-start | bytes 6291460
  20.5 0.9 %copy-start.2 = (f32[32,8,128]{2,1,0:T(8,128)S(1)}, f32[32,8,128]{2,1,0:T(8,128)}, u32[]{:S(2)}) copy-start(f32[32,8,128]{2,1,0:T(8,128)} %constant.18.clone.refs_5_.table) | copy-start | bytes 393220
  21.4 0.9 %copy-start.3 = (f32[2,8,2048]{2,1,0:T(8,128)S(1)}, f32[2,8,2048]{2,1,0:T(8,128)}, u32[]{:S(2)}) copy-start(f32[2,8,2048]{2,1,0:T(8,128)} %refs_4_.1) | copy-start | bytes 393220
  22.3 0.7 %copy-start.4 = (s32[32,64]{1,0:T(8,128)S(1)}, s32[32,64]{1,0:T(8,128)}, u32[]{:S(2)}) copy-start(s32[32,64]{1,0:T(8,128)} %param.9) | copy-start | bytes 24580
  23.1 17.8 %copy-start.1 = (f32[8,8,64,128]{3,2,1,0:T(8,128)S(1)}, f32[8,8,64,128]{3,2,1,0:T(8,128)}, u32[]{:S(2)}) copy-start(f32[8,8,64,128]{3,2,1,0:T(8,128)} %green_ref.1) | copy-start | bytes 6291460
  29.2 1.3 %collective-permute-start = (f32[4,8,512]{2,1,0:T(8,128)S(1)}, f32[4,8,512]{2,1,0:T(8,128)S(1)}, u32[]{:S(2)}, u32[]{:S(2)}) collective-permute-start(f32[4,8,512]{2,1,0:T(8,128)S(1)} %slice_bitcast_fusion), channel_id=1, source_target_pairs={{0,1},{1,0},{2,3},{3,2},{4,5},{5,4},{6,7},{7,6},{8,9},{9,8},{10,11... | collective-permute-start | bytes 196616 | tf_op jit(solution)/shard_map/ppermute | solution.py:356
  30.4 7.5 %collective-permute-start.3 = (f32[4,8,512]{2,1,0:T(8,128)S(1)}, f32[4,8,512]{2,1,0:T(8,128)S(1)}, u32[]{:S(2)}, u32[]{:S(2)}) collective-permute-start(f32[4,8,512]{2,1,0:T(8,128)S(1)} %bitcast_add_fusion), channel_id=1, source_target_pairs={{0,12},{4,8},{8,4},{12,0},{1,13},{5,9},{9,5},{13,1},{2,14},{6,10},... | collective-permute-start | bytes 196616 | tf_op jit(solution)/shard_map/ppermute | solution.py:360
  31.6 7.8 %collective-permute-start.2 = (f32[4,8,512]{2,1,0:T(8,128)S(1)}, f32[4,8,512]{2,1,0:T(8,128)S(1)}, u32[]{:S(2)}, u32[]{:S(2)}) collective-permute-start(f32[4,8,512]{2,1,0:T(8,128)S(1)} %bitcast_add_fusion), channel_id=1, source_target_pairs={{0,8},{4,12},{8,0},{12,4},{1,9},{5,13},{9,1},{13,5},{2,10},{6,14},... | collective-permute-start | bytes 196616 | tf_op jit(solution)/shard_map/ppermute | solution.py:360
  33.0 6.5 %collective-permute-start.1 = (f32[4,8,512]{2,1,0:T(8,128)S(1)}, f32[4,8,512]{2,1,0:T(8,128)S(1)}, u32[]{:S(2)}, u32[]{:S(2)}) collective-permute-start(f32[4,8,512]{2,1,0:T(8,128)S(1)} %bitcast_add_fusion), channel_id=1, source_target_pairs={{0,4},{4,0},{8,12},{12,8},{1,5},{5,1},{9,13},{13,9},{2,6},{6,2},{1... | collective-permute-start | bytes 196616 | tf_op jit(solution)/shard_map/ppermute | solution.py:360
  39.5 1.3 %collective-permute-start.4 = (f32[4,8,512]{2,1,0:T(8,128)S(1)}, f32[4,8,512]{2,1,0:T(8,128)S(1)}, u32[]{:S(2)}, u32[]{:S(2)}) collective-permute-start(f32[4,8,512]{2,1,0:T(8,128)S(1)} %add_add_fusion.mine), channel_id=1, source_target_pairs={{0,1},{1,0},{2,3},{3,2},{4,5},{5,4},{6,7},{7,6},{8,9},{9,8},{10,11... | collective-permute-start | bytes 196616 | tf_op jit(solution)/shard_map/ppermute | solution.py:368
  42.8 1.3 %copy-start.5 = (f32[8,512]{1,0:T(8,128)}, f32[8,512]{1,0:T(8,128)S(1)}, u32[]{:S(2)}) copy-start(f32[8,512]{1,0:T(8,128)S(1)} %get-tuple-element.8.refs_6_) | copy-start | bytes 49156
  42.8 1.2 %collective-permute-start.5 = (f32[8,128]{1,0:T(8,128)S(1)}, f32[8,128]{1,0:T(8,128)S(1)}, u32[]{:S(2)}, u32[]{:S(2)}) collective-permute-start(f32[8,128]{1,0:T(8,128)S(1)} %get-tuple-element.10), channel_id=1, source_target_pairs={{0,1},{1,0},{2,3},{3,2},{4,5},{5,4},{6,7},{7,6},{8,9},{9,8},{10,11... | collective-permute-start | bytes 12296 | tf_op jit(solution)/shard_map/ppermute | solution.py:386
  44.1 5.4 %collective-permute-start.8 = (f32[8,128]{1,0:T(8,128)S(1)}, f32[8,128]{1,0:T(8,128)S(1)}, u32[]{:S(2)}, u32[]{:S(2)}) collective-permute-start(f32[8,128]{1,0:T(8,128)S(1)} %fusion), channel_id=1, source_target_pairs={{0,12},{4,8},{8,4},{12,0},{1,13},{5,9},{9,5},{13,1},{2,14},{6,10},... | collective-permute-start | bytes 12296 | tf_op jit(solution)/shard_map/ppermute | solution.py:360
  45.5 4.5 %collective-permute-start.7 = (f32[8,128]{1,0:T(8,128)S(1)}, f32[8,128]{1,0:T(8,128)S(1)}, u32[]{:S(2)}, u32[]{:S(2)}) collective-permute-start(f32[8,128]{1,0:T(8,128)S(1)} %fusion), channel_id=1, source_target_pairs={{0,8},{4,12},{8,0},{12,4},{1,9},{5,13},{9,1},{13,5},{2,10},{6,14},... | collective-permute-start | bytes 12296 | tf_op jit(solution)/shard_map/ppermute | solution.py:360
  45.5 4.5 %collective-permute-start.6 = (f32[8,128]{1,0:T(8,128)S(1)}, f32[8,128]{1,0:T(8,128)S(1)}, u32[]{:S(2)}, u32[]{:S(2)}) collective-permute-start(f32[8,128]{1,0:T(8,128)S(1)} %fusion), channel_id=1, source_target_pairs={{0,4},{4,0},{8,12},{12,8},{1,5},{5,1},{9,13},{13,9},{2,6},{6,2},{1... | collective-permute-start | bytes 12296 | tf_op jit(solution)/shard_map/ppermute | solution.py:360
  49.5 0.6 %copy-start.6 = (f32[8,128]{1,0:T(8,128)}, f32[8,128]{1,0:T(8,128)S(1)}, u32[]{:S(2)}) copy-start(f32[8,128]{1,0:T(8,128)S(1)} %collective-permute-done.8.refs_4_) | copy-start | bytes 12292
  50.0 0.6 %copy-start.7 = (f32[8,128]{1,0:T(8,128)}, f32[8,128]{1,0:T(8,128)S(1)}, u32[]{:S(2)}) copy-start(f32[8,128]{1,0:T(8,128)S(1)} %collective-permute-done.7.refs_3_) | copy-start | bytes 12292
  50.1 0.6 %copy-start.8 = (f32[8,128]{1,0:T(8,128)}, f32[8,128]{1,0:T(8,128)S(1)}, u32[]{:S(2)}) copy-start(f32[8,128]{1,0:T(8,128)S(1)} %collective-permute-done.6.refs_2_) | copy-start | bytes 12292

commit v2 on v1

v2 whole, which is shorter than its diff:
```python
import math

import jax
import jax.numpy as jnp
import numpy as np
from jax import lax
from jax.experimental import pallas as pl
from jax.experimental.pallas import tpu as pltpu
from jax.sharding import PartitionSpec as P

F32 = jnp.float32
BF16 = jnp.bfloat16
LANES = 128
CHUNK = 64


def phase_table(freq_total, windows, block):
    frequency = np.arange(freq_total, dtype=np.float32) + np.float32(1.0)
    window = np.arange(windows, dtype=np.float32) + np.float32(0.5)
    phases = np.float32(4.0 * math.pi / freq_total) * frequency[:, None] * window[None, :]
    phases = phases.astype(np.float64)
    both = np.stack([np.cos(phases), -np.sin(phases)], axis=-1).astype(np.float32)
    return np.repeat(both, block, axis=-1)


def split(value):
    high = value.astype(BF16)
    return high, (value - high.astype(F32)).astype(BF16)


def low_lanes(shape, block):
    return lax.broadcasted_iota(jnp.int32, shape, len(shape) - 1) < block


def spread_columns(read, parts, spread):
    def one(p, carry):
        value = read(p)
        for j in range(value.shape[1] // LANES):
            piece = value[:, j * LANES : (j + 1) * LANES]
            turned = pltpu.roll(piece, LANES // 2, 1)
            low = low_lanes(piece.shape, LANES // 2)
            row = (p * (value.shape[1] // LANES) + j) * 16
            row = row if isinstance(row, int) else pl.multiple_of(row, 16)
            spread[pl.ds(row, 8), :] = jnp.where(low, piece, turned)
            spread[pl.ds(row + 8, 8), :] = jnp.where(low, turned, piece)
        return carry

    if parts <= 8:
        for p in range(parts):
            one(p, 0)
    else:
        lax.fori_loop(0, parts, one, 0)


def onehot_of(pattern, classes):
    doubled = jnp.concatenate([pattern, pattern], axis=1)
    return jnp.concatenate([(doubled == k).astype(F32) for k in range(classes)], axis=0)


def over_chunks(count, step):
    if count == 1:
        step(0)
    else:
        lax.fori_loop(0, count, lambda n, carry: (step(n), carry)[1], 0)


def pack_kernel(slip, adjacency, out, held, sems):
    windows, columns = slip.shape
    neighbours, triangles = adjacency.shape
    copies = [
        pltpu.make_async_copy(adjacency, held, sems.at[0]),
        pltpu.make_async_copy(slip, out.at[:, pl.ds(0, columns)], sems.at[1]),
    ]
    for copy in copies:
        copy.start()
    copies[0].wait()
    out[:neighbours, columns:] = held[...].astype(F32)
    out[neighbours:, columns:] = jnp.zeros((windows - neighbours, triangles), F32)
    copies[1].wait()


def prepare_kernel(
    place,
    green_hbm,
    pattern_hbm,
    observed_hbm,
    table_hbm,
    green_out,
    onehot_out,
    turned_out,
    apart,
    table_out,
    green_ref,
    pattern_ref,
    observed,
    green_sems,
    sems,
):
    freqs, classes, block, _ = green_ref.shape
    chunks, stations, _ = pattern_ref.shape
    first = place[0] * freqs
    copies = [
        pltpu.make_async_copy(pattern_hbm, pattern_ref, sems.at[0]),
        pltpu.make_async_copy(observed_hbm, observed, sems.at[1]),
        pltpu.make_async_copy(table_hbm.at[pl.ds(first, freqs)], table_out, sems.at[2]),
    ]
    greens = [
        pltpu.make_async_copy(green_hbm.at[f], green_ref.at[f], green_sems.at[f])
        for f in range(freqs)
    ]
    for copy in copies + greens:
        copy.start()
    copies[0].wait()

    def step(n):
        onehot = onehot_of(pattern_ref[n], classes)
        onehot_out[n] = onehot.astype(BF16)
        turned = onehot[:, :block].T.astype(BF16)
        turned_out[n] = jnp.concatenate([turned, turned], axis=1)

    over_chunks(chunks, step)
    copies[1].wait()
    for r in range(2):
        for j in range(stations // 2):
            piece = observed[r, :, j * LANES : (j + 1) * LANES]
            apart[r, 2 * j * freqs : (2 * j + 1) * freqs, :] = piece
            apart[r, (2 * j + 1) * freqs : (2 * j + 2) * freqs, :] = pltpu.roll(piece, block, 1)
    copies[2].wait()
    for f in range(freqs):
        greens[f].wait()
        for k in range(classes):
            high, low = split(green_ref[f, k])
            green_out[f, :block, k * LANES : (k + 1) * LANES] = high
            green_out[f, block:, k * LANES : (k + 1) * LANES] = low


def pattern_sums(spread, table, onehot_ref, summed):
    freqs, windows, _ = table.shape
    chunks = onehot_ref.shape[0]

    def step(n):
        base = n * CHUNK * windows
        fields = [spread[pl.ds(base + w, CHUNK, stride=windows), :] for w in range(windows)]
        spectra = []
        for f in range(freqs):
            total = table[f, 0:1] * fields[0]
            for w in range(1, windows):
                total = total + table[f, w : w + 1] * fields[w]
            spectra.append(jnp.concatenate(split(total), axis=0))
        product = jnp.dot(
            onehot_ref[n], jnp.concatenate(spectra, axis=1), preferred_element_type=F32
        )
        if chunks == 1:
            summed[...] = product
        else:
            summed[...] += product

    if chunks > 1:
        summed[...] = jnp.zeros_like(summed)
    over_chunks(chunks, step)


def predict_one(summed, green, f, stations, block):
    value = summed[:, f * LANES : (f + 1) * LANES]
    sign = jnp.where(low_lanes(value.shape, block), 1.0, -1.0)
    real = value * sign
    imag = pltpu.roll(value, block, 1)
    classes = value.shape[0] // stations
    rows = []
    for half in zip(split(real), split(imag)):
        for part in half:
            rows.append(
                jnp.concatenate(
                    [part[k * stations : (k + 1) * stations] for k in range(classes)], axis=1
                )
            )
    left = jnp.concatenate(rows, axis=0)
    out = lax.dot_general(left, green, (((1,), (1,)), ((), ())), preferred_element_type=F32)
    high = out[: 2 * stations]
    low = out[2 * stations :]
    total = high + jnp.where(low_lanes(low.shape, block), low, 0.0)
    return total + pltpu.roll(total, block, 1)


def forward_kernel(windows, codes, place, *refs):
    count = max(len(codes), 1)
    pieces, refs = refs[:count], refs[count:]
    green, onehot_ref, turned_ref, apart, table = refs[:5]
    residual_out, partial_out = refs[5:7]
    if codes:
        shards, refs = refs[7], refs[8:]
        for (even, odd), piece in zip(codes, pieces):
            code = jnp.where(place[2] == 0, even, odd)
            shards[lax.bitwise_xor(place[1], code)] = piece[...]
    else:
        shards, refs = pieces[0], refs[7:]
    spread, summed, adjoint_rows, missed, fields = refs
    freqs, rows, _ = green.shape
    block = rows // 2
    stations = apart.shape[1] // freqs
    classes = summed.shape[0] // stations
    parts = shards.shape[0]
    half = place[2]
    width = partial_out.shape[3]
    low8 = low_lanes((freqs, LANES), block)
    spread_columns(lambda p: shards[p, :, :width], parts, spread)
    pattern_sums(spread, table, onehot_ref, summed)
    predicted = [predict_one(summed, green[f], f, stations, block) for f in range(freqs)]
    lefts = []
    for f in range(freqs):
        seen = jnp.concatenate(
            [apart[r, pl.ds(f, stations, stride=freqs), :] for r in range(2)], axis=0
        )
        misfit = predicted[f] - seen
        for r in range(2):
            missed[r, pl.ds(f, stations, stride=freqs), :] = misfit[r * stations : (r + 1) * stations]
        low = low_lanes(misfit.shape, block)
        misfit = jnp.where(low, misfit, pltpu.roll(misfit, block, 1))
        high, rest = split(misfit)
        lefts.append(jnp.concatenate([high, rest[:, :block]], axis=1))
    sign = jnp.where(low_lanes((stations, LANES), block), 1.0, -1.0)
    for f in range(freqs):
        right = jnp.concatenate([green[f], green[f, :block]], axis=0)
        out = jnp.dot(lefts[f], right, preferred_element_type=F32)
        at = slice(f * LANES, (f + 1) * LANES)
        for k in range(classes):
            real = out[:stations, k * LANES : (k + 1) * LANES]
            imag = out[stations:, k * LANES : (k + 1) * LANES]
            high, rest = split(real * sign + pltpu.roll(imag, block, 1))
            adjoint_rows[k * stations : (k + 1) * stations, at] = high
            adjoint_rows[(classes + k) * stations : (classes + k + 1) * stations, at] = rest
    for r in range(2):
        for j in range(stations // 2):
            even = missed[r, 2 * j * freqs : (2 * j + 1) * freqs, :]
            odd = missed[r, (2 * j + 1) * freqs : (2 * j + 2) * freqs, :]
            residual_out[r, :, j * LANES : (j + 1) * LANES] = jnp.where(
                low8, even, pltpu.roll(odd, block, 1)
            )

    per_part = width // block
    chunk_parts = CHUNK // per_part

    def step(n):
        adjoint = jnp.dot(turned_ref[n], adjoint_rows[...], preferred_element_type=F32)
        for w in range(windows):
            total = table[0, w : w + 1, :] * adjoint[:, :LANES]
            for f in range(1, freqs):
                total = total + table[f, w : w + 1, :] * adjoint[:, f * LANES : (f + 1) * LANES]
            fields[pl.ds(w, CHUNK, stride=windows), :] = total + pltpu.roll(total, block, 1)
        for q in range(chunk_parts):
            p = n * chunk_parts + q
            side = lax.rem(p // (parts // 2) + half, 2)
            slot = lax.rem(jnp.asarray(p, jnp.int32), parts // 2)
            for j in range(per_part // 2):
                row = (q * per_part + 2 * j) * windows
                partial_out[side, slot, :, j * LANES : (j + 1) * LANES] = jnp.where(
                    low8, fields[row : row + windows, :], fields[row + windows : row + 2 * windows, :]
                )

    over_chunks(turned_ref.shape[0], step)


def smooth_kernel(place, weight, shards, out):
    count, windows, width = out.shape
    parts = shards.shape[0]
    pieces = width // LANES
    lane = lax.broadcasted_iota(jnp.int32, (windows, LANES), 1)

    def pick(source, index):
        return jnp.take_along_axis(source, index, axis=1, mode="promise_in_bounds")

    def one(slot, carry):
        p = place[2] * count + slot
        around = [jnp.maximum(p - 1, 0), p, jnp.minimum(p + 1, parts - 1)]
        source = [shards[a, :, j * LANES : (j + 1) * LANES] for a in around for j in range(pieces)]
        for q in range(pieces):
            total = None
            for j in range(3):
                start = width + (q // 2) * LANES
                row = shards[p, j : j + 1, start : start + LANES]
                row = jnp.broadcast_to(row, (windows, LANES))
                target = pick(row, (q % 2) * (LANES // 2) + lane // 2).astype(jnp.int32)
                column = 2 * target + lane % 2 - (p - 1) * width
                inside = jnp.bitwise_and(column, LANES - 1)
                which = jnp.right_shift(column, 7)
                value = jnp.zeros((windows, LANES), F32)
                for v in range(q, q + 2 * pieces + 1):
                    value = jnp.where(which == v, pick(source[v], inside), value)
                total = value if total is None else total + value
            own = source[pieces + q]
            out[slot, :, q * LANES : (q + 1) * LANES] = weight[0] * (own - total / 3.0)
        return carry

    lax.fori_loop(0, count, one, 0)


def image_kernel(
    place, mine, other, green, onehot_ref, table, own_out, image_out, norm_out, spread, summed
):
    freqs, rows, _ = green.shape
    block = rows // 2
    classes = green.shape[2] // LANES
    stations = summed.shape[0] // classes
    count, windows, width = mine.shape
    half = place[2]

    def read(p):
        slot = p % count if isinstance(p, int) else lax.rem(p, count)
        return jnp.where(p // count == half, mine[slot], other[slot])

    spread_columns(read, 2 * count, spread)
    pattern_sums(spread, table, onehot_ref, summed)
    me = place[1]
    slot = lax.rem(me, count)
    own_out[...] = jnp.where(me // count == half, mine[slot], other[slot])

    def squares(p, total):
        value = read(p)
        value = value * value
        for j in range(width // LANES):
            total = total + value[:, j * LANES : (j + 1) * LANES]
        return total

    numerator = jnp.zeros((windows, LANES), F32)
    if count <= 4:
        for p in range(2 * count):
            numerator = squares(p, numerator)
    else:
        numerator = lax.fori_loop(0, 2 * count, squares, numerator)
    image = jnp.zeros((8, LANES), F32)
    for f in range(freqs):
        predicted = predict_one(summed, green[f], f, stations, block)
        predicted = predicted * predicted
        for j in range(predicted.shape[0] // 8):
            image = image + predicted[8 * j : 8 * j + 8]
    image = jnp.where(low_lanes(image.shape, block), image, 0.0)
    image_out[...] = jnp.broadcast_to(jnp.sum(image), image_out.shape)
    norm_out[...] = jnp.broadcast_to(jnp.sum(numerator), norm_out.shape)


SMEM = pl.BlockSpec(memory_space=pltpu.SMEM)
VMEM = pl.BlockSpec(memory_space=pltpu.VMEM)
HBM = pl.BlockSpec(memory_space=pltpu.HBM)


def local(slip, green, pattern, observed, adjacency, smooth_weight, *, table):
    n_freq, n_tri, n_sta = (lax.axis_size(a) for a in ("freq", "tri", "sta"))
    parts = n_freq * n_tri
    count = parts // n_sta
    freqs, classes, block, _ = green.shape
    windows, columns = slip.shape
    stations, blocks = pattern.shape
    index = [lax.axis_index(a) for a in (("freq",), ("freq", "tri"), ("sta",))]
    place = jnp.stack(index).astype(jnp.int32)
    pattern = pattern.reshape(stations, blocks // CHUNK, CHUNK).transpose(1, 0, 2)
    chunks = blocks // CHUNK
    grant = pltpu.CompilerParams(vmem_limit_bytes=(16 if chunks == 1 else 48) * 2**20)
    cores = [(0, 1), (1, 0)]
    shape = jax.ShapeDtypeStruct

    def across(value):
        return [
            lax.ppermute(value, "freq", [(i, i ^ k) for i in range(n_freq)])
            for k in range(1, n_freq)
        ]

    prepared = pl.pallas_call(
        prepare_kernel,
        out_shape=(
            shape((freqs, 2 * block, classes * 2 * block), BF16),
            shape((chunks, classes * stations, 2 * CHUNK), BF16),
            shape((chunks, CHUNK, 2 * classes * stations), BF16),
            shape((2, stations * freqs, LANES), F32),
            shape((freqs, windows, LANES), F32),
        ),
        in_specs=[SMEM] + [HBM] * 4,
        out_specs=(VMEM,) * 5,
        scratch_shapes=[
            pltpu.VMEM(green.shape, F32),
            pltpu.VMEM(pattern.shape, jnp.int32),
            pltpu.VMEM(observed.shape, F32),
            pltpu.SemaphoreType.DMA((freqs,)),
            pltpu.SemaphoreType.DMA((3,)),
        ],
        compiler_params=grant,
        cost_estimate=pl.CostEstimate(flops=10**6, bytes_accessed=6 * 2**20, transcendentals=0),
    )(place, green, pattern, observed, table)

    packed = pl.pallas_call(
        pack_kernel,
        out_shape=shape((windows, columns + adjacency.shape[1]), F32),
        in_specs=[HBM, HBM],
        out_specs=VMEM,
        scratch_shapes=[pltpu.VMEM(adjacency.shape, jnp.int32), pltpu.SemaphoreType.DMA((2,))],
        compiler_params=grant,
        cost_estimate=pl.CostEstimate(flops=10**10, bytes_accessed=2**16, transcendentals=0),
    )(slip, adjacency)
    if (n_freq, n_tri, n_sta) == (4, 2, 2):
        pieces = [packed, lax.ppermute(packed, "tri", cores)]
        codes = [(0, 0), (1, 1)]
        fetched = []
        for k in range(1, n_freq):
            pairs = [
                (4 * (z ^ k) + 2 * (t ^ s) + s, 4 * z + 2 * t + s)
                for z in range(n_freq)
                for t in range(n_tri)
                for s in range(n_sta)
            ]
            fetched.append(lax.ppermute(packed, ("freq", "tri", "sta"), pairs))
            codes.append((2 * k, 2 * k + 1))
        fetched, prepared = lax.optimization_barrier((fetched, prepared))
        pieces += fetched + [lax.ppermute(v, "sta", cores) for v in fetched]
        codes += [(2 * k + 1, 2 * k) for k in range(1, n_freq)]
    else:
        copies = jnp.broadcast_to(packed[None], (parts,) + packed.shape)
        pieces = [lax.all_to_all(copies, ("freq", "tri"), 0, 0, tiled=True)]
        codes = []

    pieces_of_green, onehot, turned, apart, own_table = prepared
    flops = 2 * freqs * 128 * 1024 * 256
    whole = shape((parts,) + packed.shape, F32)
    outs = pl.pallas_call(
        lambda *refs: forward_kernel(windows, codes, *refs),
        out_shape=(
            shape(observed.shape, F32),
            shape((n_sta, count, windows, columns), F32),
        )
        + ((whole,) if codes else ()),
        in_specs=[SMEM] + [VMEM] * (len(pieces) + 5),
        out_specs=(VMEM,) * (3 if codes else 2),
        scratch_shapes=[
            pltpu.VMEM((blocks * windows, LANES), F32),
            pltpu.VMEM((classes * stations, freqs * LANES), F32),
            pltpu.VMEM((2 * classes * stations, freqs * LANES), BF16),
            pltpu.VMEM((2, stations * freqs, LANES), F32),
            pltpu.VMEM((CHUNK * windows, LANES), F32),
        ],
        compiler_params=grant,
        cost_estimate=pl.CostEstimate(flops=flops, bytes_accessed=4 * 2**20, transcendentals=0),
    )(place, *pieces, pieces_of_green, onehot, turned, apart, own_table)
    residual, partial = outs[:2]
    shards = outs[2] if codes else pieces[0]

    smooth = pl.pallas_call(
        smooth_kernel,
        out_shape=shape((count, windows, columns), F32),
        in_specs=[SMEM, SMEM, VMEM],
        out_specs=VMEM,
        compiler_params=grant,
        cost_estimate=pl.CostEstimate(flops=10**6, bytes_accessed=4 * 2**20, transcendentals=0),
    )(place, smooth_weight, shards)

    mine = partial[0] + lax.ppermute(partial[1], "sta", cores)
    mine = sum(across(mine), mine) if n_freq <= 8 else lax.psum(mine, "freq")
    mine = mine + smooth
    other = lax.ppermute(mine, "sta", cores)

    own, image, numerator = pl.pallas_call(
        image_kernel,
        out_shape=(shape(slip.shape, F32),) * 3,
        in_specs=[SMEM] + [VMEM] * 5,
        out_specs=(VMEM,) * 3,
        scratch_shapes=[
            pltpu.VMEM((blocks * windows, LANES), F32),
            pltpu.VMEM((classes * stations, freqs * LANES), F32),
        ],
        compiler_params=grant,
        cost_estimate=pl.CostEstimate(flops=flops, bytes_accessed=4 * 2**20, transcendentals=0),
    )(place, mine, other, pieces_of_green, onehot, own_table)

    image = image + lax.ppermute(image, "sta", cores)
    image = sum(across(image), image) if n_freq <= 8 else lax.psum(image, "freq")
    step = numerator / (image + smooth_weight[0] * numerator)
    return jnp.maximum(slip - step * own, 0.0), residual


def solution(mesh):
    n_freq = mesh.shape["freq"]
    placed = (
        P(None, ("grp", "freq", "tri")),
        P("freq", None, None, None),
        P("sta", None),
        P(None, ("grp", "freq"), "sta"),
        P(None, ("freq", "tri")),
        P("grp"),
    )

    def step(slip, green, pattern, observed, adjacency, smooth_weight):
        windows, block = slip.shape[0], green.shape[2]
        table = phase_table(green.shape[0] // n_freq * n_freq, windows, block)

        def body(*args):
            return local(*args, table=jnp.asarray(table))

        return jax.shard_map(
            body,
            mesh=mesh,
            in_specs=placed,
            out_specs=(P(None, ("grp", "freq", "tri")), P(None, ("grp", "freq"), "sta")),
            check_vma=False,
        )(slip, green, pattern, observed, adjacency, smooth_weight)

    return step
```

time: 52.5 us -> 42.2 us (0.80)
  local copies, waits for them, and re-layouts: 5.45 us -> 1.58 us
  waiting for transfers between devices: 14.9 us -> 11.6 us
  Pallas kernels: 11.8 us -> 9.36 us
  other arithmetic: 2.13 us -> 0.74 us
  starting transfers between devices: 16.4 us -> 17.3 us
    all_to_all x1 -> x0, waiting for transfers between devices: 8.84 us -> none  [local(): lax.all_to_all(jnp.broadcast_to(packed[None], (parts,) + packed.shape), (...]
    ppermute x1 -> x8, starting transfers between devices: 0.22 us -> 8.12 us  [the longest x3 5.68 us: local(): fetched.append(lax.ppermute(packed, ('freq', 'tri', 'sta'), pairs))]
    all_to_all x1 -> x0, starting transfers between devices: 7.25 us -> none  [local(): lax.all_to_all(jnp.broadcast_to(packed[None], (parts,) + packed.shape), (...]
    ppermute x1 -> x8, waiting for transfers between devices: 1.01 us -> 4.42 us  [the longest x3 2.21 us: local(): fetched.append(lax.ppermute(packed, ('freq', 'tri', 'sta'), pairs))]
    unnamed x18 -> x14, local copies, waits for them, and re-layouts: 4.71 us -> 1.57 us
    pallas_call x4 -> x5, Pallas kernels: 11.8 us -> 9.36 us  [the longest x1 3.32 us: local(): pl.pallas_call(lambda *refs: forward_kernel(windows, codes, *refs), out_s...]
    ppermute x6, waiting for transfers between devices: 2.56 us -> 4.8 us  [across(): lax.ppermute(value, 'freq', [(i, i ^ k) for i in range(n_freq)])]
    broadcast_in_dim x1 -> x0, local copies, waits for them, and re-layouts: 0.73 us -> none  [local(): jnp.broadcast_to(packed[None], (parts,) + packed.shape)]
  transfers between devices with their start and end apart: 10 -> 16, of which waited for: 7 -> 11; matrix products, arithmetic and copies ran while one was open for 1% -> 0% of each run, Pallas kernels for 5% -> 10%
where the time goes in v2:
time: 42.2 us; the launch traced here: 41.9 us
  starting transfers between devices  17.3 us (41%)
  waiting for transfers between devices  11.6 us (27%)
  Pallas kernels  9.36 us (22%)
  local copies, waits for them, and re-layouts  1.58 us (4%)
  between operations  1.41 us (3%)
  other arithmetic  0.74 us (2%)
    ppermute x6, starting transfers between devices, across(): lax.ppermute(value, 'freq', [(i, i ^ k) for i in range(n_freq)])  8.84 us
    ppermute x3, starting transfers between devices, local(): fetched.append(lax.ppermute(packed, ('freq', 'tri', 'sta'), pairs))  5.68 us
    ppermute x6, waiting for transfers between devices, across(): lax.ppermute(value, 'freq', [(i, i ^ k) for i in range(n_freq)])  4.8 us
    pallas_call x1, Pallas kernels, local(): pl.pallas_call(lambda *refs: forward_kernel(windows, codes, *refs), out_s...  3.32 us
    pallas_call x1, Pallas kernels, local(): pl.pallas_call(smooth_kernel, out_shape=shape((count, windows, columns),...  2.39 us
    ppermute x3, waiting for transfers between devices, local(): fetched.append(lax.ppermute(packed, ('freq', 'tri', 'sta'), pairs))  2.21 us
    pallas_call x1, Pallas kernels, local(): pl.pallas_call(image_kernel, out_shape=(shape(slip.shape, F32),) * 3, in_...  1.9 us
    pallas_call x1, Pallas kernels, local(): pl.pallas_call(prepare_kernel, out_shape=(shape((freqs, 2 * block, classe...  1.72 us
  transfers between devices with their start and end apart: 16, of which 11 were waited for; matrix products, arithmetic and copies ran while one was open for 0% of the time, Pallas kernels for 10%

profile of v2, /device:TPU:0, one launch (start us, length us, event | category | flops | bytes accessed | tf_op | source)
XLA Modules:
  0.0 41.9 jit_solution(2357207142540701891)
XLA Ops:
  0.7 0.9 %copy-done.3 = f32[8,512]{1,0:T(8,128)S(1)} copy-done((f32[8,512]{1,0:T(8,128)S(1)}, f32[8,512]{1,0:T(8,128)}, u32[]{:S(2)}) %copy-start.3) | copy-done | bytes 16408
  1.5 0.7 %copy-done.6 = s32[3,256]{1,0:T(4,128)S(1)} copy-done((s32[3,256]{1,0:T(4,128)S(1)}, s32[3,256]{1,0:T(4,128)}, u32[]{:S(2)}) %copy-start.6) | copy-done | bytes 3096
  2.3 3.1 %collective-permute-start.1 = (f32[8,768]{1,0:T(8,128)S(1)}, f32[8,768]{1,0:T(8,128)S(1)}, u32[]{:S(2)}, u32[]{:S(2)}) collective-permute-start(f32[8,768]{1,0:T(8,128)S(1)} %shard_map.86.refs_1_), channel_id=1, source_target_pairs={{4,0},{7,1},{6,2},{5,3},{0,4},{3,5},{2,6},{1,7},{12,8},{15,9},{14,... | collective-permute-start | bytes 73736 | tf_op jit(solution)/shard_map/ppermute | solution.py:409
  5.3 2.6 %collective-permute-start.2 = (f32[8,768]{1,0:T(8,128)S(1)}, f32[8,768]{1,0:T(8,128)S(1)}, u32[]{:S(2)}, u32[]{:S(2)}) collective-permute-start(f32[8,768]{1,0:T(8,128)S(1)} %shard_map.86.refs_1_), channel_id=1, source_target_pairs={{8,0},{11,1},{10,2},{9,3},{12,4},{15,5},{14,6},{13,7},{0,8},{3,9},... | collective-permute-start | bytes 73736 | tf_op jit(solution)/shard_map/ppermute | solution.py:409
  7.9 1.7 %collective-permute-start = (f32[8,768]{1,0:T(8,128)S(1)}, f32[8,768]{1,0:T(8,128)S(1)}, u32[]{:S(2)}, u32[]{:S(2)}) collective-permute-start(f32[8,768]{1,0:T(8,128)S(1)} %shard_map.86.refs_1_), channel_id=1, source_target_pairs={{0,2},{2,0},{1,3},{3,1},{4,6},{6,4},{5,7},{7,5},{8,10},{10,8},{9,1... | collective-permute-start | bytes 73736 | tf_op jit(solution)/shard_map/ppermute | solution.py:399
  9.7 1.7 %shard_map.87 = (bf16[8,128,1024]{2,1,0:T(8,128)(2,1)S(1)}, bf16[1,256,128]{2,1,0:T(8,128)(2,1)S(1)}, bf16[1,64,512]{2,1,0:T(8,128)(2,1)S(1)}, f32[2,256,128]{2,1,0:T(8,128)S(1)}, f32[8,8,128]{2,1,0:T(8,128)S(1)}) custom-call(s32[3]{0:T(128)S(1)} %pad_add_fusion.place.refs_0_, f32[8,8,64,128]{3,2,1,0:T(8,128)S(1)} %copy-done, s32[1,32,64]{2,1,0:T(8,128)S(1)} %bitcast.10, ...), custom_call_target="tpu_custom_call" | custom-call | flops 1000000 | bytes 6291456 | tf_op jit(solution)/shard_map/pallas_call | solution.py:367
  11.5 2.2 %collective-permute-done.3.refs_5_ = f32[8,768]{1,0:T(8,128)S(1)} collective-permute-done((f32[8,768]{1,0:T(8,128)S(1)}, f32[8,768]{1,0:T(8,128)S(1)}, u32[]{:S(2)}, u32[]{:S(2)}) %collective-permute-start.3) | collective-permute-done | bytes 24608 | tf_op jit(solution)/shard_map/ppermute | solution.py:409
  14.2 0.7 %collective-permute-done.4.refs_6_ = f32[8,768]{1,0:T(8,128)S(1)} collective-permute-done((f32[8,768]{1,0:T(8,128)S(1)}, f32[8,768]{1,0:T(8,128)S(1)}, u32[]{:S(2)}, u32[]{:S(2)}) %collective-permute-start.4) | collective-permute-done | bytes 24608 | tf_op jit(solution)/shard_map/ppermute | solution.py:412
  15.4 3.3 %shard_map.88 = (f32[2,8,2048]{2,1,0:T(8,128)}, f32[2,4,8,512]{3,2,1,0:T(8,128)S(1)}, f32[8,8,768]{2,1,0:T(8,128)S(1)}) custom-call(s32[3]{0:T(128)S(1)} %pad_add_fusion.place.refs_0_, f32[8,768]{1,0:T(8,128)S(1)} %shard_map.86.refs_1_, f32[8,768]{1,0:T(8,128)S(1)} %collective-permute-done.refs_2_, f32[8,768]{1,0:T(8,128)S(1)} %collective-permute-done.1.refs_3_, ...), custom_call_target="tpu_custom_call" | custom-call | flops 536870912 | bytes 4194304 | tf_op jit(solution)/shard_map/pallas_call | solution.py:422
  19.0 1.1 %collective-permute-done.7 = f32[4,8,512]{2,1,0:T(8,128)S(1)} collective-permute-done((f32[4,8,512]{2,1,0:T(8,128)S(1)}, f32[4,8,512]{2,1,0:T(8,128)S(1)}, u32[]{:S(2)}, u32[]{:S(2)}) %collective-permute-start.7) | collective-permute-done | bytes 65568 | tf_op jit(solution)/shard_map/ppermute | solution.py:453
  20.1 1.5 %collective-permute-start.10 = (f32[4,8,512]{2,1,0:T(8,128)S(1)}, f32[4,8,512]{2,1,0:T(8,128)S(1)}, u32[]{:S(2)}, u32[]{:S(2)}) collective-permute-start(f32[4,8,512]{2,1,0:T(8,128)S(1)} %bitcast_add_fusion), channel_id=1, source_target_pairs={{0,12},{4,8},{8,4},{12,0},{1,13},{5,9},{9,5},{13,1},{2,14},{6,10},... | collective-permute-start | bytes 196616 | tf_op jit(solution)/shard_map/ppermute | solution.py:363
  21.6 2.9 %collective-permute-start.9 = (f32[4,8,512]{2,1,0:T(8,128)S(1)}, f32[4,8,512]{2,1,0:T(8,128)S(1)}, u32[]{:S(2)}, u32[]{:S(2)}) collective-permute-start(f32[4,8,512]{2,1,0:T(8,128)S(1)} %bitcast_add_fusion), channel_id=1, source_target_pairs={{0,8},{4,12},{8,0},{12,4},{1,9},{5,13},{9,1},{13,5},{2,10},{6,14},... | collective-permute-start | bytes 196616 | tf_op jit(solution)/shard_map/ppermute | solution.py:363
  25.2 2.4 %shard_map.89 = f32[4,8,512]{2,1,0:T(8,128)S(1)} custom-call(s32[3]{0:T(128)S(1)} %pad_add_fusion.place.refs_0_, f32[1]{0:T(128)} %copy.9.weight, f32[8,8,768]{2,1,0:T(8,128)S(1)} %get-tuple-element.35.shards), custom_call_target="tpu_custom_call" | custom-call | flops 1000000 | bytes 4194304 | tf_op jit(solution)/shard_map/pallas_call | solution.py:444
  27.6 0.7 %collective-permute-done.8 = f32[4,8,512]{2,1,0:T(8,128)S(1)} collective-permute-done((f32[4,8,512]{2,1,0:T(8,128)S(1)}, f32[4,8,512]{2,1,0:T(8,128)S(1)}, u32[]{:S(2)}, u32[]{:S(2)}) %collective-permute-start.8) | collective-permute-done | bytes 65568 | tf_op jit(solution)/shard_map/ppermute | solution.py:363
  28.3 0.7 %collective-permute-done.9 = f32[4,8,512]{2,1,0:T(8,128)S(1)} collective-permute-done((f32[4,8,512]{2,1,0:T(8,128)S(1)}, f32[4,8,512]{2,1,0:T(8,128)S(1)}, u32[]{:S(2)}, u32[]{:S(2)}) %collective-permute-start.9) | collective-permute-done | bytes 65568 | tf_op jit(solution)/shard_map/ppermute | solution.py:363
  29.1 1.2 %collective-permute-done.11.other = f32[4,8,512]{2,1,0:T(8,128)S(1)} collective-permute-done((f32[4,8,512]{2,1,0:T(8,128)S(1)}, f32[4,8,512]{2,1,0:T(8,128)S(1)}, u32[]{:S(2)}, u32[]{:S(2)}) %collective-permute-start.11) | collective-permute-done | bytes 65568 | tf_op jit(solution)/shard_map/ppermute | solution.py:456
  30.3 1.9 %shard_map.90 = (f32[8,512]{1,0:T(8,128)S(1)}, f32[8,512]{1,0:T(8,128)S(1)}, f32[8,512]{1,0:T(8,128)S(1)}) custom-call(s32[3]{0:T(128)S(1)} %pad_add_fusion.place.refs_0_, f32[4,8,512]{2,1,0:T(8,128)S(1)} %add_add_fusion.mine, f32[4,8,512]{2,1,0:T(8,128)S(1)} %collective-permute-done.11.other, bf16[8,128,1024]{2,1,0:T(8,128)(2,1)S(1)} %get-tuple-element.29.refs_9_.green, ...), custom_call_target="tpu_custom_call" | custom-call | flops 536870912 | bytes 4194304 | tf_op jit(solution)/shard_map/pallas_call | solution.py:458
  32.4 1.0 %collective-permute-done.12 = f32[8,512]{1,0:T(8,128)S(1)} collective-permute-done((f32[8,512]{1,0:T(8,128)S(1)}, f32[8,512]{1,0:T(8,128)S(1)}, u32[]{:S(2)}, u32[]{:S(2)}) %collective-permute-start.12) | collective-permute-done | bytes 16416 | tf_op jit(solution)/shard_map/ppermute | solution.py:471
  33.5 0.5 %collective-permute-start.13 = (f32[8,512]{1,0:T(8,128)S(1)}, f32[8,512]{1,0:T(8,128)S(1)}, u32[]{:S(2)}, u32[]{:S(2)}) collective-permute-start(f32[8,512]{1,0:T(8,128)S(1)} %add.39), channel_id=1, source_target_pairs={{0,4},{4,0},{8,12},{12,8},{1,5},{5,1},{9,13},{13,9},{2,6},{6,2},{1... | collective-permute-start | bytes 49160 | tf_op jit(solution)/shard_map/ppermute | solution.py:363
  34.0 1.7 %collective-permute-start.14 = (f32[8,512]{1,0:T(8,128)S(1)}, f32[8,512]{1,0:T(8,128)S(1)}, u32[]{:S(2)}, u32[]{:S(2)}) collective-permute-start(f32[8,512]{1,0:T(8,128)S(1)} %add.39), channel_id=1, source_target_pairs={{0,8},{4,12},{8,0},{12,4},{1,9},{5,13},{9,1},{13,5},{2,10},{6,14},... | collective-permute-start | bytes 49160 | tf_op jit(solution)/shard_map/ppermute | solution.py:363
  35.7 2.1 %collective-permute-start.15 = (f32[8,512]{1,0:T(8,128)S(1)}, f32[8,512]{1,0:T(8,128)S(1)}, u32[]{:S(2)}, u32[]{:S(2)}) collective-permute-start(f32[8,512]{1,0:T(8,128)S(1)} %add.39), channel_id=1, source_target_pairs={{0,12},{4,8},{8,4},{12,0},{1,13},{5,9},{9,5},{13,1},{2,14},{6,10},... | collective-permute-start | bytes 49160 | tf_op jit(solution)/shard_map/ppermute | solution.py:363
  37.9 0.8 %collective-permute-done.14 = f32[8,512]{1,0:T(8,128)S(1)} collective-permute-done((f32[8,512]{1,0:T(8,128)S(1)}, f32[8,512]{1,0:T(8,128)S(1)}, u32[]{:S(2)}, u32[]{:S(2)}) %collective-permute-start.14) | collective-permute-done | bytes 16416 | tf_op jit(solution)/shard_map/ppermute | solution.py:363
  38.7 2.6 %collective-permute-done.15 = f32[8,512]{1,0:T(8,128)S(1)} collective-permute-done((f32[8,512]{1,0:T(8,128)S(1)}, f32[8,512]{1,0:T(8,128)S(1)}, u32[]{:S(2)}, u32[]{:S(2)}) %collective-permute-start.15) | collective-permute-done | bytes 16416 | tf_op jit(solution)/shard_map/ppermute | solution.py:363
  41.3 0.6 %subtract_maximum_fusion = f32[8,512]{1,0:T(8,128)} fusion(f32[8,512]{1,0:T(8,128)S(1)} %copy-done.4, f32[8,512]{1,0:T(8,128)S(1)} %get-tuple-element.38, f32[8,512]{1,0:T(8,128)S(1)} %get-tuple-element.36, f32[8,512]{1,0:T(8,128)S(1)} %collective-permute-done.15, f32[8,512]{1,0:T(8,128)S(1)} %collective-permute-done.14, f32[8,512]{1,0:T(8,128)S(1)} %add.39, ...), kind=kLoop, calls=%fused_computation.3 | loop fusion | flops 36864 | bytes 131076 | tf_op jit(solution)/shard_map/max | solution.py:474
  (33 shorter events, 1.7 us)
Async XLA Ops:
  0.6 9.1 %copy-start.2 = (f32[32,8,128]{2,1,0:T(8,128)S(1)}, f32[32,8,128]{2,1,0:T(8,128)}, u32[]{:S(2)}) copy-start(f32[32,8,128]{2,1,0:T(8,128)} %constant.17.clone.table_hbm) | copy-start | bytes 393220
  0.6 9.1 %copy-start.1 = (f32[2,8,2048]{2,1,0:T(8,128)S(1)}, f32[2,8,2048]{2,1,0:T(8,128)}, u32[]{:S(2)}) copy-start(f32[2,8,2048]{2,1,0:T(8,128)} %observed_hbm.1) | copy-start | bytes 393220
  0.7 9.1 %copy-start = (f32[8,8,64,128]{3,2,1,0:T(8,128)S(1)}, f32[8,8,64,128]{3,2,1,0:T(8,128)}, u32[]{:S(2)}) copy-start(f32[8,8,64,128]{3,2,1,0:T(8,128)} %green_hbm.1) | copy-start | bytes 6291460
  0.7 0.9 %copy-start.3 = (f32[8,512]{1,0:T(8,128)S(1)}, f32[8,512]{1,0:T(8,128)}, u32[]{:S(2)}) copy-start(f32[8,512]{1,0:T(8,128)} %slip.1) | copy-start | bytes 49156
  1.5 0.7 %copy-start.6 = (s32[3,256]{1,0:T(4,128)S(1)}, s32[3,256]{1,0:T(4,128)}, u32[]{:S(2)}) copy-start(s32[3,256]{1,0:T(4,128)} %adjacency.1) | copy-start | bytes 9220
  2.2 7.5 %copy-start.5 = (s32[32,64]{1,0:T(8,128)S(1)}, s32[32,64]{1,0:T(8,128)}, u32[]{:S(2)}) copy-start(s32[32,64]{1,0:T(8,128)} %param.9) | copy-start | bytes 24580
  2.3 9.2 %collective-permute-start.1 = (f32[8,768]{1,0:T(8,128)S(1)}, f32[8,768]{1,0:T(8,128)S(1)}, u32[]{:S(2)}, u32[]{:S(2)}) collective-permute-start(f32[8,768]{1,0:T(8,128)S(1)} %shard_map.86.refs_1_), channel_id=1, source_target_pairs={{4,0},{7,1},{6,2},{5,3},{0,4},{3,5},{2,6},{1,7},{12,8},{15,9},{14,... | collective-permute-start | bytes 73736 | tf_op jit(solution)/shard_map/ppermute | solution.py:409
  5.3 6.1 %collective-permute-start.2 = (f32[8,768]{1,0:T(8,128)S(1)}, f32[8,768]{1,0:T(8,128)S(1)}, u32[]{:S(2)}, u32[]{:S(2)}) collective-permute-start(f32[8,768]{1,0:T(8,128)S(1)} %shard_map.86.refs_1_), channel_id=1, source_target_pairs={{8,0},{11,1},{10,2},{9,3},{12,4},{15,5},{14,6},{13,7},{0,8},{3,9},... | collective-permute-start | bytes 73736 | tf_op jit(solution)/shard_map/ppermute | solution.py:409
  7.9 5.8 %collective-permute-start.3 = (f32[8,768]{1,0:T(8,128)S(1)}, f32[8,768]{1,0:T(8,128)S(1)}, u32[]{:S(2)}, u32[]{:S(2)}) collective-permute-start(f32[8,768]{1,0:T(8,128)S(1)} %shard_map.86.refs_1_), channel_id=1, source_target_pairs={{12,0},{15,1},{14,2},{13,3},{8,4},{11,5},{10,6},{9,7},{4,8},{7,9},... | collective-permute-start | bytes 73736 | tf_op jit(solution)/shard_map/ppermute | solution.py:409
  7.9 6.3 %collective-permute-start = (f32[8,768]{1,0:T(8,128)S(1)}, f32[8,768]{1,0:T(8,128)S(1)}, u32[]{:S(2)}, u32[]{:S(2)}) collective-permute-start(f32[8,768]{1,0:T(8,128)S(1)} %shard_map.86.refs_1_), channel_id=1, source_target_pairs={{0,2},{2,0},{1,3},{3,1},{4,6},{6,4},{5,7},{7,5},{8,10},{10,8},{9,1... | collective-permute-start | bytes 73736 | tf_op jit(solution)/shard_map/ppermute | solution.py:399
  13.7 1.2 %collective-permute-start.4 = (f32[8,768]{1,0:T(8,128)S(1)}, f32[8,768]{1,0:T(8,128)S(1)}, u32[]{:S(2)}, u32[]{:S(2)}) collective-permute-start(f32[8,768]{1,0:T(8,128)S(1)} %collective-permute-done.1.refs_3_), channel_id=1, source_target_pairs={{0,1},{1,0},{2,3},{3,2},{4,5},{5,4},{6,7},{7,6},{8,9},{9,8},{10,11... | collective-permute-start | bytes 73736 | tf_op jit(solution)/shard_map/ppermute | solution.py:412
  13.7 1.4 %collective-permute-start.5 = (f32[8,768]{1,0:T(8,128)S(1)}, f32[8,768]{1,0:T(8,128)S(1)}, u32[]{:S(2)}, u32[]{:S(2)}) collective-permute-start(f32[8,768]{1,0:T(8,128)S(1)} %collective-permute-done.2.refs_4_), channel_id=1, source_target_pairs={{0,1},{1,0},{2,3},{3,2},{4,5},{5,4},{6,7},{7,6},{8,9},{9,8},{10,11... | collective-permute-start | bytes 73736 | tf_op jit(solution)/shard_map/ppermute | solution.py:412
  14.2 1.2 %collective-permute-start.6 = (f32[8,768]{1,0:T(8,128)S(1)}, f32[8,768]{1,0:T(8,128)S(1)}, u32[]{:S(2)}, u32[]{:S(2)}) collective-permute-start(f32[8,768]{1,0:T(8,128)S(1)} %collective-permute-done.3.refs_5_), channel_id=1, source_target_pairs={{0,1},{1,0},{2,3},{3,2},{4,5},{5,4},{6,7},{7,6},{8,9},{9,8},{10,11... | collective-permute-start | bytes 73736 | tf_op jit(solution)/shard_map/ppermute | solution.py:412
  18.7 22.6 %copy-start.4 = (f32[8,512]{1,0:T(8,128)S(1)}, f32[8,512]{1,0:T(8,128)}, u32[]{:S(2)}) copy-start(f32[8,512]{1,0:T(8,128)} %slip.1) | copy-start | bytes 49156
  18.7 1.3 %collective-permute-start.7 = (f32[4,8,512]{2,1,0:T(8,128)S(1)}, f32[4,8,512]{2,1,0:T(8,128)S(1)}, u32[]{:S(2)}, u32[]{:S(2)}) collective-permute-start(f32[4,8,512]{2,1,0:T(8,128)S(1)} %slice_bitcast_fusion), channel_id=1, source_target_pairs={{0,1},{1,0},{2,3},{3,2},{4,5},{5,4},{6,7},{7,6},{8,9},{9,8},{10,11... | collective-permute-start | bytes 196616 | tf_op jit(solution)/shard_map/ppermute | solution.py:453
  20.1 7.5 %collective-permute-start.10 = (f32[4,8,512]{2,1,0:T(8,128)S(1)}, f32[4,8,512]{2,1,0:T(8,128)S(1)}, u32[]{:S(2)}, u32[]{:S(2)}) collective-permute-start(f32[4,8,512]{2,1,0:T(8,128)S(1)} %bitcast_add_fusion), channel_id=1, source_target_pairs={{0,12},{4,8},{8,4},{12,0},{1,13},{5,9},{9,5},{13,1},{2,14},{6,10},... | collective-permute-start | bytes 196616 | tf_op jit(solution)/shard_map/ppermute | solution.py:363
  21.6 6.6 %collective-permute-start.8 = (f32[4,8,512]{2,1,0:T(8,128)S(1)}, f32[4,8,512]{2,1,0:T(8,128)S(1)}, u32[]{:S(2)}, u32[]{:S(2)}) collective-permute-start(f32[4,8,512]{2,1,0:T(8,128)S(1)} %bitcast_add_fusion), channel_id=1, source_target_pairs={{0,4},{4,0},{8,12},{12,8},{1,5},{5,1},{9,13},{13,9},{2,6},{6,2},{1... | collective-permute-start | bytes 196616 | tf_op jit(solution)/shard_map/ppermute | solution.py:363
  21.6 7.3 %collective-permute-start.9 = (f32[4,8,512]{2,1,0:T(8,128)S(1)}, f32[4,8,512]{2,1,0:T(8,128)S(1)}, u32[]{:S(2)}, u32[]{:S(2)}) collective-permute-start(f32[4,8,512]{2,1,0:T(8,128)S(1)} %bitcast_add_fusion), channel_id=1, source_target_pairs={{0,8},{4,12},{8,0},{12,4},{1,9},{5,13},{9,1},{13,5},{2,10},{6,14},... | collective-permute-start | bytes 196616 | tf_op jit(solution)/shard_map/ppermute | solution.py:363
  29.0 1.3 %collective-permute-start.11 = (f32[4,8,512]{2,1,0:T(8,128)S(1)}, f32[4,8,512]{2,1,0:T(8,128)S(1)}, u32[]{:S(2)}, u32[]{:S(2)}) collective-permute-start(f32[4,8,512]{2,1,0:T(8,128)S(1)} %add_add_fusion.mine), channel_id=1, source_target_pairs={{0,1},{1,0},{2,3},{3,2},{4,5},{5,4},{6,7},{7,6},{8,9},{9,8},{10,11... | collective-permute-start | bytes 196616 | tf_op jit(solution)/shard_map/ppermute | solution.py:456
  32.2 1.2 %collective-permute-start.12 = (f32[8,512]{1,0:T(8,128)S(1)}, f32[8,512]{1,0:T(8,128)S(1)}, u32[]{:S(2)}, u32[]{:S(2)}) collective-permute-start(f32[8,512]{1,0:T(8,128)S(1)} %get-tuple-element.37), channel_id=1, source_target_pairs={{0,1},{1,0},{2,3},{3,2},{4,5},{5,4},{6,7},{7,6},{8,9},{9,8},{10,11... | collective-permute-start | bytes 49160 | tf_op jit(solution)/shard_map/ppermute | solution.py:471
  33.5 4.4 %collective-permute-start.13 = (f32[8,512]{1,0:T(8,128)S(1)}, f32[8,512]{1,0:T(8,128)S(1)}, u32[]{:S(2)}, u32[]{:S(2)}) collective-permute-start(f32[8,512]{1,0:T(8,128)S(1)} %add.39), channel_id=1, source_target_pairs={{0,4},{4,0},{8,12},{12,8},{1,5},{5,1},{9,13},{13,9},{2,6},{6,2},{1... | collective-permute-start | bytes 49160 | tf_op jit(solution)/shard_map/ppermute | solution.py:363
  34.0 4.7 %collective-permute-start.14 = (f32[8,512]{1,0:T(8,128)S(1)}, f32[8,512]{1,0:T(8,128)S(1)}, u32[]{:S(2)}, u32[]{:S(2)}) collective-permute-start(f32[8,512]{1,0:T(8,128)S(1)} %add.39), channel_id=1, source_target_pairs={{0,8},{4,12},{8,0},{12,4},{1,9},{5,13},{9,1},{13,5},{2,10},{6,14},... | collective-permute-start | bytes 49160 | tf_op jit(solution)/shard_map/ppermute | solution.py:363
  35.7 5.5 %collective-permute-start.15 = (f32[8,512]{1,0:T(8,128)S(1)}, f32[8,512]{1,0:T(8,128)S(1)}, u32[]{:S(2)}, u32[]{:S(2)}) collective-permute-start(f32[8,512]{1,0:T(8,128)S(1)} %add.39), channel_id=1, source_target_pairs={{0,12},{4,8},{8,4},{12,0},{1,13},{5,9},{9,5},{13,1},{2,14},{6,10},... | collective-permute-start | bytes 49160 | tf_op jit(solution)/shard_map/ppermute | solution.py:363

commit v3 on v2

--- a/solution.py
+++ b/solution.py
@@ -52,8 +52,7 @@
         lax.fori_loop(0, parts, one, 0)
 
 
-def onehot_of(pattern, classes):
-    doubled = jnp.concatenate([pattern, pattern], axis=1)
+def onehot_of(doubled, classes):
     return jnp.concatenate([(doubled == k).astype(F32) for k in range(classes)], axis=0)
 
 
@@ -64,53 +63,27 @@
         lax.fori_loop(0, count, lambda n, carry: (step(n), carry)[1], 0)
 
 
-def pack_kernel(slip, adjacency, out, held, sems):
-    windows, columns = slip.shape
-    neighbours, triangles = adjacency.shape
-    copies = [
-        pltpu.make_async_copy(adjacency, held, sems.at[0]),
-        pltpu.make_async_copy(slip, out.at[:, pl.ds(0, columns)], sems.at[1]),
-    ]
-    for copy in copies:
-        copy.start()
-    copies[0].wait()
-    out[:neighbours, columns:] = held[...].astype(F32)
-    out[neighbours:, columns:] = jnp.zeros((windows - neighbours, triangles), F32)
-    copies[1].wait()
+def positions():
+    freq = lax.axis_index("freq")
+    return freq, freq * lax.axis_size("tri") + lax.axis_index("tri"), lax.axis_index("sta")
+
+
+def doubled_kernel(pattern, out):
+    out[...] = jnp.concatenate([pattern[...], pattern[...]], axis=2)
 
 
 def prepare_kernel(
-    place,
-    green_hbm,
-    pattern_hbm,
-    observed_hbm,
-    table_hbm,
-    green_out,
-    onehot_out,
-    turned_out,
-    apart,
-    table_out,
-    green_ref,
-    pattern_ref,
-    observed,
-    green_sems,
-    sems,
+    green_ref, pattern_ref, observed, table, green_out, onehot_out, turned_out, apart, table_out
 ):
     freqs, classes, block, _ = green_ref.shape
     chunks, stations, _ = pattern_ref.shape
-    first = place[0] * freqs
-    copies = [
-        pltpu.make_async_copy(pattern_hbm, pattern_ref, sems.at[0]),
-        pltpu.make_async_copy(observed_hbm, observed, sems.at[1]),
-        pltpu.make_async_copy(table_hbm.at[pl.ds(first, freqs)], table_out, sems.at[2]),
-    ]
-    greens = [
-        pltpu.make_async_copy(green_hbm.at[f], green_ref.at[f], green_sems.at[f])
-        for f in range(freqs)
-    ]
-    for copy in copies + greens:
-        copy.start()
-    copies[0].wait()
+    first = positions()[0] * freqs
+    for f in range(freqs):
+        for k in range(classes):
+            high, low = split(green_ref[f, k])
+            green_out[f, :block, k * LANES : (k + 1) * LANES] = high
+            green_out[f, block:, k * LANES : (k + 1) * LANES] = low
+        table_out[f] = table[first + f]
 
     def step(n):
         onehot = onehot_of(pattern_ref[n], classes)
@@ -119,19 +92,11 @@
         turned_out[n] = jnp.concatenate([turned, turned], axis=1)
 
     over_chunks(chunks, step)
-    copies[1].wait()
     for r in range(2):
         for j in range(stations // 2):
             piece = observed[r, :, j * LANES : (j + 1) * LANES]
             apart[r, 2 * j * freqs : (2 * j + 1) * freqs, :] = piece
             apart[r, (2 * j + 1) * freqs : (2 * j + 2) * freqs, :] = pltpu.roll(piece, block, 1)
-    copies[2].wait()
-    for f in range(freqs):
-        greens[f].wait()
-        for k in range(classes):
-            high, low = split(green_ref[f, k])
-            green_out[f, :block, k * LANES : (k + 1) * LANES] = high
-            green_out[f, block:, k * LANES : (k + 1) * LANES] = low
 
 
 def pattern_sums(spread, table, onehot_ref, summed):
@@ -182,7 +147,8 @@
     return total + pltpu.roll(total, block, 1)
 
 
-def forward_kernel(windows, codes, place, *refs):
+def forward_kernel(windows, codes, *refs):
+    _, me, half = positions()
     count = max(len(codes), 1)
     pieces, refs = refs[:count], refs[count:]
     green, onehot_ref, turned_ref, apart, table = refs[:5]
@@ -190,8 +156,8 @@
     if codes:
         shards, refs = refs[7], refs[8:]
         for (even, odd), piece in zip(codes, pieces):
-            code = jnp.where(place[2] == 0, even, odd)
-            shards[lax.bitwise_xor(place[1], code)] = piece[...]
+            code = jnp.where(half == 0, even, odd).astype(jnp.int32)
+            shards[lax.bitwise_xor(me, code)] = piece[...]
     else:
         shards, refs = pieces[0], refs[7:]
     spread, summed, adjoint_rows, missed, fields = refs
@@ -200,10 +166,9 @@
     stations = apart.shape[1] // freqs
     classes = summed.shape[0] // stations
     parts = shards.shape[0]
-    half = place[2]
     width = partial_out.shape[3]
     low8 = low_lanes((freqs, LANES), block)
-    spread_columns(lambda p: shards[p, :, :width], parts, spread)
+    spread_columns(lambda p: shards[p], parts, spread)
     pattern_sums(spread, table, onehot_ref, summed)
     predicted = [predict_one(summed, green[f], f, stations, block) for f in range(freqs)]
     lefts = []
@@ -260,26 +225,30 @@
     over_chunks(turned_ref.shape[0], step)
 
 
-def smooth_kernel(place, weight, shards, out):
+def smooth_kernel(shards, *refs):
+    adjacency, out = refs[:-1], refs[-1]
     count, windows, width = out.shape
     parts = shards.shape[0]
+    tris = len(adjacency)
     pieces = width // LANES
     lane = lax.broadcasted_iota(jnp.int32, (windows, LANES), 1)
 
     def pick(source, index):
         return jnp.take_along_axis(source, index, axis=1, mode="promise_in_bounds")
 
-    def one(slot, carry):
-        p = place[2] * count + slot
+    out[...] = jnp.zeros(out.shape, F32)
+    _, me, half = positions()
+    for k in range(tris):
+        p = me - lax.rem(me, tris) + lax.bitwise_xor(lax.rem(me, tris), jnp.int32(k))
+        factor = jnp.where(p // count == half, 1.0, 0.0)
         around = [jnp.maximum(p - 1, 0), p, jnp.minimum(p + 1, parts - 1)]
         source = [shards[a, :, j * LANES : (j + 1) * LANES] for a in around for j in range(pieces)]
         for q in range(pieces):
             total = None
             for j in range(3):
-                start = width + (q // 2) * LANES
-                row = shards[p, j : j + 1, start : start + LANES]
+                row = adjacency[k][j : j + 1, (q // 2) * LANES : (q // 2 + 1) * LANES]
                 row = jnp.broadcast_to(row, (windows, LANES))
-                target = pick(row, (q % 2) * (LANES // 2) + lane // 2).astype(jnp.int32)
+                target = pick(row, (q % 2) * (LANES // 2) + lane // 2)
                 column = 2 * target + lane % 2 - (p - 1) * width
                 inside = jnp.bitwise_and(column, LANES - 1)
                 which = jnp.right_shift(column, 7)
@@ -288,21 +257,18 @@
                     value = jnp.where(which == v, pick(source[v], inside), value)
                 total = value if total is None else total + value
             own = source[pieces + q]
-            out[slot, :, q * LANES : (q + 1) * LANES] = weight[0] * (own - total / 3.0)
-        return carry
-
-    lax.fori_loop(0, count, one, 0)
+            out[lax.rem(p, count), :, q * LANES : (q + 1) * LANES] = factor * (own - total / 3.0)
 
 
 def image_kernel(
-    place, mine, other, green, onehot_ref, table, own_out, image_out, norm_out, spread, summed
+    mine, other, green, onehot_ref, table, weight, own_out, image_out, norm_out, spread, summed
 ):
     freqs, rows, _ = green.shape
     block = rows // 2
     classes = green.shape[2] // LANES
     stations = summed.shape[0] // classes
     count, windows, width = mine.shape
-    half = place[2]
+    _, me, half = positions()
 
     def read(p):
         slot = p % count if isinstance(p, int) else lax.rem(p, count)
@@ -310,7 +276,6 @@
 
     spread_columns(read, 2 * count, spread)
     pattern_sums(spread, table, onehot_ref, summed)
-    me = place[1]
     slot = lax.rem(me, count)
     own_out[...] = jnp.where(me // count == half, mine[slot], other[slot])
 
@@ -335,12 +300,21 @@
             image = image + predicted[8 * j : 8 * j + 8]
     image = jnp.where(low_lanes(image.shape, block), image, 0.0)
     image_out[...] = jnp.broadcast_to(jnp.sum(image), image_out.shape)
-    norm_out[...] = jnp.broadcast_to(jnp.sum(numerator), norm_out.shape)
-
-
-SMEM = pl.BlockSpec(memory_space=pltpu.SMEM)
+    norm_out[0] = jnp.broadcast_to(jnp.sum(numerator), norm_out.shape[1:])
+    norm_out[1] = weight[...] * norm_out[0]
+
+
+def update_kernel(images, norm, slip, own, out):
+    image = images[0]
+    for n in range(1, images.shape[0]):
+        image = image + images[n]
+    step = norm[0] / (image + norm[1])
+    for j in range(slip.shape[1] // LANES):
+        at = slice(j * LANES, (j + 1) * LANES)
+        out[:, at] = jnp.maximum(slip[:, at] - step * own[:, at], 0.0)
+
+
 VMEM = pl.BlockSpec(memory_space=pltpu.VMEM)
-HBM = pl.BlockSpec(memory_space=pltpu.HBM)
 
 
 def local(slip, green, pattern, observed, adjacency, smooth_weight, *, table):
@@ -350,8 +324,6 @@
     freqs, classes, block, _ = green.shape
     windows, columns = slip.shape
     stations, blocks = pattern.shape
-    index = [lax.axis_index(a) for a in (("freq",), ("freq", "tri"), ("sta",))]
-    place = jnp.stack(index).astype(jnp.int32)
     pattern = pattern.reshape(stations, blocks // CHUNK, CHUNK).transpose(1, 0, 2)
     chunks = blocks // CHUNK
     grant = pltpu.CompilerParams(vmem_limit_bytes=(16 if chunks == 1 else 48) * 2**20)
@@ -364,6 +336,14 @@
             for k in range(1, n_freq)
         ]
 
+    doubled = pl.pallas_call(
+        doubled_kernel,
+        out_shape=shape((chunks, stations, 2 * CHUNK), jnp.int32),
+        in_specs=[VMEM],
+        out_specs=VMEM,
+        compiler_params=grant,
+        cost_estimate=pl.CostEstimate(flops=10**10, bytes_accessed=2**10, transcendentals=0),
+    )(pattern)
     prepared = pl.pallas_call(
         prepare_kernel,
         out_shape=(
@@ -373,30 +353,16 @@
             shape((2, stations * freqs, LANES), F32),
             shape((freqs, windows, LANES), F32),
         ),
-        in_specs=[SMEM] + [HBM] * 4,
+        in_specs=[VMEM] * 4,
         out_specs=(VMEM,) * 5,
-        scratch_shapes=[
-            pltpu.VMEM(green.shape, F32),
-            pltpu.VMEM(pattern.shape, jnp.int32),
-            pltpu.VMEM(observed.shape, F32),
-            pltpu.SemaphoreType.DMA((freqs,)),
-            pltpu.SemaphoreType.DMA((3,)),
-        ],
         compiler_params=grant,
         cost_estimate=pl.CostEstimate(flops=10**6, bytes_accessed=6 * 2**20, transcendentals=0),
-    )(place, green, pattern, observed, table)
-
-    packed = pl.pallas_call(
-        pack_kernel,
-        out_shape=shape((windows, columns + adjacency.shape[1]), F32),
-        in_specs=[HBM, HBM],
-        out_specs=VMEM,
-        scratch_shapes=[pltpu.VMEM(adjacency.shape, jnp.int32), pltpu.SemaphoreType.DMA((2,))],
-        compiler_params=grant,
-        cost_estimate=pl.CostEstimate(flops=10**10, bytes_accessed=2**16, transcendentals=0),
-    )(slip, adjacency)
+    )(green, doubled, observed, table)
+    neighbours = [adjacency] + [
+        lax.ppermute(adjacency, "tri", [(i, i ^ k) for i in range(n_tri)]) for k in range(1, n_tri)
+    ]
     if (n_freq, n_tri, n_sta) == (4, 2, 2):
-        pieces = [packed, lax.ppermute(packed, "tri", cores)]
+        pieces = [slip, lax.ppermute(slip, "tri", cores)]
         codes = [(0, 0), (1, 1)]
         fetched = []
         for k in range(1, n_freq):
@@ -406,19 +372,20 @@
                 for t in range(n_tri)
                 for s in range(n_sta)
             ]
-            fetched.append(lax.ppermute(packed, ("freq", "tri", "sta"), pairs))
+            fetched.append(lax.ppermute(slip, ("freq", "tri", "sta"), pairs))
             codes.append((2 * k, 2 * k + 1))
-        fetched, prepared = lax.optimization_barrier((fetched, prepared))
+        fetched[0], prepared = lax.optimization_barrier((fetched[0], prepared))
+        fetched[-1], neighbours = lax.optimization_barrier((fetched[-1], neighbours))
         pieces += fetched + [lax.ppermute(v, "sta", cores) for v in fetched]
         codes += [(2 * k + 1, 2 * k) for k in range(1, n_freq)]
     else:
-        copies = jnp.broadcast_to(packed[None], (parts,) + packed.shape)
+        copies = jnp.broadcast_to(slip[None], (parts,) + slip.shape)
         pieces = [lax.all_to_all(copies, ("freq", "tri"), 0, 0, tiled=True)]
         codes = []
 
     pieces_of_green, onehot, turned, apart, own_table = prepared
     flops = 2 * freqs * 128 * 1024 * 256
-    whole = shape((parts,) + packed.shape, F32)
+    whole = shape((parts,) + slip.shape, F32)
     outs = pl.pallas_call(
         lambda *refs: forward_kernel(windows, codes, *refs),
         out_shape=(
@@ -426,7 +393,7 @@
             shape((n_sta, count, windows, columns), F32),
         )
         + ((whole,) if codes else ()),
-        in_specs=[SMEM] + [VMEM] * (len(pieces) + 5),
+        in_specs=[VMEM] * (len(pieces) + 5),
         out_specs=(VMEM,) * (3 if codes else 2),
         scratch_shapes=[
             pltpu.VMEM((blocks * windows, LANES), F32),
@@ -437,28 +404,33 @@
         ],
         compiler_params=grant,
         cost_estimate=pl.CostEstimate(flops=flops, bytes_accessed=4 * 2**20, transcendentals=0),
-    )(place, *pieces, pieces_of_green, onehot, turned, apart, own_table)
+    )(*pieces, pieces_of_green, onehot, turned, apart, own_table)
     residual, partial = outs[:2]
     shards = outs[2] if codes else pieces[0]
 
     smooth = pl.pallas_call(
         smooth_kernel,
         out_shape=shape((count, windows, columns), F32),
-        in_specs=[SMEM, SMEM, VMEM],
+        in_specs=[VMEM] * (1 + n_tri),
         out_specs=VMEM,
         compiler_params=grant,
         cost_estimate=pl.CostEstimate(flops=10**6, bytes_accessed=4 * 2**20, transcendentals=0),
-    )(place, smooth_weight, shards)
+    )(shards, *neighbours)
 
     mine = partial[0] + lax.ppermute(partial[1], "sta", cores)
+    mine = mine + smooth_weight[0] * smooth
     mine = sum(across(mine), mine) if n_freq <= 8 else lax.psum(mine, "freq")
-    mine = mine + smooth
     other = lax.ppermute(mine, "sta", cores)
 
-    own, image, numerator = pl.pallas_call(
+    ranks = n_freq * n_sta
+    own, image, norm = pl.pallas_call(
         image_kernel,
-        out_shape=(shape(slip.shape, F32),) * 3,
-        in_specs=[SMEM] + [VMEM] * 5,
+        out_shape=(
+            shape(slip.shape, F32),
+            shape((ranks, 8, LANES), F32),
+            shape((2, 8, LANES), F32),
+        ),
+        in_specs=[VMEM] * 6,
         out_specs=(VMEM,) * 3,
         scratch_shapes=[
             pltpu.VMEM((blocks * windows, LANES), F32),
@@ -466,12 +438,17 @@
         ],
         compiler_params=grant,
         cost_estimate=pl.CostEstimate(flops=flops, bytes_accessed=4 * 2**20, transcendentals=0),
-    )(place, mine, other, pieces_of_green, onehot, own_table)
-
-    image = image + lax.ppermute(image, "sta", cores)
-    image = sum(across(image), image) if n_freq <= 8 else lax.psum(image, "freq")
-    step = numerator / (image + smooth_weight[0] * numerator)
-    return jnp.maximum(slip - step * own, 0.0), residual
+    )(mine, other, pieces_of_green, onehot, own_table, smooth_weight.reshape(1, 1))
+
+    images = lax.all_to_all(image, ("freq", "sta"), 0, 0, tiled=True)
+    new_slip = pl.pallas_call(
+        update_kernel,
+        out_shape=shape(slip.shape, F32),
+        in_specs=[VMEM] * 4,
+        out_specs=VMEM,
+        compiler_params=grant,
+    )(images, norm, slip, own)
+    return new_slip, residual
 
 
 def solution(mesh):

time: 42.2 us -> 40.7 us (0.964)
  blocking collectives: 0 us -> 9.5 us
  starting transfers between devices: 17.3 us -> 12.9 us
  waiting for transfers between devices: 11.6 us -> 7.69 us
  Pallas kernels: 9.36 us -> 6.7 us
  other arithmetic: 0.74 us -> 0.04 us
  local copies, waits for them, and re-layouts: 1.58 us -> 2.25 us
    all_to_all x0 -> x1, blocking collectives: none -> 9.5 us  [local(): images = lax.all_to_all(image, ('freq', 'sta'), 0, 0, tiled=True)]
    ppermute x6 -> x3, starting transfers between devices: 8.84 us -> 4.23 us  [across(): lax.ppermute(value, 'freq', [(i, i ^ k) for i in range(n_freq)])]
    ppermute x5, waiting for transfers between devices: 3.23 us -> 0.32 us  [the longest x1 0.31 us: local(): lax.ppermute(adjacency, 'tri', [(i, i ^ k) for i in range(n_tri)])]
    pallas_call x1, Pallas kernels: 1.72 us -> 0.55 us  [local(): pl.pallas_call(prepare_kernel, out_shape=(shape((freqs, 2 * block, classe...]
    ppermute x1, waiting for transfers between devices: 1.09 us -> 0.01 us  [local(): mine = partial[0] + lax.ppermute(partial[1], 'sta', cores)]
    pallas_call x1, Pallas kernels: 2.39 us -> 1.46 us  [local(): pl.pallas_call(smooth_kernel, out_shape=shape((count, windows, columns),...]
    unnamed x14 -> x12, local copies, waits for them, and re-layouts: 1.57 us -> 2.25 us
    pallas_call x1, Pallas kernels: 3.32 us -> 2.68 us  [local(): pl.pallas_call(lambda *refs: forward_kernel(windows, codes, *refs), out_s...]
  transfers between devices with their start and end apart: 16 -> 13, of which waited for: 11 -> 8; matrix products, arithmetic and copies ran while one was open for 0% -> 0% of each run, Pallas kernels for 10% -> 5%
where the time goes in v3:
time: 40.7 us; the launch traced here: 40.5 us
  starting transfers between devices  12.9 us (32%)
  blocking collectives  9.5 us (23%)
  waiting for transfers between devices  7.69 us (19%)
  Pallas kernels  6.7 us (16%)
  local copies, waits for them, and re-layouts  2.25 us (6%)
  between operations  1.37 us (3%)
    all_to_all x1, blocking collectives, local(): images = lax.all_to_all(image, ('freq', 'sta'), 0, 0, tiled=True)  9.5 us
    ppermute x3, starting transfers between devices, local(): fetched.append(lax.ppermute(slip, ('freq', 'tri', 'sta'), pairs))  5.68 us
    ppermute x3, waiting for transfers between devices, across(): lax.ppermute(value, 'freq', [(i, i ^ k) for i in range(n_freq)])  5.27 us
    ppermute x3, starting transfers between devices, across(): lax.ppermute(value, 'freq', [(i, i ^ k) for i in range(n_freq)])  4.23 us
    pallas_call x1, Pallas kernels, local(): pl.pallas_call(lambda *refs: forward_kernel(windows, codes, *refs), out_s...  2.68 us
    unnamed x12, local copies, waits for them, and re-layouts  2.25 us
    ppermute x1, starting transfers between devices, local(): pieces = [slip, lax.ppermute(slip, 'tri', cores)]  1.49 us
    pallas_call x1, Pallas kernels, local(): pl.pallas_call(smooth_kernel, out_shape=shape((count, windows, columns),...  1.46 us
  transfers between devices with their start and end apart: 13, of which 8 were waited for; matrix products, arithmetic and copies ran while one was open for 0% of the time, Pallas kernels for 5%

profile of v3, /device:TPU:0, one launch (start us, length us, event | category | flops | bytes accessed | tf_op | source)
XLA Modules:
  0.0 40.5 jit_solution(8389975583188999034)
XLA Ops:
  0.6 3.1 %collective-permute-start.1 = (f32[8,512]{1,0:T(8,128)}, f32[8,512]{1,0:T(8,128)S(1)}, u32[]{:S(2)}, u32[]{:S(2)}) collective-permute-start(f32[8,512]{1,0:T(8,128)} %slip.1), channel_id=1, source_target_pairs={{4,0},{7,1},{6,2},{5,3},{0,4},{3,5},{2,6},{1,7},{12,8},{15,9},{14,... | collective-permute-start | bytes 49160 | tf_op jit(solution)/shard_map/ppermute | solution.py:375
  3.7 2.5 %collective-permute-start.3 = (f32[8,512]{1,0:T(8,128)}, f32[8,512]{1,0:T(8,128)S(1)}, u32[]{:S(2)}, u32[]{:S(2)}) collective-permute-start(f32[8,512]{1,0:T(8,128)} %slip.1), channel_id=1, source_target_pairs={{12,0},{15,1},{14,2},{13,3},{8,4},{11,5},{10,6},{9,7},{4,8},{7,9},... | collective-permute-start | bytes 49160 | tf_op jit(solution)/shard_map/ppermute | solution.py:375
  6.3 1.5 %collective-permute-start = (f32[8,512]{1,0:T(8,128)}, f32[8,512]{1,0:T(8,128)S(1)}, u32[]{:S(2)}, u32[]{:S(2)}) collective-permute-start(f32[8,512]{1,0:T(8,128)} %slip.1), channel_id=1, source_target_pairs={{0,2},{2,0},{1,3},{3,1},{4,6},{6,4},{5,7},{7,5},{8,10},{10,8},{9,1... | collective-permute-start | bytes 49160 | tf_op jit(solution)/shard_map/ppermute | solution.py:365
  7.8 0.5 %collective-permute-start.4 = (s32[3,256]{1,0:T(4,128)}, s32[3,256]{1,0:T(4,128)S(1)}, u32[]{:S(2)}, u32[]{:S(2)}) collective-permute-start(s32[3,256]{1,0:T(4,128)} %refs_0_.2), channel_id=1, source_target_pairs={{0,2},{2,0},{1,3},{3,1},{4,6},{6,4},{5,7},{7,5},{8,10},{10,8},{9,1... | collective-permute-start | bytes 9224 | tf_op jit(solution)/shard_map/ppermute | solution.py:362
  8.3 0.7 %copy-done.5 = s32[32,64]{1,0:T(8,128)S(1)} copy-done((s32[32,64]{1,0:T(8,128)S(1)}, s32[32,64]{1,0:T(8,128)}, u32[]{:S(2)}) %copy-start.5) | copy-done | bytes 8216
  9.1 1.5 %copy-done = f32[8,8,64,128]{3,2,1,0:T(8,128)S(1)} copy-done((f32[8,8,64,128]{3,2,1,0:T(8,128)S(1)}, f32[8,8,64,128]{3,2,1,0:T(8,128)}, u32[]{:S(2)}) %copy-start) | copy-done | bytes 2097176
  10.7 0.6 %shard_map.87 = (bf16[8,128,1024]{2,1,0:T(8,128)(2,1)S(1)}, bf16[1,256,128]{2,1,0:T(8,128)(2,1)S(1)}, bf16[1,64,512]{2,1,0:T(8,128)(2,1)S(1)}, f32[2,256,128]{2,1,0:T(8,128)S(1)}, f32[8,8,128]{2,1,0:T(8,128)S(1)}) custom-call(f32[8,8,64,128]{3,2,1,0:T(8,128)S(1)} %copy-done, s32[1,32,128]{2,1,0:T(8,128)S(1)} %shard_map.86.pattern_ref, ...), custom_call_target="tpu_custom_call" | custom-call | flops 1000000 | bytes 6291456 | tf_op jit(solution)/shard_map/pallas_call | solution.py:347
  11.3 0.3 collective-permute-done.4.refs_1_
  11.6 0.2 collective-permute-start.7
  11.8 0.3 collective-permute-start.6
  12.1 0.3 collective-permute-done.5.refs_5_
  12.5 0.3 collective-permute-done.7.refs_7_
  12.8 0.2 collective-permute-done.6.refs_6_
  13.0 2.7 %shard_map.88 = (f32[2,8,2048]{2,1,0:T(8,128)}, f32[2,4,8,512]{3,2,1,0:T(8,128)S(1)}, f32[8,8,512]{2,1,0:T(8,128)S(1)}) custom-call(f32[8,512]{1,0:T(8,128)S(1)} %copy-done.3, f32[8,512]{1,0:T(8,128)S(1)} %collective-permute-done.refs_1_, f32[8,512]{1,0:T(8,128)S(1)} %collective-permute-done.1.refs_2_, f32[8,512]{1,0:T(8,128)S(1)} %collective-permute-done.2.refs_3_, ...), custom_call_target="tpu_custom_call" | custom-call | flops 536870912 | bytes 4194304 | tf_op jit(solution)/shard_map/pallas_call | solution.py:389
  15.7 0.3 collective-permute-start.8
  16.7 1.5 %shard_map.89 = f32[4,8,512]{2,1,0:T(8,128)S(1)} custom-call(f32[8,8,512]{2,1,0:T(8,128)S(1)} %get-tuple-element.35.shards, s32[3,256]{1,0:T(4,128)S(1)} %copy-done.4, s32[3,256]{1,0:T(4,128)S(1)} %collective-permute-done.4.refs_1_), custom_call_target="tpu_custom_call" | custom-call | flops 1000000 | bytes 4194304 | tf_op jit(solution)/shard_map/pallas_call | solution.py:411
  18.2 2.9 %collective-permute-start.10 = (f32[4,8,512]{2,1,0:T(8,128)S(1)}, f32[4,8,512]{2,1,0:T(8,128)S(1)}, u32[]{:S(2)}, u32[]{:S(2)}) collective-permute-start(f32[4,8,512]{2,1,0:T(8,128)S(1)} %fusion), channel_id=1, source_target_pairs={{0,8},{4,12},{8,0},{12,4},{1,9},{5,13},{9,1},{13,5},{2,10},{6,14},... | collective-permute-start | bytes 196616 | tf_op jit(solution)/shard_map/ppermute | solution.py:335
  21.0 1.3 %collective-permute-start.11 = (f32[4,8,512]{2,1,0:T(8,128)S(1)}, f32[4,8,512]{2,1,0:T(8,128)S(1)}, u32[]{:S(2)}, u32[]{:S(2)}) collective-permute-start(f32[4,8,512]{2,1,0:T(8,128)S(1)} %fusion), channel_id=1, source_target_pairs={{0,12},{4,8},{8,4},{12,0},{1,13},{5,9},{9,5},{13,1},{2,14},{6,10},... | collective-permute-start | bytes 196616 | tf_op jit(solution)/shard_map/ppermute | solution.py:335
  22.4 2.8 %collective-permute-done.10 = f32[4,8,512]{2,1,0:T(8,128)S(1)} collective-permute-done((f32[4,8,512]{2,1,0:T(8,128)S(1)}, f32[4,8,512]{2,1,0:T(8,128)S(1)}, u32[]{:S(2)}, u32[]{:S(2)}) %collective-permute-start.10) | collective-permute-done | bytes 65568 | tf_op jit(solution)/shard_map/ppermute | solution.py:335
  25.2 2.3 %collective-permute-done.11 = f32[4,8,512]{2,1,0:T(8,128)S(1)} collective-permute-done((f32[4,8,512]{2,1,0:T(8,128)S(1)}, f32[4,8,512]{2,1,0:T(8,128)S(1)}, u32[]{:S(2)}, u32[]{:S(2)}) %collective-permute-start.11) | collective-permute-done | bytes 65568 | tf_op jit(solution)/shard_map/ppermute | solution.py:335
  27.8 1.2 %collective-permute-done.12.other = f32[4,8,512]{2,1,0:T(8,128)S(1)} collective-permute-done((f32[4,8,512]{2,1,0:T(8,128)S(1)}, f32[4,8,512]{2,1,0:T(8,128)S(1)}, u32[]{:S(2)}, u32[]{:S(2)}) %collective-permute-start.12) | collective-permute-done | bytes 65568 | tf_op jit(solution)/shard_map/ppermute | solution.py:423
  29.0 1.3 %shard_map.90 = (f32[8,512]{1,0:T(8,128)S(1)}, f32[8,8,128]{2,1,0:T(8,128)S(1)}, f32[2,8,128]{2,1,0:T(8,128)S(1)}) custom-call(f32[4,8,512]{2,1,0:T(8,128)S(1)} %add_add_fusion.mine, f32[4,8,512]{2,1,0:T(8,128)S(1)} %collective-permute-done.12.other, bf16[8,128,1024]{2,1,0:T(8,128)(2,1)S(1)} %get-tuple-element.29.refs_8_.green, ...), custom_call_target="tpu_custom_call" | custom-call | flops 536870912 | bytes 4194304 | tf_op jit(solution)/shard_map/pallas_call | solution.py:426
  30.3 9.5 %all_to_all.5.images = f32[8,8,128]{2,1,0:T(8,128)S(1)} all-to-all(f32[8,8,128]{2,1,0:T(8,128)S(1)} %get-tuple-element.38), channel_id=1, replica_groups=mesh['grp'=2,'freq'=4,'tri'=2,'sta'=2] {'freq','sta'}, dimensions={0} | all-to-all | bytes 65536 | tf_op jit(solution)/shard_map/all_to_all | solution.py:443
  39.8 0.6 %shard_map.91 = f32[8,512]{1,0:T(8,128)} custom-call(f32[8,8,128]{2,1,0:T(8,128)S(1)} %all_to_all.5.images, f32[2,8,128]{2,1,0:T(8,128)S(1)} %get-tuple-element.39.norm, f32[8,512]{1,0:T(8,128)S(1)} %copy-done.3, f32[8,512]{1,0:T(8,128)S(1)} %get-tuple-element.40.own), custom_call_target="tpu_custom_call" | custom-call | tf_op jit(solution)/shard_map/pallas_call | solution.py:444
  (24 shorter events, 0.6 us)
Async XLA Ops:
  0.6 10.6 %collective-permute-start.1 = (f32[8,512]{1,0:T(8,128)}, f32[8,512]{1,0:T(8,128)S(1)}, u32[]{:S(2)}, u32[]{:S(2)}) collective-permute-start(f32[8,512]{1,0:T(8,128)} %slip.1), channel_id=1, source_target_pairs={{4,0},{7,1},{6,2},{5,3},{0,4},{3,5},{2,6},{1,7},{12,8},{15,9},{14,... | collective-permute-start | bytes 49160 | tf_op jit(solution)/shard_map/ppermute | solution.py:375
  3.7 7.9 %collective-permute-start.3 = (f32[8,512]{1,0:T(8,128)}, f32[8,512]{1,0:T(8,128)S(1)}, u32[]{:S(2)}, u32[]{:S(2)}) collective-permute-start(f32[8,512]{1,0:T(8,128)} %slip.1), channel_id=1, source_target_pairs={{12,0},{15,1},{14,2},{13,3},{8,4},{11,5},{10,6},{9,7},{4,8},{7,9},... | collective-permute-start | bytes 49160 | tf_op jit(solution)/shard_map/ppermute | solution.py:375
  6.2 5.6 %collective-permute-start.2 = (f32[8,512]{1,0:T(8,128)}, f32[8,512]{1,0:T(8,128)S(1)}, u32[]{:S(2)}, u32[]{:S(2)}) collective-permute-start(f32[8,512]{1,0:T(8,128)} %slip.1), channel_id=1, source_target_pairs={{8,0},{11,1},{10,2},{9,3},{12,4},{15,5},{14,6},{13,7},{0,8},{3,9},... | collective-permute-start | bytes 49160 | tf_op jit(solution)/shard_map/ppermute | solution.py:375
  6.3 5.8 %collective-permute-start = (f32[8,512]{1,0:T(8,128)}, f32[8,512]{1,0:T(8,128)S(1)}, u32[]{:S(2)}, u32[]{:S(2)}) collective-permute-start(f32[8,512]{1,0:T(8,128)} %slip.1), channel_id=1, source_target_pairs={{0,2},{2,0},{1,3},{3,1},{4,6},{6,4},{5,7},{7,5},{8,10},{10,8},{9,1... | collective-permute-start | bytes 49160 | tf_op jit(solution)/shard_map/ppermute | solution.py:365
  7.8 3.8 %collective-permute-start.4 = (s32[3,256]{1,0:T(4,128)}, s32[3,256]{1,0:T(4,128)S(1)}, u32[]{:S(2)}, u32[]{:S(2)}) collective-permute-start(s32[3,256]{1,0:T(4,128)} %refs_0_.2), channel_id=1, source_target_pairs={{0,2},{2,0},{1,3},{3,1},{4,6},{6,4},{5,7},{7,5},{8,10},{10,8},{9,1... | collective-permute-start | bytes 9224 | tf_op jit(solution)/shard_map/ppermute | solution.py:362
  8.3 0.7 %copy-start.5 = (s32[32,64]{1,0:T(8,128)S(1)}, s32[32,64]{1,0:T(8,128)}, u32[]{:S(2)}) copy-start(s32[32,64]{1,0:T(8,128)} %param.9) | copy-start | bytes 24580
  9.1 1.6 %copy-start = (f32[8,8,64,128]{3,2,1,0:T(8,128)S(1)}, f32[8,8,64,128]{3,2,1,0:T(8,128)}, u32[]{:S(2)}) copy-start(f32[8,8,64,128]{3,2,1,0:T(8,128)} %green_ref.1) | copy-start | bytes 6291460
  9.1 1.6 %copy-start.1 = (f32[2,8,2048]{2,1,0:T(8,128)S(1)}, f32[2,8,2048]{2,1,0:T(8,128)}, u32[]{:S(2)}) copy-start(f32[2,8,2048]{2,1,0:T(8,128)} %observed.1) | copy-start | bytes 393220
  9.1 1.6 %copy-start.2 = (f32[32,8,128]{2,1,0:T(8,128)S(1)}, f32[32,8,128]{2,1,0:T(8,128)}, u32[]{:S(2)}) copy-start(f32[32,8,128]{2,1,0:T(8,128)} %constant.2.clone.table) | copy-start | bytes 393220
  10.7 2.4 %copy-start.3 = (f32[8,512]{1,0:T(8,128)S(1)}, f32[8,512]{1,0:T(8,128)}, u32[]{:S(2)}) copy-start(f32[8,512]{1,0:T(8,128)} %slip.1) | copy-start | bytes 49156
  10.7 6.0 %copy-start.4 = (s32[3,256]{1,0:T(4,128)S(1)}, s32[3,256]{1,0:T(4,128)}, u32[]{:S(2)}) copy-start(s32[3,256]{1,0:T(4,128)} %refs_0_.2) | copy-start | bytes 9220
  11.2 1.2 %collective-permute-start.5 = (f32[8,512]{1,0:T(8,128)S(1)}, f32[8,512]{1,0:T(8,128)S(1)}, u32[]{:S(2)}, u32[]{:S(2)}) collective-permute-start(f32[8,512]{1,0:T(8,128)S(1)} %collective-permute-done.1.refs_2_), channel_id=1, source_target_pairs={{0,1},{1,0},{2,3},{3,2},{4,5},{5,4},{6,7},{7,6},{8,9},{9,8},{10,11... | collective-permute-start | bytes 49160 | tf_op jit(solution)/shard_map/ppermute | solution.py:379
  11.6 1.2 %collective-permute-start.7 = (f32[8,512]{1,0:T(8,128)S(1)}, f32[8,512]{1,0:T(8,128)S(1)}, u32[]{:S(2)}, u32[]{:S(2)}) collective-permute-start(f32[8,512]{1,0:T(8,128)S(1)} %collective-permute-done.3.refs_4_), channel_id=1, source_target_pairs={{0,1},{1,0},{2,3},{3,2},{4,5},{5,4},{6,7},{7,6},{8,9},{9,8},{10,11... | collective-permute-start | bytes 49160 | tf_op jit(solution)/shard_map/ppermute | solution.py:379
  11.8 1.2 %collective-permute-start.6 = (f32[8,512]{1,0:T(8,128)S(1)}, f32[8,512]{1,0:T(8,128)S(1)}, u32[]{:S(2)}, u32[]{:S(2)}) collective-permute-start(f32[8,512]{1,0:T(8,128)S(1)} %collective-permute-done.2.refs_3_), channel_id=1, source_target_pairs={{0,1},{1,0},{2,3},{3,2},{4,5},{5,4},{6,7},{7,6},{8,9},{9,8},{10,11... | collective-permute-start | bytes 49160 | tf_op jit(solution)/shard_map/ppermute | solution.py:379
  15.7 2.4 %collective-permute-start.8 = (f32[4,8,512]{2,1,0:T(8,128)S(1)}, f32[4,8,512]{2,1,0:T(8,128)S(1)}, u32[]{:S(2)}, u32[]{:S(2)}) collective-permute-start(f32[4,8,512]{2,1,0:T(8,128)S(1)} %slice_bitcast_fusion), channel_id=1, source_target_pairs={{0,1},{1,0},{2,3},{3,2},{4,5},{5,4},{6,7},{7,6},{8,9},{9,8},{10,11... | collective-permute-start | bytes 196616 | tf_op jit(solution)/shard_map/ppermute | solution.py:420
  18.2 7.0 %collective-permute-start.10 = (f32[4,8,512]{2,1,0:T(8,128)S(1)}, f32[4,8,512]{2,1,0:T(8,128)S(1)}, u32[]{:S(2)}, u32[]{:S(2)}) collective-permute-start(f32[4,8,512]{2,1,0:T(8,128)S(1)} %fusion), channel_id=1, source_target_pairs={{0,8},{4,12},{8,0},{12,4},{1,9},{5,13},{9,1},{13,5},{2,10},{6,14},... | collective-permute-start | bytes 196616 | tf_op jit(solution)/shard_map/ppermute | solution.py:335
  21.0 6.5 %collective-permute-start.11 = (f32[4,8,512]{2,1,0:T(8,128)S(1)}, f32[4,8,512]{2,1,0:T(8,128)S(1)}, u32[]{:S(2)}, u32[]{:S(2)}) collective-permute-start(f32[4,8,512]{2,1,0:T(8,128)S(1)} %fusion), channel_id=1, source_target_pairs={{0,12},{4,8},{8,4},{12,0},{1,13},{5,9},{9,5},{13,1},{2,14},{6,10},... | collective-permute-start | bytes 196616 | tf_op jit(solution)/shard_map/ppermute | solution.py:335
  22.4 5.3 %collective-permute-start.9 = (f32[4,8,512]{2,1,0:T(8,128)S(1)}, f32[4,8,512]{2,1,0:T(8,128)S(1)}, u32[]{:S(2)}, u32[]{:S(2)}) collective-permute-start(f32[4,8,512]{2,1,0:T(8,128)S(1)} %fusion), channel_id=1, source_target_pairs={{0,4},{4,0},{8,12},{12,8},{1,5},{5,1},{9,13},{13,9},{2,6},{6,2},{1... | collective-permute-start | bytes 196616 | tf_op jit(solution)/shard_map/ppermute | solution.py:335
  27.7 1.3 %collective-permute-start.12 = (f32[4,8,512]{2,1,0:T(8,128)S(1)}, f32[4,8,512]{2,1,0:T(8,128)S(1)}, u32[]{:S(2)}, u32[]{:S(2)}) collective-permute-start(f32[4,8,512]{2,1,0:T(8,128)S(1)} %add_add_fusion.mine), channel_id=1, source_target_pairs={{0,1},{1,0},{2,3},{3,2},{4,5},{5,4},{6,7},{7,6},{8,9},{9,8},{10,11... | collective-permute-start | bytes 196616 | tf_op jit(solution)/shard_map/ppermute | solution.py:423

commit v4 on v3

--- a/solution.py
+++ b/solution.py
@@ -68,16 +68,35 @@
     return freq, freq * lax.axis_size("tri") + lax.axis_index("tri"), lax.axis_index("sta")
 
 
-def doubled_kernel(pattern, out):
-    out[...] = jnp.concatenate([pattern[...], pattern[...]], axis=2)
+def ahead_kernel(out):
+    out[...] = jnp.zeros(out.shape, F32)
+
+
+def pack_kernel(slip, adjacency, out):
+    windows, columns = slip.shape
+    neighbours, triangles = adjacency.shape
+    out[:, :columns] = slip[...]
+    out[:neighbours, columns:] = adjacency[...].astype(F32)
+    out[neighbours:, columns:] = jnp.zeros((windows - neighbours, triangles), F32)
 
 
 def prepare_kernel(
-    green_ref, pattern_ref, observed, table, green_out, onehot_out, turned_out, apart, table_out
+    green_ref,
+    pattern_ref,
+    observed,
+    table,
+    ahead,
+    green_out,
+    onehot_out,
+    turned_out,
+    apart,
+    table_out,
+    ahead_out,
 ):
     freqs, classes, block, _ = green_ref.shape
     chunks, stations, _ = pattern_ref.shape
     first = positions()[0] * freqs
+    ahead_out[...] = ahead[...]
     for f in range(freqs):
         for k in range(classes):
             high, low = split(green_ref[f, k])
@@ -86,7 +105,8 @@
         table_out[f] = table[first + f]
 
     def step(n):
-        onehot = onehot_of(pattern_ref[n], classes)
+        value = pattern_ref[n]
+        onehot = onehot_of(jnp.concatenate([value, value], axis=1), classes)
         onehot_out[n] = onehot.astype(BF16)
         turned = onehot[:, :block].T.astype(BF16)
         turned_out[n] = jnp.concatenate([turned, turned], axis=1)
@@ -151,15 +171,16 @@
     _, me, half = positions()
     count = max(len(codes), 1)
     pieces, refs = refs[:count], refs[count:]
-    green, onehot_ref, turned_ref, apart, table = refs[:5]
-    residual_out, partial_out = refs[5:7]
+    green, onehot_ref, turned_ref, apart, table, ahead, weight = refs[:7]
+    residual_out, partial_out, weight_out = refs[7:10]
+    weight_out[...] = ahead[...] + weight[...]
     if codes:
-        shards, refs = refs[7], refs[8:]
+        shards, refs = refs[10], refs[11:]
         for (even, odd), piece in zip(codes, pieces):
             code = jnp.where(half == 0, even, odd).astype(jnp.int32)
-            shards[lax.bitwise_xor(me, code)] = piece[...]
+            shards[lax.bitwise_xor(me, code)] = piece[:, : shards.shape[2]]
     else:
-        shards, refs = pieces[0], refs[7:]
+        shards, refs = pieces[0], refs[10:]
     spread, summed, adjoint_rows, missed, fields = refs
     freqs, rows, _ = green.shape
     block = rows // 2
@@ -225,7 +246,7 @@
     over_chunks(turned_ref.shape[0], step)
 
 
-def smooth_kernel(shards, *refs):
+def smooth_kernel(shards, weight, *refs):
     adjacency, out = refs[:-1], refs[-1]
     count, windows, width = out.shape
     parts = shards.shape[0]
@@ -240,22 +261,25 @@
     _, me, half = positions()
     for k in range(tris):
         p = me - lax.rem(me, tris) + lax.bitwise_xor(lax.rem(me, tris), jnp.int32(k))
-        factor = jnp.where(p // count == half, 1.0, 0.0)
+        factor = jnp.where(p // count == half, weight[...], 0.0)
         around = [jnp.maximum(p - 1, 0), p, jnp.minimum(p + 1, parts - 1)]
         source = [shards[a, :, j * LANES : (j + 1) * LANES] for a in around for j in range(pieces)]
         for q in range(pieces):
-            total = None
             for j in range(3):
-                row = adjacency[k][j : j + 1, (q // 2) * LANES : (q // 2 + 1) * LANES]
+                start = width + (q // 2) * LANES
+                row = adjacency[k][j : j + 1, start : start + LANES]
                 row = jnp.broadcast_to(row, (windows, LANES))
-                target = pick(row, (q % 2) * (LANES // 2) + lane // 2)
+                target = pick(row, (q % 2) * (LANES // 2) + lane // 2).astype(jnp.int32)
+                if j == 0:
+                    total = jnp.where(target < p * (width // 2), source[q], source[2 * pieces + q])
+                    continue
                 column = 2 * target + lane % 2 - (p - 1) * width
                 inside = jnp.bitwise_and(column, LANES - 1)
                 which = jnp.right_shift(column, 7)
                 value = jnp.zeros((windows, LANES), F32)
                 for v in range(q, q + 2 * pieces + 1):
                     value = jnp.where(which == v, pick(source[v], inside), value)
-                total = value if total is None else total + value
+                total = total + value
             own = source[pieces + q]
             out[lax.rem(p, count), :, q * LANES : (q + 1) * LANES] = factor * (own - total / 3.0)
 
@@ -336,14 +360,14 @@
             for k in range(1, n_freq)
         ]
 
-    doubled = pl.pallas_call(
-        doubled_kernel,
-        out_shape=shape((chunks, stations, 2 * CHUNK), jnp.int32),
-        in_specs=[VMEM],
+    ahead = pl.pallas_call(
+        ahead_kernel,
+        out_shape=shape((8, LANES), F32),
         out_specs=VMEM,
         compiler_params=grant,
         cost_estimate=pl.CostEstimate(flops=10**10, bytes_accessed=2**10, transcendentals=0),
-    )(pattern)
+    )()
+    adjacency, ahead = lax.optimization_barrier((adjacency, ahead))
     prepared = pl.pallas_call(
         prepare_kernel,
         out_shape=(
@@ -352,17 +376,25 @@
             shape((chunks, CHUNK, 2 * classes * stations), BF16),
             shape((2, stations * freqs, LANES), F32),
             shape((freqs, windows, LANES), F32),
+            shape((8, LANES), F32),
         ),
-        in_specs=[VMEM] * 4,
-        out_specs=(VMEM,) * 5,
+        in_specs=[VMEM] * 5,
+        out_specs=(VMEM,) * 6,
         compiler_params=grant,
         cost_estimate=pl.CostEstimate(flops=10**6, bytes_accessed=6 * 2**20, transcendentals=0),
-    )(green, doubled, observed, table)
-    neighbours = [adjacency] + [
-        lax.ppermute(adjacency, "tri", [(i, i ^ k) for i in range(n_tri)]) for k in range(1, n_tri)
+    )(green, pattern, observed, table, ahead)
+    packed = pl.pallas_call(
+        pack_kernel,
+        out_shape=shape((windows, columns + adjacency.shape[1]), F32),
+        in_specs=[VMEM] * 2,
+        out_specs=VMEM,
+        compiler_params=grant,
+    )(slip, adjacency)
+    neighbours = [packed] + [
+        lax.ppermute(packed, "tri", [(i, i ^ k) for i in range(n_tri)]) for k in range(1, n_tri)
     ]
     if (n_freq, n_tri, n_sta) == (4, 2, 2):
-        pieces = [slip, lax.ppermute(slip, "tri", cores)]
+        pieces = list(neighbours)
         codes = [(0, 0), (1, 1)]
         fetched = []
         for k in range(1, n_freq):
@@ -375,7 +407,6 @@
             fetched.append(lax.ppermute(slip, ("freq", "tri", "sta"), pairs))
             codes.append((2 * k, 2 * k + 1))
         fetched[0], prepared = lax.optimization_barrier((fetched[0], prepared))
-        fetched[-1], neighbours = lax.optimization_barrier((fetched[-1], neighbours))
         pieces += fetched + [lax.ppermute(v, "sta", cores) for v in fetched]
         codes += [(2 * k + 1, 2 * k) for k in range(1, n_freq)]
     else:
@@ -383,7 +414,7 @@
         pieces = [lax.all_to_all(copies, ("freq", "tri"), 0, 0, tiled=True)]
         codes = []
 
-    pieces_of_green, onehot, turned, apart, own_table = prepared
+    pieces_of_green, onehot, turned, apart, own_table, ahead = prepared
     flops = 2 * freqs * 128 * 1024 * 256
     whole = shape((parts,) + slip.shape, F32)
     outs = pl.pallas_call(
@@ -391,10 +422,11 @@
         out_shape=(
             shape(observed.shape, F32),
             shape((n_sta, count, windows, columns), F32),
+            shape((8, LANES), F32),
         )
         + ((whole,) if codes else ()),
-        in_specs=[VMEM] * (len(pieces) + 5),
-        out_specs=(VMEM,) * (3 if codes else 2),
+        in_specs=[VMEM] * (len(pieces) + 7),
+        out_specs=(VMEM,) * (4 if codes else 3),
         scratch_shapes=[
             pltpu.VMEM((blocks * windows, LANES), F32),
             pltpu.VMEM((classes * stations, freqs * LANES), F32),
@@ -404,21 +436,21 @@
         ],
         compiler_params=grant,
         cost_estimate=pl.CostEstimate(flops=flops, bytes_accessed=4 * 2**20, transcendentals=0),
-    )(*pieces, pieces_of_green, onehot, turned, apart, own_table)
-    residual, partial = outs[:2]
-    shards = outs[2] if codes else pieces[0]
+    )(*pieces, pieces_of_green, onehot, turned, apart, own_table, ahead, smooth_weight.reshape(1, 1))
+    residual, partial, weights = outs[:3]
+    shards = outs[3] if codes else pieces[0]
 
     smooth = pl.pallas_call(
         smooth_kernel,
         out_shape=shape((count, windows, columns), F32),
-        in_specs=[VMEM] * (1 + n_tri),
+        in_specs=[VMEM] * (2 + n_tri),
         out_specs=VMEM,
         compiler_params=grant,
         cost_estimate=pl.CostEstimate(flops=10**6, bytes_accessed=4 * 2**20, transcendentals=0),
-    )(shards, *neighbours)
+    )(shards, weights, *neighbours)
 
     mine = partial[0] + lax.ppermute(partial[1], "sta", cores)
-    mine = mine + smooth_weight[0] * smooth
+    mine = mine + smooth
     mine = sum(across(mine), mine) if n_freq <= 8 else lax.psum(mine, "freq")
     other = lax.ppermute(mine, "sta", cores)
 
@@ -438,7 +470,7 @@
         ],
         compiler_params=grant,
         cost_estimate=pl.CostEstimate(flops=flops, bytes_accessed=4 * 2**20, transcendentals=0),
-    )(mine, other, pieces_of_green, onehot, own_table, smooth_weight.reshape(1, 1))
+    )(mine, other, pieces_of_green, onehot, own_table, weights)
 
     images = lax.all_to_all(image, ("freq", "sta"), 0, 0, tiled=True)
     new_slip = pl.pallas_call(

time: 40.7 us -> 37.9 us (0.931)
  local copies, waits for them, and re-layouts: 2.25 us -> 0.03 us
  blocking collectives: 9.5 us -> 8.28 us
  waiting for transfers between devices: 7.69 us -> 8.61 us
  Pallas kernels: 6.7 us -> 6.24 us
    ppermute x3, waiting for transfers between devices: 0.01 us -> 3.19 us  [local(): fetched.append(lax.ppermute(slip, ('freq', 'tri', 'sta'), pairs))]
    unnamed x12, local copies, waits for them, and re-layouts: 2.25 us -> 0.03 us
    ppermute x3, waiting for transfers between devices: 5.27 us -> 3.94 us  [across(): lax.ppermute(value, 'freq', [(i, i ^ k) for i in range(n_freq)])]
    all_to_all x1, blocking collectives: 9.5 us -> 8.28 us  [local(): images = lax.all_to_all(image, ('freq', 'sta'), 0, 0, tiled=True)]
    ppermute x3, waiting for transfers between devices: 0.86 us -> 0.16 us  [local(): pieces += fetched + [lax.ppermute(v, 'sta', cores) for v in fetched]]
    pallas_call x1, Pallas kernels: 1.46 us -> 0.82 us  [local(): pl.pallas_call(smooth_kernel, out_shape=shape((count, windows, columns),...]
    ppermute x2 -> x1, starting transfers between devices: 2.03 us -> 1.77 us  [local(): lax.ppermute(packed, 'tri', [(i, i ^ k) for i in range(n_tri)])]
  transfers between devices with their start and end apart: 13 -> 12, of which waited for: 8 -> 6; matrix products, arithmetic and copies ran while one was open for 0% -> 0% of each run, Pallas kernels for 5% -> 4%
where the time goes in v4:
time: 37.9 us; the launch traced here: 37.7 us
  starting transfers between devices  13 us (34%)
  waiting for transfers between devices  8.61 us (23%)
  blocking collectives  8.28 us (22%)
  Pallas kernels  6.24 us (16%)
  between operations  1.43 us (4%)
    all_to_all x1, blocking collectives, local(): images = lax.all_to_all(image, ('freq', 'sta'), 0, 0, tiled=True)  8.28 us
    ppermute x3, starting transfers between devices, local(): fetched.append(lax.ppermute(slip, ('freq', 'tri', 'sta'), pairs))  5.68 us
    ppermute x3, starting transfers between devices, across(): lax.ppermute(value, 'freq', [(i, i ^ k) for i in range(n_freq)])  4.45 us
    ppermute x3, waiting for transfers between devices, across(): lax.ppermute(value, 'freq', [(i, i ^ k) for i in range(n_freq)])  3.94 us
    ppermute x3, waiting for transfers between devices, local(): fetched.append(lax.ppermute(slip, ('freq', 'tri', 'sta'), pairs))  3.19 us
    pallas_call x1, Pallas kernels, local(): pl.pallas_call(lambda *refs: forward_kernel(windows, codes, *refs), out_s...  2.86 us
    ppermute x1, starting transfers between devices, local(): lax.ppermute(packed, 'tri', [(i, i ^ k) for i in range(n_tri)])  1.77 us
    pallas_call x1, Pallas kernels, local(): pl.pallas_call(image_kernel, out_shape=(shape(slip.shape, F32), shape((ra...  1.36 us
  transfers between devices with their start and end apart: 12, of which 6 were waited for; matrix products, arithmetic and copies ran while one was open for 0% of the time, Pallas kernels for 4%

profile of v4, /device:TPU:0, one launch (start us, length us, event | category | flops | bytes accessed | tf_op | source)
XLA Modules:
  0.0 37.7 jit_solution(3487796292312806860)
XLA Ops:
  0.6 0.0 copy-start.2
  0.7 4.1 %collective-permute-start.2 = (f32[8,512]{1,0:T(8,128)}, f32[8,512]{1,0:T(8,128)S(1)}, u32[]{:S(2)}, u32[]{:S(2)}) collective-permute-start(f32[8,512]{1,0:T(8,128)} %slip.3), channel_id=1, source_target_pairs={{8,0},{11,1},{10,2},{9,3},{12,4},{15,5},{14,6},{13,7},{0,8},{3,9},... | collective-permute-start | bytes 49160 | tf_op jit(solution)/shard_map/ppermute | solution.py:407
  4.8 1.6 %collective-permute-start.1 = (f32[8,512]{1,0:T(8,128)}, f32[8,512]{1,0:T(8,128)S(1)}, u32[]{:S(2)}, u32[]{:S(2)}) collective-permute-start(f32[8,512]{1,0:T(8,128)} %slip.3), channel_id=1, source_target_pairs={{4,0},{7,1},{6,2},{5,3},{0,4},{3,5},{2,6},{1,7},{12,8},{15,9},{14,... | collective-permute-start | bytes 49160 | tf_op jit(solution)/shard_map/ppermute | solution.py:407
  6.4 0.0 collective-permute-start.3
  6.4 1.8 %collective-permute-start = (f32[8,768]{1,0:T(8,128)S(1)}, f32[8,768]{1,0:T(8,128)S(1)}, u32[]{:S(2)}, u32[]{:S(2)}) collective-permute-start(f32[8,768]{1,0:T(8,128)S(1)} %shard_map.87.refs_0_), channel_id=1, source_target_pairs={{0,2},{2,0},{1,3},{3,1},{4,6},{6,4},{5,7},{7,5},{8,10},{10,8},{9,1... | collective-permute-start | bytes 73736 | tf_op jit(solution)/shard_map/ppermute | solution.py:394
  8.2 0.6 %shard_map.88 = (bf16[8,128,1024]{2,1,0:T(8,128)(2,1)S(1)}, bf16[1,256,128]{2,1,0:T(8,128)(2,1)S(1)}, bf16[1,64,512]{2,1,0:T(8,128)(2,1)S(1)}, f32[2,256,128]{2,...) custom-call(f32[8,8,64,128]{3,2,1,0:T(8,128)S(1)} %copy-done, s32[1,32,64]{2,1,0:T(8,128)S(1)} %bitcast.9, ...), custom_call_target="tpu_custom_call" | custom-call | flops 1000000 | bytes 6291456 | tf_op jit(solution)/shard_map/pallas_call | solution.py:371
  8.7 0.0 collective-permute-done.1.refs_2_
  8.8 0.2 collective-permute-start.5
  9.0 3.2 %collective-permute-done.3.refs_4_ = f32[8,512]{1,0:T(8,128)S(1)} collective-permute-done((f32[8,512]{1,0:T(8,128)}, f32[8,512]{1,0:T(8,128)S(1)}, u32[]{:S(2)}, u32[]{:S(2)}) %collective-permute-start.3) | collective-permute-done | bytes 16416 | tf_op jit(solution)/shard_map/ppermute | solution.py:407
  12.2 0.5 %collective-permute-start.4 = (f32[8,512]{1,0:T(8,128)S(1)}, f32[8,512]{1,0:T(8,128)S(1)}, u32[]{:S(2)}, u32[]{:S(2)}) collective-permute-start(f32[8,512]{1,0:T(8,128)S(1)} %collective-permute-done.1.refs_2_), channel_id=1, source_target_pairs={{0,1},{1,0},{2,3},{3,2},{4,5},{5,4},{6,7},{7,6},{8,9},{9,8},{10,11... | collective-permute-start | bytes 49160 | tf_op jit(solution)/shard_map/ppermute | solution.py:410
  13.4 0.2 collective-permute-done.4.refs_5_
  13.5 2.9 %shard_map.89 = (f32[2,8,2048]{2,1,0:T(8,128)}, f32[2,4,8,512]{3,2,1,0:T(8,128)S(1)}, f32[8,128]{1,0:T(8,128)S(1)}, f32[8,8,512]{2,1,0:T(8,128)S(1)}) custom-call(f32[8,768]{1,0:T(8,128)S(1)} %shard_map.87.refs_0_, f32[8,768]{1,0:T(8,128)S(1)} %collective-permute-done.refs_1_, f32[8,512]{1,0:T(8,128)S(1)} %collective-permute-done.1.refs_2_, ...), custom_call_target="tpu_custom_call" | custom-call | flops 536870912 | bytes 4194304 | tf_op jit(solution)/shard_map/pallas_call | solution.py:420
  16.4 0.3 collective-permute-start.7
  16.7 0.8 %shard_map.90 = f32[4,8,512]{2,1,0:T(8,128)S(1)} custom-call(f32[8,8,512]{2,1,0:T(8,128)S(1)} %get-tuple-element.40.shards, f32[8,128]{1,0:T(8,128)S(1)} %get-tuple-element.41.weight, f32[8,768]{1,0:T(8,128)S(1)} %shard_map.87.refs_0_, f32[8,768]{1,0:T(8,128)S(1)} %collective-permute-done.refs_1_), custom_call_target="tpu_custom_call" | custom-call | flops 1000000 | bytes 4194304 | tf_op jit(solution)/shard_map/pallas_call | solution.py:443
  17.6 0.1 collective-permute-done.7
  17.7 0.8 %collective-permute-start.10 = (f32[4,8,512]{2,1,0:T(8,128)S(1)}, f32[4,8,512]{2,1,0:T(8,128)S(1)}, u32[]{:S(2)}, u32[]{:S(2)}) collective-permute-start(f32[4,8,512]{2,1,0:T(8,128)S(1)} %fusion), channel_id=1, source_target_pairs={{0,12},{4,8},{8,4},{12,0},{1,13},{5,9},{9,5},{13,1},{2,14},{6,10},... | collective-permute-start | bytes 196616 | tf_op jit(solution)/shard_map/ppermute | solution.py:359
  18.5 3.6 %collective-permute-start.8 = (f32[4,8,512]{2,1,0:T(8,128)S(1)}, f32[4,8,512]{2,1,0:T(8,128)S(1)}, u32[]{:S(2)}, u32[]{:S(2)}) collective-permute-start(f32[4,8,512]{2,1,0:T(8,128)S(1)} %fusion), channel_id=1, source_target_pairs={{0,4},{4,0},{8,12},{12,8},{1,5},{5,1},{9,13},{13,9},{2,6},{6,2},{1... | collective-permute-start | bytes 196616 | tf_op jit(solution)/shard_map/ppermute | solution.py:359
  22.1 2.4 %collective-permute-done.10 = f32[4,8,512]{2,1,0:T(8,128)S(1)} collective-permute-done((f32[4,8,512]{2,1,0:T(8,128)S(1)}, f32[4,8,512]{2,1,0:T(8,128)S(1)}, u32[]{:S(2)}, u32[]{:S(2)}) %collective-permute-start.10) | collective-permute-done | bytes 65568 | tf_op jit(solution)/shard_map/ppermute | solution.py:359
  24.5 1.5 %collective-permute-done.9 = f32[4,8,512]{2,1,0:T(8,128)S(1)} collective-permute-done((f32[4,8,512]{2,1,0:T(8,128)S(1)}, f32[4,8,512]{2,1,0:T(8,128)S(1)}, u32[]{:S(2)}, u32[]{:S(2)}) %collective-permute-start.9) | collective-permute-done | bytes 65568 | tf_op jit(solution)/shard_map/ppermute | solution.py:359
  26.1 0.1 collective-permute-start.11
  26.1 1.2 %collective-permute-done.11.other = f32[4,8,512]{2,1,0:T(8,128)S(1)} collective-permute-done((f32[4,8,512]{2,1,0:T(8,128)S(1)}, f32[4,8,512]{2,1,0:T(8,128)S(1)}, u32[]{:S(2)}, u32[]{:S(2)}) %collective-permute-start.11) | collective-permute-done | bytes 65568 | tf_op jit(solution)/shard_map/ppermute | solution.py:455
  27.4 1.4 %shard_map.91 = (f32[8,512]{1,0:T(8,128)S(1)}, f32[8,8,128]{2,1,0:T(8,128)S(1)}, f32[2,8,128]{2,1,0:T(8,128)S(1)}) custom-call(f32[4,8,512]{2,1,0:T(8,128)S(1)} %add_add_fusion.mine, f32[4,8,512]{2,1,0:T(8,128)S(1)} %collective-permute-done.11.other, bf16[8,128,1024]{2,1,0:T(8,128)(2,1)S(1)} %get-tuple-element.33.refs_8_.green, ...), custom_call_target="tpu_custom_call" | custom-call | flops 536870912 | bytes 4194304 | tf_op jit(solution)/shard_map/pallas_call | solution.py:458
  28.8 8.3 %all_to_all.5.images = f32[8,8,128]{2,1,0:T(8,128)S(1)} all-to-all(f32[8,8,128]{2,1,0:T(8,128)S(1)} %get-tuple-element.42), channel_id=1, replica_groups=mesh['grp'=2,'freq'=4,'tri'=2,'sta'=2] {'freq','sta'}, dimensions={0} | all-to-all | bytes 65536 | tf_op jit(solution)/shard_map/all_to_all | solution.py:475
  37.0 0.6 %shard_map.92 = f32[8,512]{1,0:T(8,128)} custom-call(f32[8,8,128]{2,1,0:T(8,128)S(1)} %all_to_all.5.images, f32[2,8,128]{2,1,0:T(8,128)S(1)} %get-tuple-element.43.norm, f32[8,512]{1,0:T(8,128)S(1)} %copy-done.3, f32[8,512]{1,0:T(8,128)S(1)} %get-tuple-element.44.own), custom_call_target="tpu_custom_call" | custom-call | tf_op jit(solution)/shard_map/pallas_call | solution.py:476
  (23 shorter events, 0.1 us)
Async XLA Ops:
  0.6 7.5 %copy-start.2 = (f32[32,8,128]{2,1,0:T(8,128)S(1)}, f32[32,8,128]{2,1,0:T(8,128)}, u32[]{:S(2)}) copy-start(f32[32,8,128]{2,1,0:T(8,128)} %constant.2.clone.table) | copy-start | bytes 393220
  0.6 5.7 %copy-start.3 = (f32[8,512]{1,0:T(8,128)S(1)}, f32[8,512]{1,0:T(8,128)}, u32[]{:S(2)}) copy-start(f32[8,512]{1,0:T(8,128)} %slip.3) | copy-start | bytes 49156
  0.7 5.7 %copy-start.5 = (s32[3,256]{1,0:T(4,128)S(1)}, s32[3,256]{1,0:T(4,128)}, u32[]{:S(2)}) copy-start(s32[3,256]{1,0:T(4,128)} %adjacency) | copy-start | bytes 9220
  0.7 7.5 %copy-start.1 = (f32[2,8,2048]{2,1,0:T(8,128)S(1)}, f32[2,8,2048]{2,1,0:T(8,128)}, u32[]{:S(2)}) copy-start(f32[2,8,2048]{2,1,0:T(8,128)} %observed.1) | copy-start | bytes 393220
  0.7 7.5 %copy-start.4 = (s32[32,64]{1,0:T(8,128)S(1)}, s32[32,64]{1,0:T(8,128)}, u32[]{:S(2)}) copy-start(s32[32,64]{1,0:T(8,128)} %param.9) | copy-start | bytes 24580
  0.7 7.5 %copy-start = (f32[8,8,64,128]{3,2,1,0:T(8,128)S(1)}, f32[8,8,64,128]{3,2,1,0:T(8,128)}, u32[]{:S(2)}) copy-start(f32[8,8,64,128]{3,2,1,0:T(8,128)} %green_ref.1) | copy-start | bytes 6291460
  0.7 8.1 %collective-permute-start.2 = (f32[8,512]{1,0:T(8,128)}, f32[8,512]{1,0:T(8,128)S(1)}, u32[]{:S(2)}, u32[]{:S(2)}) collective-permute-start(f32[8,512]{1,0:T(8,128)} %slip.3), channel_id=1, source_target_pairs={{8,0},{11,1},{10,2},{9,3},{12,4},{15,5},{14,6},{13,7},{0,8},{3,9},... | collective-permute-start | bytes 49160 | tf_op jit(solution)/shard_map/ppermute | solution.py:407
  4.8 4.0 %collective-permute-start.1 = (f32[8,512]{1,0:T(8,128)}, f32[8,512]{1,0:T(8,128)S(1)}, u32[]{:S(2)}, u32[]{:S(2)}) collective-permute-start(f32[8,512]{1,0:T(8,128)} %slip.3), channel_id=1, source_target_pairs={{4,0},{7,1},{6,2},{5,3},{0,4},{3,5},{2,6},{1,7},{12,8},{15,9},{14,... | collective-permute-start | bytes 49160 | tf_op jit(solution)/shard_map/ppermute | solution.py:407
  6.4 5.8 %collective-permute-start.3 = (f32[8,512]{1,0:T(8,128)}, f32[8,512]{1,0:T(8,128)S(1)}, u32[]{:S(2)}, u32[]{:S(2)}) collective-permute-start(f32[8,512]{1,0:T(8,128)} %slip.3), channel_id=1, source_target_pairs={{12,0},{15,1},{14,2},{13,3},{8,4},{11,5},{10,6},{9,7},{4,8},{7,9},... | collective-permute-start | bytes 49160 | tf_op jit(solution)/shard_map/ppermute | solution.py:407
  6.4 6.9 %collective-permute-start = (f32[8,768]{1,0:T(8,128)S(1)}, f32[8,768]{1,0:T(8,128)S(1)}, u32[]{:S(2)}, u32[]{:S(2)}) collective-permute-start(f32[8,768]{1,0:T(8,128)S(1)} %shard_map.87.refs_0_), channel_id=1, source_target_pairs={{0,2},{2,0},{1,3},{3,1},{4,6},{6,4},{5,7},{7,5},{8,10},{10,8},{9,1... | collective-permute-start | bytes 73736 | tf_op jit(solution)/shard_map/ppermute | solution.py:394
  8.8 4.6 %collective-permute-start.5 = (f32[8,512]{1,0:T(8,128)S(1)}, f32[8,512]{1,0:T(8,128)S(1)}, u32[]{:S(2)}, u32[]{:S(2)}) collective-permute-start(f32[8,512]{1,0:T(8,128)S(1)} %collective-permute-done.2.refs_3_), channel_id=1, source_target_pairs={{0,1},{1,0},{2,3},{3,2},{4,5},{5,4},{6,7},{7,6},{8,9},{9,8},{10,11... | collective-permute-start | bytes 49160 | tf_op jit(solution)/shard_map/ppermute | solution.py:410
  12.2 1.2 %collective-permute-start.6 = (f32[8,512]{1,0:T(8,128)S(1)}, f32[8,512]{1,0:T(8,128)S(1)}, u32[]{:S(2)}, u32[]{:S(2)}) collective-permute-start(f32[8,512]{1,0:T(8,128)S(1)} %collective-permute-done.3.refs_4_), channel_id=1, source_target_pairs={{0,1},{1,0},{2,3},{3,2},{4,5},{5,4},{6,7},{7,6},{8,9},{9,8},{10,11... | collective-permute-start | bytes 49160 | tf_op jit(solution)/shard_map/ppermute | solution.py:410
  12.2 1.3 %collective-permute-start.4 = (f32[8,512]{1,0:T(8,128)S(1)}, f32[8,512]{1,0:T(8,128)S(1)}, u32[]{:S(2)}, u32[]{:S(2)}) collective-permute-start(f32[8,512]{1,0:T(8,128)S(1)} %collective-permute-done.1.refs_2_), channel_id=1, source_target_pairs={{0,1},{1,0},{2,3},{3,2},{4,5},{5,4},{6,7},{7,6},{8,9},{9,8},{10,11... | collective-permute-start | bytes 49160 | tf_op jit(solution)/shard_map/ppermute | solution.py:410
  16.4 1.3 %collective-permute-start.7 = (f32[4,8,512]{2,1,0:T(8,128)S(1)}, f32[4,8,512]{2,1,0:T(8,128)S(1)}, u32[]{:S(2)}, u32[]{:S(2)}) collective-permute-start(f32[4,8,512]{2,1,0:T(8,128)S(1)} %slice_bitcast_fusion), channel_id=1, source_target_pairs={{0,1},{1,0},{2,3},{3,2},{4,5},{5,4},{6,7},{7,6},{8,9},{9,8},{10,11... | collective-permute-start | bytes 196616 | tf_op jit(solution)/shard_map/ppermute | solution.py:452
  17.7 6.9 %collective-permute-start.10 = (f32[4,8,512]{2,1,0:T(8,128)S(1)}, f32[4,8,512]{2,1,0:T(8,128)S(1)}, u32[]{:S(2)}, u32[]{:S(2)}) collective-permute-start(f32[4,8,512]{2,1,0:T(8,128)S(1)} %fusion), channel_id=1, source_target_pairs={{0,12},{4,8},{8,4},{12,0},{1,13},{5,9},{9,5},{13,1},{2,14},{6,10},... | collective-permute-start | bytes 196616 | tf_op jit(solution)/shard_map/ppermute | solution.py:359
  18.5 7.6 %collective-permute-start.9 = (f32[4,8,512]{2,1,0:T(8,128)S(1)}, f32[4,8,512]{2,1,0:T(8,128)S(1)}, u32[]{:S(2)}, u32[]{:S(2)}) collective-permute-start(f32[4,8,512]{2,1,0:T(8,128)S(1)} %fusion), channel_id=1, source_target_pairs={{0,8},{4,12},{8,0},{12,4},{1,9},{5,13},{9,1},{13,5},{2,10},{6,14},... | collective-permute-start | bytes 196616 | tf_op jit(solution)/shard_map/ppermute | solution.py:359
  18.5 7.6 %collective-permute-start.8 = (f32[4,8,512]{2,1,0:T(8,128)S(1)}, f32[4,8,512]{2,1,0:T(8,128)S(1)}, u32[]{:S(2)}, u32[]{:S(2)}) collective-permute-start(f32[4,8,512]{2,1,0:T(8,128)S(1)} %fusion), channel_id=1, source_target_pairs={{0,4},{4,0},{8,12},{12,8},{1,5},{5,1},{9,13},{13,9},{2,6},{6,2},{1... | collective-permute-start | bytes 196616 | tf_op jit(solution)/shard_map/ppermute | solution.py:359
  26.1 1.3 %collective-permute-start.11 = (f32[4,8,512]{2,1,0:T(8,128)S(1)}, f32[4,8,512]{2,1,0:T(8,128)S(1)}, u32[]{:S(2)}, u32[]{:S(2)}) collective-permute-start(f32[4,8,512]{2,1,0:T(8,128)S(1)} %add_add_fusion.mine), channel_id=1, source_target_pairs={{0,1},{1,0},{2,3},{3,2},{4,5},{5,4},{6,7},{7,6},{8,9},{9,8},{10,11... | collective-permute-start | bytes 196616 | tf_op jit(solution)/shard_map/ppermute | solution.py:455

commit v5 on v4

--- a/solution.py
+++ b/solution.py
@@ -172,7 +172,7 @@
     count = max(len(codes), 1)
     pieces, refs = refs[:count], refs[count:]
     green, onehot_ref, turned_ref, apart, table, ahead, weight = refs[:7]
-    residual_out, partial_out, weight_out = refs[7:10]
+    missed, partial_out, weight_out = refs[7:10]
     weight_out[...] = ahead[...] + weight[...]
     if codes:
         shards, refs = refs[10], refs[11:]
@@ -181,7 +181,7 @@
             shards[lax.bitwise_xor(me, code)] = piece[:, : shards.shape[2]]
     else:
         shards, refs = pieces[0], refs[10:]
-    spread, summed, adjoint_rows, missed, fields = refs
+    spread, summed, adjoint_rows, fields = refs
     freqs, rows, _ = green.shape
     block = rows // 2
     stations = apart.shape[1] // freqs
@@ -215,14 +215,6 @@
             high, rest = split(real * sign + pltpu.roll(imag, block, 1))
             adjoint_rows[k * stations : (k + 1) * stations, at] = high
             adjoint_rows[(classes + k) * stations : (classes + k + 1) * stations, at] = rest
-    for r in range(2):
-        for j in range(stations // 2):
-            even = missed[r, 2 * j * freqs : (2 * j + 1) * freqs, :]
-            odd = missed[r, (2 * j + 1) * freqs : (2 * j + 2) * freqs, :]
-            residual_out[r, :, j * LANES : (j + 1) * LANES] = jnp.where(
-                low8, even, pltpu.roll(odd, block, 1)
-            )
-
     per_part = width // block
     chunk_parts = CHUNK // per_part
 
@@ -244,6 +236,20 @@
                 )
 
     over_chunks(turned_ref.shape[0], step)
+
+
+def residual_kernel(missed, residual_out):
+    freqs = residual_out.shape[1]
+    stations = missed.shape[1] // freqs
+    block = residual_out.shape[2] // stations
+    low8 = low_lanes((freqs, LANES), block)
+    for r in range(2):
+        for j in range(stations // 2):
+            even = missed[r, 2 * j * freqs : (2 * j + 1) * freqs, :]
+            odd = missed[r, (2 * j + 1) * freqs : (2 * j + 2) * freqs, :]
+            residual_out[r, :, j * LANES : (j + 1) * LANES] = jnp.where(
+                low8, even, pltpu.roll(odd, block, 1)
+            )
 
 
 def smooth_kernel(shards, weight, *refs):
@@ -397,7 +403,8 @@
         pieces = list(neighbours)
         codes = [(0, 0), (1, 1)]
         fetched = []
-        for k in range(1, n_freq):
+        order = range(n_freq - 1, 0, -1)
+        for k in order:
             pairs = [
                 (4 * (z ^ k) + 2 * (t ^ s) + s, 4 * z + 2 * t + s)
                 for z in range(n_freq)
@@ -408,7 +415,7 @@
             codes.append((2 * k, 2 * k + 1))
         fetched[0], prepared = lax.optimization_barrier((fetched[0], prepared))
         pieces += fetched + [lax.ppermute(v, "sta", cores) for v in fetched]
-        codes += [(2 * k + 1, 2 * k) for k in range(1, n_freq)]
+        codes += [(2 * k + 1, 2 * k) for k in order]
     else:
         copies = jnp.broadcast_to(slip[None], (parts,) + slip.shape)
         pieces = [lax.all_to_all(copies, ("freq", "tri"), 0, 0, tiled=True)]
@@ -420,7 +427,7 @@
     outs = pl.pallas_call(
         lambda *refs: forward_kernel(windows, codes, *refs),
         out_shape=(
-            shape(observed.shape, F32),
+            shape((2, stations * freqs, LANES), F32),
             shape((n_sta, count, windows, columns), F32),
             shape((8, LANES), F32),
         )
@@ -431,14 +438,22 @@
             pltpu.VMEM((blocks * windows, LANES), F32),
             pltpu.VMEM((classes * stations, freqs * LANES), F32),
             pltpu.VMEM((2 * classes * stations, freqs * LANES), BF16),
-            pltpu.VMEM((2, stations * freqs, LANES), F32),
             pltpu.VMEM((CHUNK * windows, LANES), F32),
         ],
         compiler_params=grant,
         cost_estimate=pl.CostEstimate(flops=flops, bytes_accessed=4 * 2**20, transcendentals=0),
     )(*pieces, pieces_of_green, onehot, turned, apart, own_table, ahead, smooth_weight.reshape(1, 1))
-    residual, partial, weights = outs[:3]
+    missed, partial, weights = outs[:3]
     shards = outs[3] if codes else pieces[0]
+
+    residual = pl.pallas_call(
+        residual_kernel,
+        out_shape=shape(observed.shape, F32),
+        in_specs=[VMEM],
+        out_specs=VMEM,
+        compiler_params=grant,
+        cost_estimate=pl.CostEstimate(flops=10**6, bytes_accessed=2**20, transcendentals=0),
+    )(missed)
 
     smooth = pl.pallas_call(
         smooth_kernel,
@@ -451,7 +466,12 @@
 
     mine = partial[0] + lax.ppermute(partial[1], "sta", cores)
     mine = mine + smooth
-    mine = sum(across(mine), mine) if n_freq <= 8 else lax.psum(mine, "freq")
+    if n_freq <= 8:
+        others = across(mine)
+        others[-1], residual = lax.optimization_barrier((others[-1], residual))
+        mine = sum(others, mine)
+    else:
+        mine = lax.psum(mine, "freq")
     other = lax.ppermute(mine, "sta", cores)
 
     ranks = n_freq * n_sta

time: 37.9 us -> 37 us (0.976)
  waiting for transfers between devices: 8.61 us -> 7.41 us
    ppermute x3, waiting for transfers between devices: 3.19 us -> 2.02 us  [local(): fetched.append(lax.ppermute(slip, ('freq', 'tri', 'sta'), pairs))]
    pallas_call x0 -> x1, Pallas kernels: none -> 0.76 us  [local(): pl.pallas_call(residual_kernel, out_shape=shape(observed.shape, F32), in_...]
    pallas_call x1, Pallas kernels: 2.86 us -> 2.27 us  [local(): pl.pallas_call(lambda *refs: forward_kernel(windows, codes, *refs), out_s...]
  transfers between devices with their start and end apart: 12 -> 12, of which waited for: 6 -> 6; matrix products, arithmetic and copies ran while one was open for 0% -> 0% of each run, Pallas kernels for 4% -> 6%
where the time goes in v5:
time: 37 us; the launch traced here: 36.8 us
  starting transfers between devices  12.8 us (35%)
  blocking collectives  8.64 us (23%)
  waiting for transfers between devices  7.41 us (20%)
  Pallas kernels  6.4 us (17%)
  between operations  1.41 us (4%)
    all_to_all x1, blocking collectives, local(): images = lax.all_to_all(image, ('freq', 'sta'), 0, 0, tiled=True)  8.64 us
    ppermute x3, starting transfers between devices, local(): fetched.append(lax.ppermute(slip, ('freq', 'tri', 'sta'), pairs))  5.68 us
    ppermute x3, starting transfers between devices, across(): lax.ppermute(value, 'freq', [(i, i ^ k) for i in range(n_freq)])  4.45 us
    ppermute x3, waiting for transfers between devices, across(): lax.ppermute(value, 'freq', [(i, i ^ k) for i in range(n_freq)])  3.7 us
    pallas_call x1, Pallas kernels, local(): pl.pallas_call(lambda *refs: forward_kernel(windows, codes, *refs), out_s...  2.27 us
    ppermute x3, waiting for transfers between devices, local(): fetched.append(lax.ppermute(slip, ('freq', 'tri', 'sta'), pairs))  2.02 us
    ppermute x1, starting transfers between devices, local(): lax.ppermute(packed, 'tri', [(i, i ^ k) for i in range(n_tri)])  1.56 us
    pallas_call x1, Pallas kernels, local(): pl.pallas_call(image_kernel, out_shape=(shape(slip.shape, F32), shape((ra...  1.36 us
  transfers between devices with their start and end apart: 12, of which 6 were waited for; matrix products, arithmetic and copies ran while one was open for 0% of the time, Pallas kernels for 6%

profile of v5, /device:TPU:0, one launch (start us, length us, event | category | flops | bytes accessed | tf_op | source)
XLA Modules:
  0.0 36.8 jit_solution(777484576092195374)
XLA Ops:
  0.7 4.1 %collective-permute-start.2 = (f32[8,512]{1,0:T(8,128)}, f32[8,512]{1,0:T(8,128)S(1)}, u32[]{:S(2)}, u32[]{:S(2)}) collective-permute-start(f32[8,512]{1,0:T(8,128)} %slip.3), channel_id=1, source_target_pairs={{8,0},{11,1},{10,2},{9,3},{12,4},{15,5},{14,6},{13,7},{0,8},{3,9},... | collective-permute-start | bytes 49160 | tf_op jit(solution)/shard_map/ppermute | solution.py:414
  4.8 1.3 %collective-permute-start.1 = (f32[8,512]{1,0:T(8,128)}, f32[8,512]{1,0:T(8,128)S(1)}, u32[]{:S(2)}, u32[]{:S(2)}) collective-permute-start(f32[8,512]{1,0:T(8,128)} %slip.3), channel_id=1, source_target_pairs={{12,0},{15,1},{14,2},{13,3},{8,4},{11,5},{10,6},{9,7},{4,8},{7,9},... | collective-permute-start | bytes 49160 | tf_op jit(solution)/shard_map/ppermute | solution.py:414
  6.1 0.2 collective-permute-start.3
  6.4 1.6 %collective-permute-start = (f32[8,768]{1,0:T(8,128)S(1)}, f32[8,768]{1,0:T(8,128)S(1)}, u32[]{:S(2)}, u32[]{:S(2)}) collective-permute-start(f32[8,768]{1,0:T(8,128)S(1)} %shard_map.87.refs_0_), channel_id=1, source_target_pairs={{0,2},{2,0},{1,3},{3,1},{4,6},{6,4},{5,7},{7,5},{8,10},{10,8},{9,1... | collective-permute-start | bytes 73736 | tf_op jit(solution)/shard_map/ppermute | solution.py:400
  8.0 0.6 %shard_map.88 = (bf16[8,128,1024]{2,1,0:T(8,128)(2,1)S(1)}, bf16[1,256,128]{2,1,0:T(8,128)(2,1)S(1)}, bf16[1,64,512]{2,1,0:T(8,128)(2,1)S(1)}, f32[2,256,128]{2,...) custom-call(f32[8,8,64,128]{3,2,1,0:T(8,128)S(1)} %copy-done, s32[1,32,64]{2,1,0:T(8,128)S(1)} %bitcast.9, ...), custom_call_target="tpu_custom_call" | custom-call | flops 1000000 | bytes 6291456 | tf_op jit(solution)/shard_map/pallas_call | solution.py:377
  8.5 2.0 %collective-permute-done.1.refs_2_ = f32[8,512]{1,0:T(8,128)S(1)} collective-permute-done((f32[8,512]{1,0:T(8,128)}, f32[8,512]{1,0:T(8,128)S(1)}, u32[]{:S(2)}, u32[]{:S(2)}) %collective-permute-start.1) | collective-permute-done | bytes 16416 | tf_op jit(solution)/shard_map/ppermute | solution.py:414
  10.6 0.2 collective-permute-start.5
  10.8 0.3 collective-permute-start.6
  11.1 0.2 collective-permute-start.4
  12.0 0.3 collective-permute-done.4.refs_5_
  12.3 2.3 %shard_map.89 = (f32[2,256,128]{2,1,0:T(8,128)S(1)}, f32[2,4,8,512]{3,2,1,0:T(8,128)S(1)}, f32[8,128]{1,0:T(8,128)S(1)}, f32[8,8,512]{2,1,0:T(8,128)S(1)}) custom-call(f32[8,768]{1,0:T(8,128)S(1)} %shard_map.87.refs_0_, f32[8,768]{1,0:T(8,128)S(1)} %collective-permute-done.refs_1_, f32[8,512]{1,0:T(8,128)S(1)} %collective-permute-done.1.refs_2_, ...), custom_call_target="tpu_custom_call" | custom-call | flops 536870912 | bytes 4194304 | tf_op jit(solution)/shard_map/pallas_call | solution.py:427
  14.5 0.3 collective-permute-start.7
  14.8 0.8 %shard_map.90 = f32[4,8,512]{2,1,0:T(8,128)S(1)} custom-call(f32[8,8,512]{2,1,0:T(8,128)S(1)} %get-tuple-element.42.shards, f32[8,128]{1,0:T(8,128)S(1)} %get-tuple-element.43.weight, f32[8,768]{1,0:T(8,128)S(1)} %shard_map.87.refs_0_, f32[8,768]{1,0:T(8,128)S(1)} %collective-permute-done.refs_1_), custom_call_target="tpu_custom_call" | custom-call | flops 1000000 | bytes 4194304 | tf_op jit(solution)/shard_map/pallas_call | solution.py:458
  15.7 0.2 collective-permute-done.7
  15.9 1.8 %collective-permute-start.10 = (f32[4,8,512]{2,1,0:T(8,128)S(1)}, f32[4,8,512]{2,1,0:T(8,128)S(1)}, u32[]{:S(2)}, u32[]{:S(2)}) collective-permute-start(f32[4,8,512]{2,1,0:T(8,128)S(1)} %fusion), channel_id=1, source_target_pairs={{0,12},{4,8},{8,4},{12,0},{1,13},{5,9},{9,5},{13,1},{2,14},{6,10},... | collective-permute-start | bytes 196616 | tf_op jit(solution)/shard_map/ppermute | solution.py:365
  17.7 2.7 %collective-permute-start.8 = (f32[4,8,512]{2,1,0:T(8,128)S(1)}, f32[4,8,512]{2,1,0:T(8,128)S(1)}, u32[]{:S(2)}, u32[]{:S(2)}) collective-permute-start(f32[4,8,512]{2,1,0:T(8,128)S(1)} %fusion), channel_id=1, source_target_pairs={{0,4},{4,0},{8,12},{12,8},{1,5},{5,1},{9,13},{13,9},{2,6},{6,2},{1... | collective-permute-start | bytes 196616 | tf_op jit(solution)/shard_map/ppermute | solution.py:365
  20.3 0.8 %shard_map.91 = f32[2,8,2048]{2,1,0:T(8,128)} custom-call(f32[2,256,128]{2,1,0:T(8,128)S(1)} %get-tuple-element.44.missed), custom_call_target="tpu_custom_call" | custom-call | flops 1000000 | bytes 1048576 | tf_op jit(solution)/shard_map/pallas_call | solution.py:449
  21.1 1.7 %collective-permute-done.10 = f32[4,8,512]{2,1,0:T(8,128)S(1)} collective-permute-done((f32[4,8,512]{2,1,0:T(8,128)S(1)}, f32[4,8,512]{2,1,0:T(8,128)S(1)}, u32[]{:S(2)}, u32[]{:S(2)}) %collective-permute-start.10) | collective-permute-done | bytes 65568 | tf_op jit(solution)/shard_map/ppermute | solution.py:365
  22.8 2.0 %collective-permute-done.9 = f32[4,8,512]{2,1,0:T(8,128)S(1)} collective-permute-done((f32[4,8,512]{2,1,0:T(8,128)S(1)}, f32[4,8,512]{2,1,0:T(8,128)S(1)}, u32[]{:S(2)}, u32[]{:S(2)}) %collective-permute-start.9) | collective-permute-done | bytes 65568 | tf_op jit(solution)/shard_map/ppermute | solution.py:365
  24.8 0.1 collective-permute-start.11
  24.9 1.2 %collective-permute-done.11.other = f32[4,8,512]{2,1,0:T(8,128)S(1)} collective-permute-done((f32[4,8,512]{2,1,0:T(8,128)S(1)}, f32[4,8,512]{2,1,0:T(8,128)S(1)}, u32[]{:S(2)}, u32[]{:S(2)}) %collective-permute-start.11) | collective-permute-done | bytes 65568 | tf_op jit(solution)/shard_map/ppermute | solution.py:475
  26.1 1.4 %shard_map.92 = (f32[8,512]{1,0:T(8,128)S(1)}, f32[8,8,128]{2,1,0:T(8,128)S(1)}, f32[2,8,128]{2,1,0:T(8,128)S(1)}) custom-call(f32[4,8,512]{2,1,0:T(8,128)S(1)} %add_add_fusion.mine, f32[4,8,512]{2,1,0:T(8,128)S(1)} %collective-permute-done.11.other, bf16[8,128,1024]{2,1,0:T(8,128)(2,1)S(1)} %get-tuple-element.35.refs_8_.green, ...), custom_call_target="tpu_custom_call" | custom-call | flops 536870912 | bytes 4194304 | tf_op jit(solution)/shard_map/pallas_call | solution.py:478
  27.5 8.6 %all_to_all.5.images = f32[8,8,128]{2,1,0:T(8,128)S(1)} all-to-all(f32[8,8,128]{2,1,0:T(8,128)S(1)} %get-tuple-element.46), channel_id=1, replica_groups=mesh['grp'=2,'freq'=4,'tri'=2,'sta'=2] {'freq','sta'}, dimensions={0} | all-to-all | bytes 65536 | tf_op jit(solution)/shard_map/all_to_all | solution.py:495
  36.1 0.6 %shard_map.93 = f32[8,512]{1,0:T(8,128)} custom-call(f32[8,8,128]{2,1,0:T(8,128)S(1)} %all_to_all.5.images, f32[2,8,128]{2,1,0:T(8,128)S(1)} %get-tuple-element.47.norm, f32[8,512]{1,0:T(8,128)S(1)} %copy-done.3, f32[8,512]{1,0:T(8,128)S(1)} %get-tuple-element.48.own), custom_call_target="tpu_custom_call" | custom-call | tf_op jit(solution)/shard_map/pallas_call | solution.py:496
  (24 shorter events, 0.1 us)
Async XLA Ops:
  0.6 7.3 %copy-start.2 = (f32[32,8,128]{2,1,0:T(8,128)S(1)}, f32[32,8,128]{2,1,0:T(8,128)}, u32[]{:S(2)}) copy-start(f32[32,8,128]{2,1,0:T(8,128)} %constant.2.clone.table) | copy-start | bytes 393220
  0.6 5.7 %copy-start.3 = (f32[8,512]{1,0:T(8,128)S(1)}, f32[8,512]{1,0:T(8,128)}, u32[]{:S(2)}) copy-start(f32[8,512]{1,0:T(8,128)} %slip.3) | copy-start | bytes 49156
  0.7 5.7 %copy-start.5 = (s32[3,256]{1,0:T(4,128)S(1)}, s32[3,256]{1,0:T(4,128)}, u32[]{:S(2)}) copy-start(s32[3,256]{1,0:T(4,128)} %adjacency) | copy-start | bytes 9220
  0.7 7.3 %copy-start.1 = (f32[2,8,2048]{2,1,0:T(8,128)S(1)}, f32[2,8,2048]{2,1,0:T(8,128)}, u32[]{:S(2)}) copy-start(f32[2,8,2048]{2,1,0:T(8,128)} %observed.1) | copy-start | bytes 393220
  0.7 7.3 %copy-start.4 = (s32[32,64]{1,0:T(8,128)S(1)}, s32[32,64]{1,0:T(8,128)}, u32[]{:S(2)}) copy-start(s32[32,64]{1,0:T(8,128)} %param.9) | copy-start | bytes 24580
  0.7 7.3 %copy-start = (f32[8,8,64,128]{3,2,1,0:T(8,128)S(1)}, f32[8,8,64,128]{3,2,1,0:T(8,128)}, u32[]{:S(2)}) copy-start(f32[8,8,64,128]{3,2,1,0:T(8,128)} %green_ref.1) | copy-start | bytes 6291460
  0.7 9.9 %collective-permute-start.2 = (f32[8,512]{1,0:T(8,128)}, f32[8,512]{1,0:T(8,128)S(1)}, u32[]{:S(2)}, u32[]{:S(2)}) collective-permute-start(f32[8,512]{1,0:T(8,128)} %slip.3), channel_id=1, source_target_pairs={{8,0},{11,1},{10,2},{9,3},{12,4},{15,5},{14,6},{13,7},{0,8},{3,9},... | collective-permute-start | bytes 49160 | tf_op jit(solution)/shard_map/ppermute | solution.py:414
  4.8 5.8 %collective-permute-start.1 = (f32[8,512]{1,0:T(8,128)}, f32[8,512]{1,0:T(8,128)S(1)}, u32[]{:S(2)}, u32[]{:S(2)}) collective-permute-start(f32[8,512]{1,0:T(8,128)} %slip.3), channel_id=1, source_target_pairs={{12,0},{15,1},{14,2},{13,3},{8,4},{11,5},{10,6},{9,7},{4,8},{7,9},... | collective-permute-start | bytes 49160 | tf_op jit(solution)/shard_map/ppermute | solution.py:414
  6.1 4.6 %collective-permute-start.3 = (f32[8,512]{1,0:T(8,128)}, f32[8,512]{1,0:T(8,128)S(1)}, u32[]{:S(2)}, u32[]{:S(2)}) collective-permute-start(f32[8,512]{1,0:T(8,128)} %slip.3), channel_id=1, source_target_pairs={{4,0},{7,1},{6,2},{5,3},{0,4},{3,5},{2,6},{1,7},{12,8},{15,9},{14,... | collective-permute-start | bytes 49160 | tf_op jit(solution)/shard_map/ppermute | solution.py:414
  6.4 5.6 %collective-permute-start = (f32[8,768]{1,0:T(8,128)S(1)}, f32[8,768]{1,0:T(8,128)S(1)}, u32[]{:S(2)}, u32[]{:S(2)}) collective-permute-start(f32[8,768]{1,0:T(8,128)S(1)} %shard_map.87.refs_0_), channel_id=1, source_target_pairs={{0,2},{2,0},{1,3},{3,1},{4,6},{6,4},{5,7},{7,5},{8,10},{10,8},{9,1... | collective-permute-start | bytes 73736 | tf_op jit(solution)/shard_map/ppermute | solution.py:400
  10.6 1.4 %collective-permute-start.5 = (f32[8,512]{1,0:T(8,128)S(1)}, f32[8,512]{1,0:T(8,128)S(1)}, u32[]{:S(2)}, u32[]{:S(2)}) collective-permute-start(f32[8,512]{1,0:T(8,128)S(1)} %collective-permute-done.2.refs_3_), channel_id=1, source_target_pairs={{0,1},{1,0},{2,3},{3,2},{4,5},{5,4},{6,7},{7,6},{8,9},{9,8},{10,11... | collective-permute-start | bytes 49160 | tf_op jit(solution)/shard_map/ppermute | solution.py:417
  10.8 1.2 %collective-permute-start.6 = (f32[8,512]{1,0:T(8,128)S(1)}, f32[8,512]{1,0:T(8,128)S(1)}, u32[]{:S(2)}, u32[]{:S(2)}) collective-permute-start(f32[8,512]{1,0:T(8,128)S(1)} %collective-permute-done.3.refs_4_), channel_id=1, source_target_pairs={{0,1},{1,0},{2,3},{3,2},{4,5},{5,4},{6,7},{7,6},{8,9},{9,8},{10,11... | collective-permute-start | bytes 49160 | tf_op jit(solution)/shard_map/ppermute | solution.py:417
  11.1 1.2 %collective-permute-start.4 = (f32[8,512]{1,0:T(8,128)S(1)}, f32[8,512]{1,0:T(8,128)S(1)}, u32[]{:S(2)}, u32[]{:S(2)}) collective-permute-start(f32[8,512]{1,0:T(8,128)S(1)} %collective-permute-done.1.refs_2_), channel_id=1, source_target_pairs={{0,1},{1,0},{2,3},{3,2},{4,5},{5,4},{6,7},{7,6},{8,9},{9,8},{10,11... | collective-permute-start | bytes 49160 | tf_op jit(solution)/shard_map/ppermute | solution.py:417
  14.5 1.3 %collective-permute-start.7 = (f32[4,8,512]{2,1,0:T(8,128)S(1)}, f32[4,8,512]{2,1,0:T(8,128)S(1)}, u32[]{:S(2)}, u32[]{:S(2)}) collective-permute-start(f32[4,8,512]{2,1,0:T(8,128)S(1)} %slice_bitcast_fusion), channel_id=1, source_target_pairs={{0,1},{1,0},{2,3},{3,2},{4,5},{5,4},{6,7},{7,6},{8,9},{9,8},{10,11... | collective-permute-start | bytes 196616 | tf_op jit(solution)/shard_map/ppermute | solution.py:467
  15.9 6.9 %collective-permute-start.10 = (f32[4,8,512]{2,1,0:T(8,128)S(1)}, f32[4,8,512]{2,1,0:T(8,128)S(1)}, u32[]{:S(2)}, u32[]{:S(2)}) collective-permute-start(f32[4,8,512]{2,1,0:T(8,128)S(1)} %fusion), channel_id=1, source_target_pairs={{0,12},{4,8},{8,4},{12,0},{1,13},{5,9},{9,5},{13,1},{2,14},{6,10},... | collective-permute-start | bytes 196616 | tf_op jit(solution)/shard_map/ppermute | solution.py:365
  17.7 7.1 %collective-permute-start.9 = (f32[4,8,512]{2,1,0:T(8,128)S(1)}, f32[4,8,512]{2,1,0:T(8,128)S(1)}, u32[]{:S(2)}, u32[]{:S(2)}) collective-permute-start(f32[4,8,512]{2,1,0:T(8,128)S(1)} %fusion), channel_id=1, source_target_pairs={{0,8},{4,12},{8,0},{12,4},{1,9},{5,13},{9,1},{13,5},{2,10},{6,14},... | collective-permute-start | bytes 196616 | tf_op jit(solution)/shard_map/ppermute | solution.py:365
  17.7 7.1 %collective-permute-start.8 = (f32[4,8,512]{2,1,0:T(8,128)S(1)}, f32[4,8,512]{2,1,0:T(8,128)S(1)}, u32[]{:S(2)}, u32[]{:S(2)}) collective-permute-start(f32[4,8,512]{2,1,0:T(8,128)S(1)} %fusion), channel_id=1, source_target_pairs={{0,4},{4,0},{8,12},{12,8},{1,5},{5,1},{9,13},{13,9},{2,6},{6,2},{1... | collective-permute-start | bytes 196616 | tf_op jit(solution)/shard_map/ppermute | solution.py:365
  24.8 1.3 %collective-permute-start.11 = (f32[4,8,512]{2,1,0:T(8,128)S(1)}, f32[4,8,512]{2,1,0:T(8,128)S(1)}, u32[]{:S(2)}, u32[]{:S(2)}) collective-permute-start(f32[4,8,512]{2,1,0:T(8,128)S(1)} %add_add_fusion.mine), channel_id=1, source_target_pairs={{0,1},{1,0},{2,3},{3,2},{4,5},{5,4},{6,7},{7,6},{8,9},{9,8},{10,11... | collective-permute-start | bytes 196616 | tf_op jit(solution)/shard_map/ppermute | solution.py:475
